TPU v7x, 32 devices: a whole 2x2x4 slice. The times are simulated.
32 devices in a mesh: tok: 8 (over z, y), qry: 4 (over x, core).
Axes of the slice: x: 2, y: 2, z: 4, core: 2. Of those that a mesh axis runs over, the one named last changes fastest.
Arguments:
- content_in: bfloat16 [64, 512, 768], P(('tok', 'qry')), may hold values from -6 to 6
- query_in: bfloat16 [64, 80, 768], P('tok', 'qry'), may hold values from -6 to 6
- seq_lengths: int32 [64], P('tok'), may hold values from 256 to 512, as said below
- perm_ranks: int32 [64, 512], P('tok'), may hold values from 0 to 511, as said below
- w_query: bfloat16 [768, 768], replicated, may hold values from -0.21875 to 0.21875
- w_key: bfloat16 [768, 768], replicated, may hold values from -0.21875 to 0.21875
- w_value: bfloat16 [768, 768], replicated, may hold values from -0.21875 to 0.21875
- w_output: bfloat16 [768, 768], replicated, may hold values from -1.25 to 1.25
- w_inner: bfloat16 [768, 3072], replicated, may hold values from -0.21875 to 0.21875
- w_outer: bfloat16 [3072, 768], replicated, may hold values from -0.109375 to 0.109375
- b_before: bfloat16 [2, 768], replicated, may hold values from -3 to 3
- b_after: bfloat16 [2, 768], replicated, may hold values from -3 to 3
- b_hidden: bfloat16 [3072], replicated, may hold values from -3 to 3
- norm_gain: bfloat16 [2, 768], replicated, may hold values from 0.5 to 1.5
- norm_shift: bfloat16 [2, 768], replicated, may hold values from -3 to 3
- rel_table: bfloat16 [12, 32], replicated, may hold values from -4 to 4
- cot_content: bfloat16 [64, 512, 768], P(('tok', 'qry')), may hold values from -6 to 6
- cot_query: bfloat16 [64, 80, 768], P('tok', 'qry'), may hold values from -6 to 6
Outputs:
- content_out: bfloat16 [64, 512, 768], P(('tok', 'qry'))
- query_out: bfloat16 [64, 80, 768], P('tok', 'qry')
- d_content: float32 [64, 512, 768], P(('tok', 'qry'))
- d_query: float32 [64, 80, 768], P('tok', 'qry')
- g_query: float32 [768, 768], P('tok')
- g_key: float32 [768, 768], P('tok')
- g_value: float32 [768, 768], P('tok')
- g_output: float32 [768, 768], P('tok')
- g_inner: float32 [768, 3072], P('tok')
- g_outer: float32 [3072, 768], P('tok')
- g_before: float32 [2, 768], P(None, 'tok')
- g_after: float32 [2, 768], P(None, 'tok')
- g_hidden: float32 [3072], P('tok')
- g_gain: float32 [2, 768], P(None, 'tok')
- g_shift: float32 [2, 768], P(None, 'tok')
- g_table: float32 [12, 32], replicated
Inputs may be any that keep to these rules, and one draw needn't show every extreme that they name: `seq_lengths`: lengths of the sequences; some sequence has length 512 and some half of 512. `perm_ranks`: each row is a permutation of 0 to 511 that gives the positions below the sequence's length the ranks below that length.
All inputs are finite; a program needn't handle non-finite values.
Results may differ from a plain program's by a relative error of at most 0.017.
Values may be sent and summed in bfloat16 or wider, within the bound.
No kernel may reach another device: no remote copies, remote signals or barrier semaphores. Data moves between devices by JAX's collectives and lax.ppermute only.
A program may use at most 256 MiB of HBM per device.

v0:
```python
import jax
import jax.numpy as jnp
from jax import lax
from jax.sharding import PartitionSpec as P

HEADS = 12
BUCKETS = 32
PRED = 80


EPS = 1e-05
NEG = -1e30
HIGH_PRECISION = lax.Precision.HIGHEST
BORDERS = (12, 16, 23, 32, 46, 64, 91)
SQRT_HALF = 0.7071067811865476
INV_ROOT = 0.3989422804014327


def bucket_of(offset):
    distance = jnp.abs(offset)
    beyond = 8 + sum(((distance >= border).astype(jnp.int32) for border in BORDERS))
    return jnp.where(distance < 8, distance, beyond) + 16 * (offset > 0).astype(jnp.int32)


def norm_apply(inputs, gain_row, shift_row):
    centre = inputs - jnp.mean(inputs, axis=-1, keepdims=True)
    spread = jnp.mean(centre * centre, axis=-1, keepdims=True)
    return centre * lax.rsqrt(spread + EPS) * gain_row + shift_row


def split_into_heads(matrix):
    return matrix.reshape(matrix.shape[0], matrix.shape[1], HEADS, -1)


def score_block(query_vectors, key_matrix_rows, position_bias, visible):
    scores = jnp.einsum(
        "akop,anop->aokn",
        split_into_heads(query_vectors),
        split_into_heads(key_matrix_rows),
        preferred_element_type=jnp.float32,
    )
    return jnp.where(visible[:, None], scores * 0.125 + position_bias, NEG)


def attend_forward(query_vectors, key_matrix_rows, value_matrix_rows, position_bias, visible):
    scores = score_block(query_vectors, key_matrix_rows, position_bias, visible)
    top_score = jnp.max(scores, axis=-1, keepdims=True)
    shifted = jnp.exp(scores - top_score)
    row_total = jnp.sum(shifted, axis=-1, keepdims=True)
    attention_reduced = (shifted / row_total).astype(jnp.bfloat16)
    context = jnp.einsum(
        "owkz,ozwy->okwy",
        attention_reduced,
        split_into_heads(value_matrix_rows),
        preferred_element_type=jnp.float32,
    )
    return (
        context.reshape(query_vectors.shape).astype(jnp.bfloat16),
        top_score + jnp.log(row_total),
    )


def attend_backward(
    query_vectors,
    key_matrix_rows,
    value_matrix_rows,
    position_bias,
    visible,
    log_total,
    d_context,
    one_hot_bucket,
    table_form,
):
    scores = score_block(query_vectors, key_matrix_rows, position_bias, visible)
    attn_probs = jnp.exp(scores - log_total)
    d_probs = jnp.einsum(
        "akop,anop->aokn",
        split_into_heads(d_context),
        split_into_heads(value_matrix_rows),
        preferred_element_type=jnp.float32,
    )
    centred = d_probs - jnp.sum(d_probs * attn_probs, axis=-1, keepdims=True)
    score_gradient = (attn_probs * centred).astype(jnp.bfloat16)
    d_values = jnp.einsum(
        "bnye,bynj->benj",
        attn_probs.astype(jnp.bfloat16),
        split_into_heads(d_context),
        preferred_element_type=jnp.float32,
    )
    d_queries = (
        jnp.einsum(
            "owkz,ozwy->okwy",
            score_gradient,
            split_into_heads(key_matrix_rows),
            preferred_element_type=jnp.float32,
        )
        * 0.125
    )
    d_keys = (
        jnp.einsum(
            "bnye,bynj->benj",
            score_gradient,
            split_into_heads(query_vectors),
            preferred_element_type=jnp.float32,
        )
        * 0.125
    )
    d_table = jnp.einsum(
        table_form, score_gradient, one_hot_bucket, preferred_element_type=jnp.float32
    )
    return (
        d_queries.reshape(query_vectors.shape),
        d_keys.reshape(key_matrix_rows.shape),
        d_values.reshape(value_matrix_rows.shape),
        d_table[None],
    )


def per_sequence(function, members):
    widened = jax.tree.map(lambda member: member[:, None], members)
    result = lax.map(lambda pieces: function(*pieces), widened)
    return jax.tree.map(lambda member: member[:, 0], result)


def query_layout(lengths_part, ranks_part, first_slot, slot_total, table_float32):
    places = jnp.arange(ranks_part.shape[1], dtype=jnp.int32)
    slot_rank = (
        lengths_part[:, None] - PRED + first_slot + jnp.arange(slot_total, dtype=jnp.int32)[None, :]
    )
    seen_query = ranks_part[:, None, :] < slot_rank[:, :, None]
    slot_place = jnp.sum(
        jnp.where(ranks_part[:, None, :] == slot_rank[:, :, None], places, 0), axis=-1
    )
    buckets = bucket_of(places[None, None, :] - slot_place[:, :, None])
    one_hot_bucket = (
        buckets[:, None] == jnp.arange(BUCKETS, dtype=jnp.int32)[None, :, None, None]
    ).astype(jnp.bfloat16)
    position_bias = jnp.einsum(
        "cz,qzvd->qcvd", table_float32, one_hot_bucket.astype(jnp.float32), precision=HIGH_PRECISION
    )
    return (seen_query, one_hot_bucket, position_bias)


def project(rows_in, weight, bias_row):
    flat_rows = rows_in.reshape(-1, rows_in.shape[-1])
    result = jnp.dot(flat_rows, weight, preferred_element_type=jnp.float32)
    if bias_row is not None:
        result = result + bias_row
    return result.astype(jnp.bfloat16).reshape(rows_in.shape)


def branch_forward(stream_in, context, params):
    w_output, w_inner, w_outer, after_bias, inner_bias, gains_f32, shifts_f32 = params
    model_width = stream_in.shape[-1]
    flat_in = stream_in.reshape(-1, model_width).astype(jnp.float32)
    flat_ctx = context.reshape(-1, model_width)
    first_sum = (
        flat_in + jnp.dot(flat_ctx, w_output, preferred_element_type=jnp.float32) + after_bias[0]
    )
    hidden = norm_apply(first_sum, gains_f32[0], shifts_f32[0])
    hidden_low = hidden.astype(jnp.bfloat16)
    inner_pre = jnp.dot(hidden_low, w_inner, preferred_element_type=jnp.float32) + inner_bias
    activated = (inner_pre * 0.5 * (1.0 + lax.erf(inner_pre * SQRT_HALF))).astype(jnp.bfloat16)
    second_sum = (
        hidden + jnp.dot(activated, w_outer, preferred_element_type=jnp.float32) + after_bias[1]
    )
    output = norm_apply(second_sum, gains_f32[1], shifts_f32[1]).astype(jnp.bfloat16)
    return (
        output.reshape(stream_in.shape),
        (flat_ctx, first_sum, hidden_low, inner_pre, activated, second_sum),
    )


def branch_backward(saved, cotangent, params):
    w_output, w_inner, w_outer, after_bias, inner_bias, gains_f32, shifts_f32 = params
    flat_ctx, first_sum, hidden_low, inner_pre, activated, second_sum = saved
    flat_cot = cotangent.reshape(second_sum.shape).astype(jnp.float32)
    second_back = jax.vjp(norm_apply, second_sum, gains_f32[1], shifts_f32[1])[1]
    d_second, gain_second, shift_second = second_back(flat_cot)
    d_outer = d_second.astype(jnp.bfloat16)
    d_active = jnp.dot(d_outer, w_outer.T, preferred_element_type=jnp.float32)
    slope = (
        0.5 * (1.0 + lax.erf(inner_pre * SQRT_HALF))
        + inner_pre * jnp.exp(-0.5 * inner_pre * inner_pre) * INV_ROOT
    )
    d_inner = (d_active * slope).astype(jnp.bfloat16)
    d_hidden = d_second + jnp.dot(d_inner, w_inner.T, preferred_element_type=jnp.float32)
    first_back = jax.vjp(norm_apply, first_sum, gains_f32[0], shifts_f32[0])[1]
    d_first, gain_first, shift_first = first_back(d_hidden)
    d_attended = d_first.astype(jnp.bfloat16)
    d_context = jnp.dot(d_attended, w_output.T, preferred_element_type=jnp.float32).astype(
        jnp.bfloat16
    )
    gradients = (
        jnp.dot(flat_ctx.T, d_attended, preferred_element_type=jnp.float32),
        jnp.dot(hidden_low.T, d_inner, preferred_element_type=jnp.float32),
        jnp.dot(activated.T, d_outer, preferred_element_type=jnp.float32),
        jnp.stack(
            [
                jnp.sum(d_attended, axis=0, dtype=jnp.float32),
                jnp.sum(d_outer, axis=0, dtype=jnp.float32),
            ]
        ),
        jnp.sum(d_inner, axis=0, dtype=jnp.float32),
        jnp.stack([gain_first, gain_second]),
        jnp.stack([shift_first, shift_second]),
    )
    return (d_first, d_context, gradients)


def on_device(
    content_in,
    query_in,
    seq_lengths,
    perm_ranks,
    w_query,
    w_key,
    w_value,
    w_output,
    w_inner,
    w_outer,
    b_before,
    b_after,
    b_hidden,
    norm_gain,
    norm_shift,
    rel_table,
    cot_content,
    cot_query,
):
    seq_count = content_in.shape[0]
    seq_len = content_in.shape[1]
    slot_count = query_in.shape[1]
    model_width = content_in.shape[2]
    my_group = lax.axis_index("qry")
    own_lengths = lax.dynamic_slice_in_dim(seq_lengths, my_group * seq_count, seq_count)
    own_ranks = lax.dynamic_slice_in_dim(perm_ranks, my_group * seq_count, seq_count, 0)
    places = jnp.arange(seq_len, dtype=jnp.int32)
    threshold = jnp.maximum(
        own_lengths[:, None] - PRED, jnp.minimum(own_ranks, own_lengths[:, None])
    )
    seen_content = (own_ranks[:, None, :] < threshold[:, :, None]) | (
        places[:, None] == places[None, :]
    )[None]
    table_float32 = rel_table.astype(jnp.float32)
    bucket_grid = bucket_of(places[None, :] - places[:, None])
    one_hot_c = (bucket_grid[None] == jnp.arange(BUCKETS, dtype=jnp.int32)[:, None, None]).astype(
        jnp.bfloat16
    )
    bias_content = jnp.einsum(
        "hb,bij->hij", table_float32, one_hot_c.astype(jnp.float32), precision=HIGH_PRECISION
    )
    before_f32 = b_before.astype(jnp.float32)
    q_content = project(content_in, w_query, before_f32[0])
    k_content = project(content_in, w_key, None)
    v_content = project(content_in, w_value, before_f32[1])
    q_query = project(query_in, w_query, before_f32[0])
    content_ctx, content_lse = per_sequence(
        lambda q_rows, k_rows, v_rows, seen_rows: attend_forward(
            q_rows, k_rows, v_rows, bias_content, seen_rows
        ),
        (q_content, k_content, v_content, seen_content),
    )
    seen_query, one_hot_q, bias_query = query_layout(
        seq_lengths, perm_ranks, my_group * slot_count, slot_count, table_float32
    )
    k_group, v_group = (
        lax.all_gather(k_content, "qry", axis=0, tiled=True),
        lax.all_gather(v_content, "qry", axis=0, tiled=True),
    )
    query_ctx, query_lse = attend_forward(q_query, k_group, v_group, bias_query, seen_query)
    params = (
        w_output,
        w_inner,
        w_outer,
        b_after.astype(jnp.float32),
        b_hidden.astype(jnp.float32),
        norm_gain.astype(jnp.float32),
        norm_shift.astype(jnp.float32),
    )
    content_out, content_saved = branch_forward(content_in, content_ctx, params)
    query_out, query_saved = branch_forward(query_in, query_ctx, params)
    first_content, d_content_ctx, content_grads = branch_backward(
        content_saved, cot_content, params
    )
    first_query, d_query_ctx, query_grads = branch_backward(query_saved, cot_query, params)
    g_output, g_inner, g_outer, g_after, g_hidden, g_gain, g_shift = jax.tree.map(
        jnp.add, content_grads, query_grads
    )
    d_query_ctx = d_query_ctx.reshape(query_in.shape)
    dq_local, dk_part, dv_part, table_query = attend_backward(
        q_query,
        k_group,
        v_group,
        bias_query,
        seen_query,
        query_lse,
        d_query_ctx,
        one_hot_q,
        "kfyz,kqyz->fq",
    )
    dk_extra, dv_extra = (
        lax.psum_scatter(
            dk_part.astype(jnp.bfloat16), "qry", scatter_dimension=0, tiled=True
        ).astype(jnp.float32),
        lax.psum_scatter(
            dv_part.astype(jnp.bfloat16), "qry", scatter_dimension=0, tiled=True
        ).astype(jnp.float32),
    )
    dq_query = dq_local.astype(jnp.bfloat16)
    dq_content, dk_content, dv_content, table_content = per_sequence(
        lambda q_rows, k_rows, v_rows, seen_rows, lse_rows, dctx_rows: attend_backward(
            q_rows,
            k_rows,
            v_rows,
            bias_content,
            seen_rows,
            lse_rows,
            dctx_rows,
            one_hot_c,
            "ypde,ude->pu",
        ),
        (
            q_content,
            k_content,
            v_content,
            seen_content,
            content_lse,
            d_content_ctx.reshape(content_in.shape),
        ),
    )
    flat_dq = dq_content.astype(jnp.bfloat16).reshape(-1, model_width)
    flat_dk = (dk_content + dk_extra).astype(jnp.bfloat16).reshape(-1, model_width)
    flat_dv = (dv_content + dv_extra).astype(jnp.bfloat16).reshape(-1, model_width)
    flat_dqq = dq_query.reshape(-1, model_width)
    flat_content = content_in.reshape(-1, model_width)
    flat_query = query_in.reshape(-1, model_width)
    g_query = jnp.dot(flat_content.T, flat_dq, preferred_element_type=jnp.float32) + jnp.dot(
        flat_query.T, flat_dqq, preferred_element_type=jnp.float32
    )
    g_key = jnp.dot(flat_content.T, flat_dk, preferred_element_type=jnp.float32)
    g_value = jnp.dot(flat_content.T, flat_dv, preferred_element_type=jnp.float32)
    g_before = jnp.stack(
        [
            jnp.sum(flat_dq, axis=0, dtype=jnp.float32)
            + jnp.sum(flat_dqq, axis=0, dtype=jnp.float32),
            jnp.sum(flat_dv, axis=0, dtype=jnp.float32),
        ]
    )
    d_content = first_content + jnp.dot(flat_dq, w_query.T, preferred_element_type=jnp.float32)
    d_content = d_content + jnp.dot(flat_dk, w_key.T, preferred_element_type=jnp.float32)
    d_content = d_content + jnp.dot(flat_dv, w_value.T, preferred_element_type=jnp.float32)
    d_query = first_query + jnp.dot(flat_dqq, w_query.T, preferred_element_type=jnp.float32)
    table_local = jnp.sum(table_content, axis=0) + table_query[0]
    g_table = lax.psum(table_local, ("tok", "qry"))
    all_parts = (
        lax.psum_scatter(g_query, "tok", scatter_dimension=0, tiled=True),
        lax.psum_scatter(g_key, "tok", scatter_dimension=0, tiled=True),
        lax.psum_scatter(g_value, "tok", scatter_dimension=0, tiled=True),
        lax.psum_scatter(g_output, "tok", scatter_dimension=0, tiled=True),
        lax.psum_scatter(g_inner, "tok", scatter_dimension=0, tiled=True),
        lax.psum_scatter(g_outer, "tok", scatter_dimension=0, tiled=True),
        lax.psum_scatter(g_before, "tok", scatter_dimension=1, tiled=True),
        lax.psum_scatter(g_after, "tok", scatter_dimension=1, tiled=True),
        lax.psum_scatter(g_hidden, "tok", scatter_dimension=0, tiled=True),
        lax.psum_scatter(g_gain, "tok", scatter_dimension=1, tiled=True),
        lax.psum_scatter(g_shift, "tok", scatter_dimension=1, tiled=True),
    )
    final_grads = (
        lax.psum(all_parts[0].astype(jnp.bfloat16), "qry").astype(jnp.float32),
        lax.psum(all_parts[1].astype(jnp.bfloat16), "qry").astype(jnp.float32),
        lax.psum(all_parts[2].astype(jnp.bfloat16), "qry").astype(jnp.float32),
        lax.psum(all_parts[3].astype(jnp.bfloat16), "qry").astype(jnp.float32),
        lax.psum(all_parts[4].astype(jnp.bfloat16), "qry").astype(jnp.float32),
        lax.psum(all_parts[5].astype(jnp.bfloat16), "qry").astype(jnp.float32),
        lax.psum(all_parts[6].astype(jnp.bfloat16), "qry").astype(jnp.float32),
        lax.psum(all_parts[7].astype(jnp.bfloat16), "qry").astype(jnp.float32),
        lax.psum(all_parts[8].astype(jnp.bfloat16), "qry").astype(jnp.float32),
        lax.psum(all_parts[9].astype(jnp.bfloat16), "qry").astype(jnp.float32),
        lax.psum(all_parts[10].astype(jnp.bfloat16), "qry").astype(jnp.float32),
    )
    return (
        content_out,
        query_out,
        d_content.reshape(content_in.shape),
        d_query.reshape(query_in.shape),
        final_grads[0],
        final_grads[1],
        final_grads[2],
        final_grads[3],
        final_grads[4],
        final_grads[5],
        final_grads[6],
        final_grads[7],
        final_grads[8],
        final_grads[9],
        final_grads[10],
        g_table,
    )


def solution(mesh):
    placed = (
        P(("tok", "qry"), None, None),
        P("tok", "qry", None),
        P("tok"),
        P("tok", None),
        P(),
        P(),
        P(),
        P(),
        P(),
        P(),
        P(),
        P(),
        P(),
        P(),
        P(),
        P(),
        P(("tok", "qry"), None, None),
        P("tok", "qry", None),
    )
    return jax.shard_map(
        on_device,
        mesh=mesh,
        in_specs=placed,
        out_specs=(
            P(("tok", "qry"), None, None),
            P("tok", "qry", None),
            P(("tok", "qry"), None, None),
            P("tok", "qry", None),
            P("tok", None),
            P("tok", None),
            P("tok", None),
            P("tok", None),
            P("tok", None),
            P("tok", None),
            P(None, "tok"),
            P(None, "tok"),
            P("tok"),
            P(None, "tok"),
            P(None, "tok"),
            P(),
        ),
        check_vma=False,
    )
```

profile of v0, /device:TPU:0, one launch (start us, length us, event | category | flops | bytes accessed | tf_op | source)
XLA Modules:
  0.0 1357.7 jit_solution(16811530737969618237)
XLA Ops:
  7.3 4.4 convolution_convert_fusion.2
  11.9 4.0 add_convert_fusion.2
  22.2 4.1 add_convert_fusion.1
  39.6 8.4 fusion.27
  48.0 17.8 %copy.115 = f32[12,512,512]{1,2,0:T(8,128)} copy(f32[12,512,512]{2,0,1:T(8,128)} %fusion.27) | data formatting | bytes 25165824 | tf_op jit(solution)/shard_map/while | solution.py:121
  67.3 31.2 %while.29 = (s32[]{:T(128)}, bf16[2,1,512,768]{3,2,0,1:T(8,128)(2,1)}, f32[2,1,12,512,1]{3,2,4,1,0:T(8,128)S(1)}, bf16[2,1,512,768]{2,3,1,0:T(8,128)(2,1)}, pred...) while((s32[]{:T(128)}, ...), condition=%wide.region_3.4_spmd, body=%wide.region_0.3_spmd.sunk | while | flops 834004992 | bytes 62349432 | solution.py:121
  70.2 7.7 fusion.212
  86.1 6.3 fusion.212
  98.5 3.4 fusion.107
  103.0 3.9 fusion.26
  107.0 11.3 multiply_convert_fusion.2
  118.3 8.7 copy.119
  127.0 7.5 fusion.109
  138.1 8.7 copy.118
  146.8 6.0 fusion.53
  154.1 3.4 convolution_add_fusion.2
  157.6 4.3 fusion.111
  172.5 7.1 convolution_convert_fusion
  179.6 8.6 copy.136
  190.9 9.7 fusion.108
  206.5 13.4 convert_reduce_fusion
  219.9 6.0 multiply_reduce_fusion.2
  239.3 4.7 multiply_convert_fusion.1
  244.0 8.6 copy.133
  253.4 153.3 %while.30 = (s32[]{:T(128)}, bf16[2,1,512,768]{3,2,0,1:T(8,128)(2,1)}, f32[2,1,512,768]{3,2,0,1:T(8,128)}, f32[2,1,512,768]{3,2,0,1:T(8,128)}, f32[2,1,12,32]{3,...) while((s32[]{:T(128)}, ...), condition=%wide.region_21.22_spmd.clone, body=%wide.region_19.21_spmd.clone.sunk | while | flops 2264000512 | bytes 352059968 | solution.py:121
  259.5 8.8 subtract_exponential_fusion.5
  268.3 3.9 fusion.227
  273.3 3.1 copy.244
  276.4 12.2 multiply_reduce_fusion.13
  288.5 6.7 multiply_convert_fusion.8
  299.2 5.9 convolution_multiply_fusion.7
  307.1 14.5 %copy.246 = bf16[12,512,512]{2,0,1:T(8,128)(2,1)} copy(bf16[12,512,512]{1,2,0:T(8,128)(2,1)} %copy-done.4) | data formatting | bytes 12582912 | tf_op jit(solution)/shard_map/while/body/eval_jaxpr/convert_element_type | solution.py:83
  321.6 6.9 fusion.228
  337.5 6.6 subtract_exponential_fusion.5
  344.1 3.9 fusion.227
  349.1 3.1 copy.244
  352.2 11.4 multiply_reduce_fusion.13
  363.6 6.7 multiply_convert_fusion.8
  374.2 5.9 convolution_multiply_fusion.7
  382.1 14.5 %copy.246 = bf16[12,512,512]{2,0,1:T(8,128)(2,1)} copy(bf16[12,512,512]{1,2,0:T(8,128)(2,1)} %copy-done.4) | data formatting | bytes 12582912 | tf_op jit(solution)/shard_map/while/body/eval_jaxpr/convert_element_type | solution.py:83
  396.6 6.9 fusion.228
  406.8 5.3 convert_reduce_fusion.7
  417.9 4.1 fusion.43
  424.1 3.5 fusion.115
  429.7 3.0 convert_reduce_fusion.4
  445.1 9.4 fusion.97
  454.5 5.1 convolution_add_fusion.1
  459.7 8.0 fusion.116
  467.7 4.5 convolution_add_fusion
  474.4 5.0 fusion.112
  482.7 3.9 fusion.60
  491.1 37.9 %all-reduce = bf16[3072]{0:T(1024)(128)(2,1)S(1)} all-reduce(f32[3072]{0:T(1024)S(1)} %add.584), channel_id=12, replica_groups=mesh['tok'=8,'qry'=4] {'tok'}, use_global_device_ids=true, to_apply=%region_54.55.clone | all-reduce | flops 3072 | bytes 18432
  529.1 36.9 %psum.95 = f32[12,32]{1,0:T(8,128)} all-reduce(f32[12,32]{1,0:T(8,128)S(1)} %copy-done.101), channel_id=1, replica_groups=mesh['tok'=8,'qry'=4] {'tok','qry'}, use_global_device_ids=true, to_apply=%region_69.70 | all-reduce | flops 384 | bytes 3072 | tf_op jit(solution)/shard_map/psum | solution.py:355
  567.8 38.5 %reduce-scatter.45.cloned.1.call-done = f32[96,2]{1,0:T(8,128)} async-done(((f32[768,2]{1,0:T(8,128)}), f32[96,2]{1,0:T(8,128)}) %reduce-scatter.45.cloned.1.call-update) | async-done | bytes 784
  607.2 70.8 %reduce-scatter.37.cloned.1.call-done = f32[96,768]{1,0:T(8,128)} async-done(((f32[768,768]{1,0:T(8,128)}), f32[96,768]{1,0:T(8,128)}) %reduce-scatter.37.cloned.1.call-update) | async-done | bytes 294928
  679.7 70.0 %reduce-scatter.31.cloned.1.call-done = f32[96,768]{1,0:T(8,128)} async-done(((f32[768,768]{1,0:T(8,128)}), f32[96,768]{1,0:T(8,128)}) %reduce-scatter.31.cloned.1.call-update) | async-done | bytes 294928 | tf_op jit(solution)/shard_map/reduce_scatter | solution.py:360
  751.3 69.9 %reduce-scatter.41.cloned.1.call-done = f32[96,768]{1,0:T(8,128)} async-done(((f32[768,768]{1,0:T(8,128)}), f32[96,768]{1,0:T(8,128)}) %reduce-scatter.41.cloned.1.call-update) | async-done | bytes 294928
  823.0 69.9 %reduce-scatter.39.cloned.1.call-done = f32[96,768]{1,0:T(8,128)} async-done(((f32[768,768]{1,0:T(8,128)}), f32[96,768]{1,0:T(8,128)}) %reduce-scatter.39.cloned.1.call-update) | async-done | bytes 294928
  894.7 164.1 %reduce-scatter.33.cloned.1.call-done = f32[96,3072]{1,0:T(8,128)} async-done(((f32[768,3072]{1,0:T(8,128)}), f32[96,3072]{1,0:T(8,128)}) %reduce-scatter.33.cloned.1.call-update) | async-done | bytes 1179664 | tf_op jit(solution)/shard_map/reduce_scatter | solution.py:361
  1060.9 163.9 %reduce-scatter.35.cloned.1.call-done = f32[384,768]{1,0:T(8,128)} async-done(((f32[3072,768]{1,0:T(8,128)}), f32[384,768]{1,0:T(8,128)}) %reduce-scatter.35.cloned.1.call-update) | async-done | bytes 1179664 | tf_op jit(solution)/shard_map/reduce_scatter | solution.py:362
  1230.5 3.1 add_add_fusion.2
  1233.7 54.7 %reduce-scatter.43.cloned.1.call-done = f32[96,2]{1,0:T(8,128)} async-done(((f32[768,2]{1,0:T(8,128)}), f32[96,2]{1,0:T(8,128)}) %reduce-scatter.43.cloned.1.call-update) | async-done | bytes 784
  1289.2 5.7 all-reduce.1
  1297.7 43.0 %all-reduce.5.cloned.1.call-done = (bf16[96,768]{0,1:T(8,128)(2,1)}, bf16[96,768]{0,1:T(8,128)(2,1)}, bf16[96,768]{0,1:T(8,128)(2,1)}, bf16[96,768]{1,0:T(8,128)...) async-done(((bf16[96,768]{0,1:T(8,128)(2,1)}, bf16[96,768]{0,1:T(8,128)(2,1)}, bf16[96,768]{0,1:T(8,128)(2,1)}, bf16[96,768]{1,0:T(8,128)(2,1)}, ...) | async-done | bytes 1769488 | tf_op jit(solution)/shard_map/psum | solution.py:370
  (502 shorter events, 170.9 us)
Async XLA Ops:
  7.2 91.3 %copy-start = (bf16[768,768]{1,0:T(8,128)(2,1)S(1)}, bf16[768,768]{1,0:T(8,128)(2,1)}, u32[]{:S(2)}) copy-start(bf16[768,768]{1,0:T(8,128)(2,1)} %param.29) | copy-start | bytes 3538948
  7.2 111.1 %all-gather.5.cloned.1.call-start = ((), (), s32[]{:S(2)}) async-start(), calls=%async_computation.13 | async-start | bytes 7864320 | tf_op jit(solution)/shard_map/all_gather | solution.py:268
  11.7 126.3 %all-gather.3.cloned.1.call-start = ((), (), s32[]{:S(2)}) async-start(), calls=%async_computation.12 | async-start | bytes 7864320 | tf_op jit(solution)/shard_map/all_gather | solution.py:269
  15.9 413.8 %reduce-scatter.29.cloned.1.call-start = ((), (), s32[]{:S(2)}) async-start(), calls=%async_computation.15 | async-start | bytes 7864320 | tf_op jit(solution)/shard_map/reduce_scatter | solution.py:306
  17.2 22.4 %copy-start.24 = (s32[512,512]{1,0:T(8,128)}, s32[512,512]{1,0:T(8,128)S(1)}, u32[]{:S(2)}) copy-start(s32[512,512]{1,0:T(8,128)S(1)} %fusion.63) | copy-start | bytes 3145732
  48.0 17.8 %copy-start.72 = (s32[8,512]{1,0:T(8,128)S(1)}, s32[8,512]{1,0:T(8,128)}, u32[]{:S(2)}) copy-start(s32[8,512]{1,0:T(8,128)} %param.25) | copy-start | bytes 49156
  48.0 18.8 %copy-start.55 = (pred[512,512]{0,1:T(8,128)(4,1)S(1)}, pred[512,512]{0,1:T(8,128)(4,1)}, u32[]{:S(2)}) copy-start(pred[512,512]{0,1:T(8,128)(4,1)} %iota_compare_fusion.12) | copy-start | bytes 786436
  66.7 124.2 %copy-start.69 = (f32[768]{0:T(1024)}, f32[768]{0:T(1024)S(1)}, u32[]{:S(2)}) copy-start(f32[768]{0:T(1024)S(1)} %get-tuple-element.288) | copy-start | bytes 9220
  66.7 160.4 %copy-start.62 = (f32[768]{0:T(1024)}, f32[768]{0:T(1024)S(1)}, u32[]{:S(2)}) copy-start(f32[768]{0:T(1024)S(1)} %get-tuple-element.400) | copy-start | bytes 9220
  67.3 31.2 %copy-start.85 = (f32[768]{0:T(1024)S(1)}, f32[768]{0:T(1024)}, u32[]{:S(2)}) copy-start(f32[768]{0:T(1024)} %get-tuple-element.290) | copy-start | bytes 9220
  101.9 125.3 %copy-start.64 = (f32[1024]{0:T(1024)}, f32[1024]{0:T(1024)S(1)}, u32[]{:S(2)}) copy-start(f32[1024]{0:T(1024)S(1)} %broadcast_multiply_fusion.1) | copy-start | bytes 12292
  102.4 124.8 %copy-start.66 = (f32[1024]{0:T(1024)}, f32[1024]{0:T(1024)S(1)}, u32[]{:S(2)}) copy-start(f32[1024]{0:T(1024)S(1)} %fusion.91) | copy-start | bytes 12292
  118.3 8.7 copy-start.20
  146.8 6.5 copy-start.44
  153.8 16.0 %copy-start.16 = (f32[160,768]{1,0:T(8,128)}, f32[160,768]{1,0:T(8,128)S(1)}, u32[]{:S(2)}) copy-start(f32[160,768]{1,0:T(8,128)S(1)} %get-tuple-element.387) | copy-start | bytes 1474564
  153.8 16.0 %copy-start.77 = (f32[160]{0:T(256)}, f32[160]{0:T(256)S(1)}, u32[]{:S(2)}) copy-start(f32[160]{0:T(256)S(1)} %broadcast_multiply_fusion.3) | copy-start | bytes 1924
  154.1 15.7 %copy-start.79 = (f32[160]{0:T(256)}, f32[160]{0:T(256)S(1)}, u32[]{:S(2)}) copy-start(f32[160]{0:T(256)S(1)} %fusion.93) | copy-start | bytes 1924
  157.5 7.2 copy-start.22
  157.5 7.2 slice-start.8
  157.5 7.1 slice-start.9
  170.1 9.5 copy-start.99
  172.5 7.1 copy-start.28
  188.3 249.1 %reduce-scatter.27.cloned.1.call-start = ((), (), s32[]{:S(2)}) async-start(), calls=%async_computation.14 | async-start | bytes 7864320 | tf_op jit(solution)/shard_map/reduce_scatter | solution.py:303
  205.5 14.4 %slice-start.6 = ((s8[4718592]{0:T(1024)(128)(4,1)}), s8[4194304]{0:T(1024)(128)(4,1)S(1)}, s32[]{:S(2)}) async-start(s8[4718592]{0:T(1024)(128)(4,1)} %bitcast.297), calls=%async_computation.33 | async-start | bytes 8388608
  205.9 14.0 %copy-start.49 = (bf16[1024,768]{1,0:T(8,128)(2,1)}, bf16[1024,768]{1,0:T(8,128)(2,1)S(1)}, u32[]{:S(2)}) copy-start(bf16[1024,768]{1,0:T(8,128)(2,1)S(1)} %get-tuple-element.353) | copy-start | bytes 4718596
  206.5 13.4 copy-start.8
  206.5 13.4 slice-start.7
  252.7 313.4 %reduce-scatter.49.cloned.1.call-start = ((), (), s32[]{:S(2)}) async-start(), calls=%async_computation.25 | async-start | bytes 442368
  253.4 153.4 %copy-start.88 = (f32[768]{0:T(1024)S(1)}, f32[768]{0:T(1024)}, u32[]{:S(2)}) copy-start(f32[768]{0:T(1024)} %get-tuple-element.282) | copy-start | bytes 9220
  253.4 153.4 %copy-start.82 = (f32[768]{0:T(1024)S(1)}, f32[768]{0:T(1024)}, u32[]{:S(2)}) copy-start(f32[768]{0:T(1024)} %get-tuple-element.280) | copy-start | bytes 9220
  253.4 153.4 %copy-start.81 = (f32[768]{0:T(1024)S(1)}, f32[768]{0:T(1024)}, u32[]{:S(2)}) copy-start(f32[768]{0:T(1024)} %get-tuple-element.284) | copy-start | bytes 9220
  276.4 12.2 copy-start.3
  307.1 14.5 %copy-start.25 = (s32[512,512]{1,0:T(8,128)S(1)}, s32[512,512]{1,0:T(8,128)}, u32[]{:S(2)}) copy-start(s32[512,512]{1,0:T(8,128)} %get-tuple-element.613) | copy-start | bytes 3145732 | tf_op jit(solution)/shard_map/while
  321.6 6.9 copy-start.5
  321.6 6.9 copy-start.36
  321.6 6.9 copy-start.38
  352.2 11.4 copy-start.3
  382.1 14.5 %copy-start.25 = (s32[512,512]{1,0:T(8,128)S(1)}, s32[512,512]{1,0:T(8,128)}, u32[]{:S(2)}) copy-start(s32[512,512]{1,0:T(8,128)} %get-tuple-element.613) | copy-start | bytes 3145732 | tf_op jit(solution)/shard_map/while
  396.6 6.9 copy-start.5
  396.6 6.9 copy-start.36
  396.6 6.9 copy-start.38
  406.8 6.8 copy-start.68
  415.7 151.2 %reduce-scatter.47.cloned.1.call-start = ((), (), s32[]{:S(2)}) async-start(), calls=%async_computation.24 | async-start | bytes 442368
  416.8 189.5 %reduce-scatter.45.cloned.1.call-start = ((), (), s32[]{:S(2)}) async-start(), calls=%async_computation.23 | async-start | bytes 442368
  417.9 260.1 %reduce-scatter.37.cloned.1.call-start = ((), (), s32[]{:S(2)}) async-start(), calls=%async_computation.19 | async-start | bytes 2654208
  424.0 325.7 %reduce-scatter.31.cloned.1.call-start = ((), (), s32[]{:S(2)}) async-start(), calls=%async_computation.16 | async-start | bytes 2654208 | tf_op jit(solution)/shard_map/reduce_scatter | solution.py:360
  429.6 391.6 %reduce-scatter.41.cloned.1.call-start = ((), (), s32[]{:S(2)}) async-start(), calls=%async_computation.21 | async-start | bytes 2654208
  437.3 455.5 %reduce-scatter.39.cloned.1.call-start = ((), (), s32[]{:S(2)}) async-start(), calls=%async_computation.20 | async-start | bytes 2654208
  445.0 9.5 copy-start.17
  445.0 9.5 copy-start.35
  445.0 9.5 copy-start.78
  445.0 9.5 copy-start.80
  445.0 613.7 %reduce-scatter.33.cloned.1.call-start = ((), (), s32[]{:S(2)}) async-start(), calls=%async_computation.17 | async-start | bytes 10616832 | tf_op jit(solution)/shard_map/reduce_scatter | solution.py:361
  459.6 8.1 copy-start.23
  459.6 8.1 copy-start.58
  459.7 765.1 %reduce-scatter.35.cloned.1.call-start = ((), (), s32[]{:S(2)}) async-start(), calls=%async_computation.18 | async-start | bytes 10616832 | tf_op jit(solution)/shard_map/reduce_scatter | solution.py:362
  472.2 816.1 %reduce-scatter.43.cloned.1.call-start = ((), (), s32[]{:S(2)}) async-start(), calls=%async_computation.22 | async-start | bytes 442368
  474.4 8.2 copy-start.12
  487.5 41.6 %copy-start.101 = (f32[12,32]{1,0:T(8,128)S(1)}, f32[12,32]{1,0:T(8,128)}, u32[]{:S(2)}) copy-start(f32[12,32]{1,0:T(8,128)} %fusion.60) | copy-start | bytes 4612
  487.5 853.2 %all-reduce.5.cloned.1.call-start = ((), (), s32[]{:S(2)}) async-start(), calls=%async_computation.26 | async-start | bytes 3833856 | tf_op jit(solution)/shard_map/psum | solution.py:370
  751.3 475.6 %copy-start.52 = (bf16[2,512,768]{2,1,0:T(8,128)(2,1)S(1)}, bf16[2,512,768]{2,1,0:T(8,128)(2,1)}, u32[]{:S(2)}) copy-start(bf16[2,512,768]{2,1,0:T(8,128)(2,1)} %copy-done.51) | copy-start | bytes 4718596
  751.3 475.6 %copy-start.111 = (bf16[768,768]{1,0:T(8,128)(2,1)S(1)}, bf16[768,768]{1,0:T(8,128)(2,1)}, u32[]{:S(2)}) copy-start(bf16[768,768]{1,0:T(8,128)(2,1)} %param.27) | copy-start | bytes 3538948
  1230.5 120.5 %copy-start.1 = (bf16[768,768]{1,0:T(8,128)(2,1)S(1)}, bf16[768,768]{1,0:T(8,128)(2,1)}, u32[]{:S(2)}) copy-start(bf16[768,768]{1,0:T(8,128)(2,1)} %param.29) | copy-start | bytes 3538948
  1340.7 9.2 copy-start.59
  (89 other events, 294.9 us)
Sparse Core Ops, SparseCore 0:
  11.8 49.0 all-gather.4
  63.1 46.3 all-gather.2
  188.4 61.1 reduce-scatter.28
  252.8 61.1 reduce-scatter.26
  415.8 63.2 reduce-scatter.48
  482.2 60.3 reduce-scatter.46
  545.9 60.3 reduce-scatter.44
  609.8 68.0 reduce-scatter.36
  681.4 68.2 reduce-scatter.30
  753.0 68.1 reduce-scatter.40
  824.7 68.1 reduce-scatter.38
  896.3 162.3 reduce-scatter.32
  1062.3 162.3 reduce-scatter.34
  1227.9 60.4 reduce-scatter.42
  1292.1 48.5 all-reduce.4
where the time goes:
time: 1370 us; the launch traced here: 1360 us
  waiting for transfers between devices  745 us (54%)
  matrix products  269 us (20%)
  local copies, waits for them, and re-layouts  190 us (14%)
  blocking collectives  80.5 us (6%)
  other arithmetic  55.1 us (4%)
  between operations  16.4 us (1%)
    unnamed x22, waiting for transfers between devices  304 us
    reduce_scatter x1, waiting for transfers between devices, on_device(): lax.psum_scatter(g_inner, 'tok', scatter_dimension=0, tiled=True)  164 us
    reduce_scatter x1, waiting for transfers between devices, on_device(): lax.psum_scatter(g_outer, 'tok', scatter_dimension=0, tiled=True)  164 us
    reduce_scatter x1, waiting for transfers between devices, on_device(): lax.psum_scatter(g_output, 'tok', scatter_dimension=0, tiled=True)  70 us
    psum x1, waiting for transfers between devices, on_device(): lax.psum(all_parts[0].astype(jnp.bfloat16), 'qry').astype(jnp.float32)  43 us
    unnamed x246, local copies, waits for them, and re-layouts  40.8 us
    unnamed x1, blocking collectives  37.9 us
    dot_general x5, matrix products, score_block(): jnp.einsum('akop,anop->aokn', split_into_heads(query_vectors), split_into...  37 us
  transfers between devices with their start and end apart: 15, of which 9 were waited for; matrix products, arithmetic and copies ran while one was open for 31% of the time, Pallas kernels for 0%

commit v1 on v0

v1 whole, which is shorter than its diff:
```python
import functools

import jax
import jax.numpy as jnp
from jax import lax
from jax.experimental import pallas as pl
from jax.experimental.pallas import tpu as pltpu
from jax.sharding import PartitionSpec as P

HEADS = 12
HEAD = 64
BUCKETS = 32
PRED = 80
EPS = 1e-05
NEG = -1e30
BORDERS = (12, 16, 23, 32, 46, 64, 91)
LOG2E = 1.4426950408889634
LN2 = 0.6931471805599453
SQRT_HALF = 0.7071067811865476
INV_ROOT = 0.3989422804014327
F32 = jnp.float32
BF16 = jnp.bfloat16
PAIRS = HEADS // 2
TILE = 128
VMEM_LIMIT = 60 * 1024 * 1024
STEP = 320
BACK_STEP = 256
SUB = 64
CHUNK = 768
GRAD_TILE = 512


def nn(a, b):
    return lax.dot_general(a, b, (((1,), (0,)), ((), ())), preferred_element_type=F32)


def nt(a, b):
    return lax.dot_general(a, b, (((1,), (1,)), ((), ())), preferred_element_type=F32)


def tn(a, b):
    return lax.dot_general(a, b, (((0,), (0,)), ((), ())), preferred_element_type=F32)


def bucket_of(offset):
    distance = jnp.abs(offset)
    beyond = 8 + sum(((distance >= border).astype(jnp.int32) for border in BORDERS))
    return jnp.where(distance < 8, distance, beyond) + 16 * (offset > 0).astype(jnp.int32)


def full_spec(shape):
    zeros = (0,) * len(shape)
    return pl.BlockSpec(shape, lambda *_: zeros, pipeline_mode=pl.Buffered(1))


def params():
    return pltpu.CompilerParams(vmem_limit_bytes=VMEM_LIMIT)


def slot_position(rank_row, slot_rank, width):
    lanes = lax.broadcasted_iota(jnp.int32, (1, width), 1).astype(F32)
    place = jnp.sum(jnp.where(rank_row == slot_rank, lanes, 0.0), axis=1, keepdims=True)
    place = place.astype(jnp.int32)
    return place >> 7, place & 127


def pieces(start, size, length, sub):
    at = start
    while at < start + size:
        limit = length if at < length else start + size
        many = min(sub, start + size - at, limit - at)
        yield at, many
        at += many


def row_steps(total, step):
    return [(at, min(step, total - at)) for at in range(0, total, step)]


def plus(total, term):
    return term if total is None else total + term


def attention_forward_kernel(
    xc, xq, wq, wk, wv, before, rank_row, thr_c, thr_q, offsets, table,
    ctx_out, e_out, rr_out, q_out, k_out, v_out, mask, s_buf,
):
    pair = pl.program_id(1)
    length = xc.shape[1]
    slots = xq.shape[1]
    total = length + slots
    tiles = length // TILE

    @pl.when(pair == 0)
    def _():
        scale = 0.125 * LOG2E
        x = xc[0]
        bias = before[...].astype(F32)
        q_out[0, :length] = ((nn(x, wq[...]) + bias[0:1]) * scale).astype(BF16)
        k_out[0] = nn(x, wk[...]).astype(BF16)
        v_out[0] = (nn(x, wv[...]) + bias[1:2]).astype(BF16)
        q_out[0, length:] = ((nn(xq[0], wq[...]) + bias[0:1]) * scale).astype(BF16)
        ranks = rank_row[0]
        for i in range(tiles):
            rows = slice(i * TILE, (i + 1) * TILE)
            seen = ranks < thr_c[0, rows]
            row = lax.broadcasted_iota(jnp.int32, (TILE, length), 0) + i * TILE
            col = lax.broadcasted_iota(jnp.int32, (TILE, length), 1)
            mask[rows] = jnp.where(seen | (row == col), 0.0, NEG)
        mask[length:] = jnp.where(ranks < thr_q[0], 0.0, NEG)

    cols = pl.ds(pl.multiple_of(pair * TILE, TILE), TILE)
    k_pair = k_out[0, :, cols]
    v_pair = v_out[0, :, cols]
    q_pair = q_out[0, :, cols]
    lane = lax.broadcasted_iota(jnp.int32, (1, TILE), 1)
    block_of, row_of = slot_position(rank_row[0], thr_q[0], length)
    pick = (row_of == lax.broadcasted_iota(jnp.int32, (slots, TILE), 1)).astype(BF16)
    zero = jnp.zeros((), BF16)
    setup = []
    for h in range(2):
        own = (lane < HEAD) if h == 0 else (lane >= HEAD)
        strip = pltpu.roll(
            jnp.broadcast_to(offsets[h], (TILE, 512)), 0, 1, stride=1, stride_axis=0
        )[:, : 3 * TILE]
        setup.append((
            jnp.where(own, q_pair, zero),
            jnp.where(own, v_pair, zero),
            strip * LOG2E,
            nn(pick, strip.astype(BF16)) * LOG2E,
            table[2 * pair + h, 15] * LOG2E,
            table[2 * pair + h, 31] * LOG2E,
        ))
    inverse = {}
    context = {}

    def scores(h, at, size):
        s_buf[h, at : at + size] = nt(setup[h][0][at : at + size], k_pair)

    def normalise(h, at, size):
        strip, slot_strip, far_low, far_high = setup[h][2:]
        for t, m in pieces(at, size, length, SUB):
            s = s_buf[h, t : t + m]
            parts = []
            for j in range(tiles):
                if t < length:
                    i, a = t // TILE, t % TILE
                    d = j - i + 1
                    if 0 <= d <= 2:
                        bias = strip[a : a + m, d * TILE : (d + 1) * TILE]
                    else:
                        bias = far_high if j > i else far_low
                else:
                    a = t - length
                    away = j - block_of[a : a + m]
                    bias = jnp.where(away >= 2, far_high, far_low)
                    for d in range(3):
                        near = slot_strip[a : a + m, d * TILE : (d + 1) * TILE]
                        bias = jnp.where(away == d - 1, near, bias)
                parts.append(s[:, j * TILE : (j + 1) * TILE] + bias)
            s = jnp.concatenate(parts, axis=1) + mask[t : t + m]
            top = jnp.max(s, axis=1, keepdims=True)
            e = jnp.exp2(s - top)
            e_out[0, h, t : t + m] = e.astype(BF16)
            inverse[h, t] = 1.0 / jnp.sum(e, axis=1, keepdims=True)

    def attend(h, at, size):
        context[h, at] = nn(e_out[0, h, at : at + size], setup[h][1])
        if h == 0:
            return
        both = context.pop((0, at)) + context.pop((1, at))
        for t, m in pieces(at, size, length, SUB):
            r = jnp.where(lane < HEAD, inverse[0, t], inverse[1, t])
            rr_out[0, t : t + m] = r
            ctx_out[0, t : t + m] = (both[t - at : t - at + m] * r).astype(BF16)

    work = [(h, at, size) for at, size in row_steps(total, STEP) for h in range(2)]
    scores(*work[0])
    for n, item in enumerate(work):
        if n + 1 < len(work):
            scores(*work[n + 1])
        normalise(*item)
        if n:
            attend(*work[n - 1])
    attend(*work[-1])


def attention_forward(xc, xq, wq, wk, wv, before, rank_row, thr_c, thr_q, offsets, table):
    seqs, length, width = xc.shape
    slots = xq.shape[1]
    rows = length + slots

    def by_seq(shape):
        return pl.BlockSpec((1,) + shape, lambda s, p: (s, 0, 0))

    by_pair = pl.BlockSpec((1, rows, TILE), lambda s, p: (s, 0, p))
    return pl.pallas_call(
        attention_forward_kernel,
        grid=(seqs, PAIRS),
        in_specs=[
            by_seq((length, width)),
            by_seq((slots, width)),
            full_spec((width, width)),
            full_spec((width, width)),
            full_spec((width, width)),
            full_spec((2, width)),
            by_seq((1, length)),
            by_seq((length, 1)),
            by_seq((slots, 1)),
            pl.BlockSpec((2, 1, 512), lambda s, p: (p, 0, 0)),
            pl.BlockSpec(memory_space=pltpu.SMEM),
        ],
        out_specs=[
            by_pair,
            pl.BlockSpec((1, 2, rows, length), lambda s, p: (s, p, 0, 0)),
            by_pair,
            by_seq((rows, width)),
            by_seq((length, width)),
            by_seq((length, width)),
        ],
        out_shape=[
            jax.ShapeDtypeStruct((seqs, rows, width), BF16),
            jax.ShapeDtypeStruct((seqs, HEADS, rows, length), BF16),
            jax.ShapeDtypeStruct((seqs, rows, width), F32),
            jax.ShapeDtypeStruct((seqs, rows, width), BF16),
            jax.ShapeDtypeStruct((seqs, length, width), BF16),
            jax.ShapeDtypeStruct((seqs, length, width), BF16),
        ],
        scratch_shapes=[pltpu.VMEM((rows, length), F32), pltpu.VMEM((2, rows, length), F32)],
        compiler_params=params(),
        name="attention_forward",
    )(xc, xq, wq, wk, wv, before, rank_row, thr_c, thr_q, offsets, table)


def attention_backward_kernel(
    first, q, k, v, e_in, ctx, d_ctx, rr, rank_row, thr_q,
    dq_out, dk_out, dv_out, sums, table_out, near_acc, far_acc, dp_buf, ds_buf, sums_acc,
):
    seq = pl.program_id(1)
    length = k.shape[1]
    slots = thr_q.shape[1]
    total = length + slots
    tiles = length // TILE

    @pl.when(seq == 0)
    def _():
        near_acc[...] = jnp.zeros_like(near_acc)
        far_acc[...] = jnp.zeros_like(far_acc)
        sums_acc[...] = jnp.zeros_like(sums_acc)

    lane = lax.broadcasted_iota(jnp.int32, (1, TILE), 1)
    block_of, row_of = slot_position(rank_row[0], thr_q[0], length)
    pick = (row_of == lax.broadcasted_iota(jnp.int32, (slots, TILE), 1)).astype(BF16)
    q_pair, k_pair, v_pair = q[0], k[0], v[0]
    d_context = d_ctx[0].astype(F32) * rr[0]
    product = d_context * ctx[0].astype(F32)
    zero = jnp.zeros((), BF16)
    low_d = d_context.astype(BF16)
    d_turned, q_turned = low_d.T, q_pair.T
    setup = []
    for h in range(2):
        own = (lane < HEAD) if h == 0 else (lane >= HEAD)
        setup.append((
            jnp.where(own, k_pair, zero),
            jnp.where(own, low_d, zero),
            jnp.sum(jnp.where(own, product, 0.0), axis=1, keepdims=True),
        ))
    near = [[{}, {}, {}], [{}, {}, {}]]
    far = [[None, None], [None, None]]
    spread = [None, None]
    dq, dk, dv = {}, [None, None], [None, None]

    def fold(x):
        return jnp.sum(x.reshape(-1, 8, TILE), axis=0)

    def d_probs(h, at, size):
        dp_buf[h, at : at + size] = nt(setup[h][1][at : at + size], v_pair)

    def d_scores(h, at, size):
        for t, m in pieces(at, size, length, SUB):
            ds = e_in[0, h, t : t + m].astype(F32) * (dp_buf[h, t : t + m] - setup[h][2][t : t + m])
            ds_buf[h, t : t + m] = ds.astype(BF16)
            parts = [ds[:, j * TILE : (j + 1) * TILE] for j in range(tiles)]
            if t < length:
                i, a = t // TILE, t % TILE
                for j in range(tiles):
                    if abs(j - i) <= 1:
                        group = near[h][j - i + 1]
                        group[a] = plus(group.get(a), parts[j])
                    else:
                        side = 1 if j > i else 0
                        far[h][side] = plus(far[h][side], fold(parts[j]))
            else:
                a = t - length
                slot_near = [0.0] * 3
                low = high = 0.0
                for j in range(tiles):
                    away = j - block_of[a : a + m]
                    for d in range(3):
                        slot_near[d] = slot_near[d] + jnp.where(away == d - 1, parts[j], 0.0)
                    high = high + jnp.where(away >= 2, parts[j], 0.0)
                    low = low + jnp.where(away <= -2, parts[j], 0.0)
                far[h][0] = plus(far[h][0], fold(low))
                far[h][1] = plus(far[h][1], fold(high))
                slot_near = jnp.concatenate(slot_near, axis=1).astype(BF16)
                spread[h] = plus(spread[h], tn(pick[a : a + m], slot_near))

    def d_queries(h, at, size):
        dq[at] = plus(dq.get(at), nn(ds_buf[h, at : at + size], setup[h][0]))

    def d_values(h):
        dv[h] = nn(d_turned[h * HEAD : (h + 1) * HEAD], e_in[0, h])

    def d_keys(h):
        dk[h] = nn(q_turned[h * HEAD : (h + 1) * HEAD], ds_buf[h])

    steps = row_steps(total, BACK_STEP)
    work = [(h, at, size) for h in range(2) for at, size in steps]
    d_probs(*work[0])
    d_values(0)
    for n, item in enumerate(work):
        if n + 1 < len(work):
            d_probs(*work[n + 1])
        d_scores(*item)
        if n == len(steps) - 1:
            d_values(1)
        if n:
            d_queries(*work[n - 1])
        if n == len(steps):
            d_keys(0)
    d_queries(*work[-1])
    d_keys(1)

    for h in range(2):
        columns = [
            jnp.concatenate([group[a] for a in sorted(group)], axis=0) for group in near[h]
        ]
        near_acc[h] += jnp.concatenate(columns, axis=1) + spread[h]
        far_acc[h, 0] += far[h][0]
        far_acc[h, 1] += far[h][1]
    dq_sum = None
    for at, size in steps:
        low = (dq[at] * 0.125).astype(BF16)
        dq_out[0, at : at + size] = low
        dq_sum = plus(dq_sum, fold(low.astype(F32)))
    dk_out[0] = (jnp.concatenate(dk, axis=0).T * LN2).astype(BF16)
    low = jnp.concatenate(dv, axis=0).T.astype(BF16)
    dv_out[0] = low
    sums_acc[0] += dq_sum
    sums_acc[1] += fold(low.astype(F32))

    @pl.when(seq == pl.num_programs(1) - 1)
    def _():
        for n in range(2):
            sums[n : n + 1] = jnp.sum(sums_acc[n], axis=0, keepdims=True)
        row = lax.broadcasted_iota(jnp.int32, (8, 512), 0)
        place = lax.broadcasted_iota(jnp.int32, (512, TILE), 0)
        bucket = bucket_of(jnp.where(place < 384, place, place - 512) - 128)
        column = lax.broadcasted_iota(jnp.int32, (512, TILE), 1)
        one_hot = (bucket == column).astype(BF16)
        lane32 = lax.broadcasted_iota(jnp.int32, (1, TILE), 1)
        for h in range(2):
            x = jnp.concatenate([near_acc[h], jnp.zeros((TILE, 512 - 3 * TILE), F32)], axis=1)
            half = TILE // 2
            while half >= 8:
                x = x[:half] + pltpu.roll(x[half:], 512 - half, 1)
                half //= 2
            for bit in (4, 2, 1):
                x = jnp.where((row & bit) != 0, pltpu.roll(x, 512 - bit, 1), x)
            high = x.astype(BF16)
            rest = (x - high.astype(F32)).astype(BF16)
            total_h = jnp.sum(nn(high, one_hot) + nn(rest, one_hot), axis=0, keepdims=True)
            low_far = jnp.sum(far_acc[h, 0])
            high_far = jnp.sum(far_acc[h, 1])
            total_h = total_h + jnp.where(lane32 == 15, low_far, 0.0)
            table_out[0, h : h + 1] = total_h + jnp.where(lane32 == 31, high_far, 0.0)


def attention_backward(half, q, k, v, e, ctx, d_ctx, rr, rank_row, thr_q):
    seqs, length, width = k.shape
    rows = q.shape[1]
    slots = rows - length
    count = PAIRS // 2

    def pick(n):
        return pl.BlockSpec((1, n, TILE), lambda p, s, half: (s, 0, half[0] * count + p))

    def put(n):
        return pl.BlockSpec((1, n, TILE), lambda p, s, half: (s, 0, p))

    def by_seq(shape):
        return pl.BlockSpec((1,) + shape, lambda p, s, half: (s, 0, 0))

    wide = count * TILE
    return pl.pallas_call(
        attention_backward_kernel,
        grid_spec=pltpu.PrefetchScalarGridSpec(
            num_scalar_prefetch=1,
            grid=(count, seqs),
            in_specs=[
                pick(rows), pick(length), pick(length),
                pl.BlockSpec(
                    (1, 2, rows, length), lambda p, s, half: (s, half[0] * count + p, 0, 0)
                ),
                pick(rows), pick(rows), pick(rows),
                by_seq((1, length)), by_seq((slots, 1)),
            ],
            out_specs=[
                put(rows), put(length), put(length),
                pl.BlockSpec((2, TILE), lambda p, s, half: (0, p)),
                pl.BlockSpec((1, 2, TILE), lambda p, s, half: (p, 0, 0)),
            ],
            scratch_shapes=[
                pltpu.VMEM((2, TILE, 3 * TILE), F32),
                pltpu.VMEM((2, 2, 8, TILE), F32),
                pltpu.VMEM((2, rows, length), F32),
                pltpu.VMEM((2, rows, length), BF16),
                pltpu.VMEM((2, 8, TILE), F32),
            ],
        ),
        out_shape=[
            jax.ShapeDtypeStruct((seqs, rows, wide), BF16),
            jax.ShapeDtypeStruct((seqs, length, wide), BF16),
            jax.ShapeDtypeStruct((seqs, length, wide), BF16),
            jax.ShapeDtypeStruct((2, wide), F32),
            jax.ShapeDtypeStruct((count, 2, TILE), F32),
        ],
        compiler_params=params(),
        name="attention_backward",
    )(half, q, k, v, e, ctx, d_ctx, rr, rank_row, thr_q)


def normal_parts(u):
    density = jnp.exp2((-0.5 * LOG2E) * (u * u))
    t = 1.0 / (1.0 + (0.3275911 * SQRT_HALF) * jnp.abs(u))
    tail = t * (
        0.127414796
        + t * (-0.142248368 + t * (0.7107068705 + t * (-0.7265760135 + t * 0.5307027145)))
    )
    tail = tail * density
    return jnp.where(u >= 0, 1.0 - tail, tail), density


def norm_parts(u):
    mean = jnp.mean(u, axis=1, keepdims=True)
    centre = u - mean
    spread = jnp.mean(centre * centre, axis=1, keepdims=True)
    scale = lax.rsqrt(spread + EPS)
    return centre * scale, scale


def norm_back(y, gain, unit, scale):
    e = y * gain
    mean = jnp.mean(e, axis=1, keepdims=True)
    along = jnp.mean(e * unit, axis=1, keepdims=True)
    return (e - mean - unit * along) * scale


def column_sum(x):
    return jnp.sum(x.reshape(-1, 8, x.shape[1]), axis=0)


def weight_copies(w_output, w_inner, w_outer, wo, wi, wu, sems, forward):
    first = [pltpu.make_async_copy(w_output, wo, sems.at[0])]
    chunks = []
    for n in range(w_inner.shape[1] // CHUNK):
        part = pl.ds(n * CHUNK, CHUNK)
        inner = pltpu.make_async_copy(w_inner.at[:, part], wi.at[:, part], sems.at[1 + 2 * n])
        outer = pltpu.make_async_copy(w_outer.at[part], wu.at[part], sems.at[2 + 2 * n])
        chunks += [inner, outer] if forward else [outer, inner]
    return first + chunks if forward else chunks + first


def weight_scratch(width, ff):
    return [
        pltpu.VMEM((width, width), BF16),
        pltpu.VMEM((width, ff), BF16),
        pltpu.VMEM((ff, width), BF16),
        pltpu.SemaphoreType.DMA((1 + 2 * (ff // CHUNK),)),
    ]


def rows_forward_kernel(
    half, ctx, xc, xq, cot_c, cot_q, w_output, w_inner, w_outer, after, hidden_bias, gain, shift,
    out_c, out_q, slope_out, hidden_out, unit_out, scale_out, outer_out, sums, grad_other, grad_mine,
    wo, wi, wu, sems, acc, act, outer, sums_acc,
):
    step = pl.program_id(0)
    seqs = pl.num_programs(0) - act.shape[1] // GRAD_TILE
    rows = acc.shape[0]

    def row_part():
        copies = weight_copies(w_output, w_inner, w_outer, wo, wi, wu, sems, True)

        @pl.when(step == 0)
        def _():
            for copy in copies:
                copy.start()

        def ready(n):
            @pl.when(step == 0)
            def _():
                copies[n].wait()

        at = pl.multiple_of(step * rows, 16)
        length = xc.shape[1]
        after_f, gain_f, shift_f = (a[...].astype(F32) for a in (after, gain, shift))
        stream = jnp.concatenate([xc[0], xq[0]], axis=0).astype(F32)
        ready(0)
        first = stream + nn(ctx[0], wo[...]) + after_f[0:1]
        unit, scale = norm_parts(first)
        unit_out[...] = unit.astype(BF16)
        scale_out[...] = jnp.broadcast_to(scale, scale_out.shape)
        hidden = unit * gain_f[0:1] + shift_f[0:1]
        low = hidden.astype(BF16)
        hidden_out[...] = low
        acc[...] = hidden + after_f[1:2]
        for n in range(wi.shape[1] // CHUNK):
            part = slice(n * CHUNK, (n + 1) * CHUNK)
            ready(1 + 2 * n)
            u = nn(low, wi[:, part]) + hidden_bias[:, part].astype(F32)
            phi, density = normal_parts(u)
            active = (u * phi).astype(BF16)
            act[pl.ds(at, rows), part] = active
            slope_out[:, part] = (phi + u * density * INV_ROOT).astype(BF16)
            ready(2 + 2 * n)
            acc[...] += nn(active, wu[part, :])
        unit2, scale2 = norm_parts(acc[...])
        out = (unit2 * gain_f[1:2] + shift_f[1:2]).astype(BF16)
        out_c[0] = out[:length]
        out_q[0] = out[length:]
        y = jnp.concatenate([cot_c[0], cot_q[0]], axis=0).astype(F32)
        d_second = norm_back(y, gain_f[1:2], unit2, scale2)
        d_outer = d_second.astype(BF16)
        outer_out[...] = d_outer
        outer[pl.ds(at, rows)] = d_outer
        terms = [column_sum(y * unit2), column_sum(y), column_sum(d_outer.astype(F32))]
        for n, term in enumerate(terms):
            sums_acc[n] += term
            sums[n : n + 1] = jnp.sum(sums_acc[n], axis=0, keepdims=True)

    @pl.when(step == 0)
    def _():
        for acc_ref in (sums_acc,):
            acc_ref[...] = jnp.zeros_like(acc_ref)

    @pl.when(step < seqs)
    def _():
        row_part()

    @pl.when(step >= seqs)
    def _():
        cols = pl.ds(pl.multiple_of((step - seqs) * GRAD_TILE, GRAD_TILE), GRAD_TILE)
        grad = tn(act[:, cols], outer[...]).astype(BF16)
        part = grad.shape[1] // 2
        first = half[0] == 0
        grad_mine[...] = jnp.where(first, grad[:, :part], grad[:, part:])
        grad_other[...] = jnp.where(first, grad[:, part:], grad[:, :part])


def rows_backward_kernel(
    half, outer, slope, unit, scale, hidden, ctx, w_output, w_inner, w_outer, gain,
    first_c, first_q, d_ctx, sums, inner_sums, grad_other, grad_mine,
    wo, wi, wu, sems, acc, inner, attended, hidden_t, ctx_t, sums_acc, inner_acc,
):
    step = pl.program_id(0)
    tiles = 3
    seqs = pl.num_programs(0) - 2 * tiles
    rows = acc.shape[0]
    width, ff = wi.shape

    def row_part():
        copies = weight_copies(w_output, w_inner, w_outer, wo, wi, wu, sems, False)

        @pl.when(step == 0)
        def _():
            for copy in copies:
                copy.start()

        def ready(n):
            @pl.when(step == 0)
            def _():
                copies[n].wait()

        at = pl.multiple_of(step * rows, 16)
        acc[...] = outer[...].astype(F32)
        chunks = ff // CHUNK
        for n in range(chunks):
            part = slice(n * CHUNK, (n + 1) * CHUNK)
            ready(2 * n)
            d_act = nt(outer[...], wu[part, :])
            d_inner = (d_act * slope[:, part].astype(F32)).astype(BF16)
            inner[pl.ds(at, rows), part] = d_inner
            term = column_sum(d_inner.astype(F32))
            inner_acc[:, part] += term
            ready(2 * n + 1)
            acc[...] += nt(d_inner, wi[:, part])
        inner_sums[...] = jnp.sum(inner_acc[...], axis=0, keepdims=True)
        unit1 = unit[...].astype(F32)
        d_hidden = acc[...]
        d_first = norm_back(d_hidden, gain[0:1].astype(F32), unit1, scale[:, :1])
        length = first_c.shape[1]
        first_c[0] = d_first[:length]
        first_q[0] = d_first[length:]
        low = d_first.astype(BF16)
        attended[pl.ds(at, rows)] = low
        ready(2 * chunks)
        d_ctx[0] = nt(low, wo[...]).astype(BF16)
        terms = [column_sum(d_hidden * unit1), column_sum(d_hidden), column_sum(low.astype(F32))]
        for n, term in enumerate(terms):
            sums_acc[n] += term
            sums[n : n + 1] = jnp.sum(sums_acc[n], axis=0, keepdims=True)

    @pl.when(step == 0)
    def _():
        for acc_ref in (sums_acc, inner_acc):
            acc_ref[...] = jnp.zeros_like(acc_ref)

    @pl.when(step < seqs)
    def _():
        row_part()

    @pl.when(step == seqs)
    def _():
        hidden_t[...] = hidden[...].T
        ctx_t[...] = ctx[...].T

    wide, narrow = ff // 2 // tiles, width // 2 // tiles

    def grad(which, tile):
        at = pl.multiple_of(which * (ff // 2) + tile * wide, wide)
        to = pl.multiple_of(which * (width // 2) + tile * narrow, narrow)
        left = nn(hidden_t[...], inner[:, pl.ds(at, wide)]).astype(BF16)
        right = nn(ctx_t[...], attended[:, pl.ds(to, narrow)]).astype(BF16)
        return jnp.concatenate([left, right], axis=1)

    @pl.when(jnp.logical_and(step >= seqs, step < seqs + tiles))
    def _():
        grad_other[...] = grad(1 - half[0], step - seqs)

    @pl.when(step >= seqs + tiles)
    def _():
        grad_mine[...] = grad(half[0], step - seqs - tiles)


def rows_forward(
    half, ctx, xc, xq, cot_c, cot_q, w_output, w_inner, w_outer, after, hidden_bias, gain, shift
):
    seqs, rows, width = ctx.shape
    length, slots = xc.shape[1], xq.shape[1]
    ff = w_inner.shape[1]
    total = seqs * rows

    def by_seq(n):
        return pl.BlockSpec((1, n, width), lambda s, half: (jnp.minimum(s, seqs - 1), 0, 0))

    def block(n):
        return pl.BlockSpec((rows, n), lambda s, half: (jnp.minimum(s, seqs - 1), 0))

    grad_block = pl.BlockSpec(
        (GRAD_TILE, width // 2), lambda s, half: (jnp.maximum(s - seqs, 0), 0)
    )
    hbm = pl.BlockSpec(memory_space=pl.ANY)
    return pl.pallas_call(
        rows_forward_kernel,
        grid_spec=pltpu.PrefetchScalarGridSpec(
            num_scalar_prefetch=1,
            grid=(seqs + ff // GRAD_TILE,),
            in_specs=[
            by_seq(rows), by_seq(length), by_seq(slots), by_seq(length), by_seq(slots),
            hbm, hbm, hbm,
            full_spec((2, width)), full_spec((1, ff)), full_spec((2, width)), full_spec((2, width)),
        ],
        out_specs=[
            by_seq(length), by_seq(slots), block(ff), block(width),
            block(width), block(TILE), block(width), full_spec((3, width)),
            grad_block, grad_block,
        ],
        scratch_shapes=weight_scratch(width, ff) + [
            pltpu.VMEM((rows, width), F32),
            pltpu.VMEM((total, ff), BF16),
            pltpu.VMEM((total, width), BF16),
            pltpu.VMEM((3, 8, width), F32),
        ],
        ),
        out_shape=[
            jax.ShapeDtypeStruct((seqs, length, width), BF16),
            jax.ShapeDtypeStruct((seqs, slots, width), BF16),
            jax.ShapeDtypeStruct((total, ff), BF16),
            jax.ShapeDtypeStruct((total, width), BF16),
            jax.ShapeDtypeStruct((total, width), BF16),
            jax.ShapeDtypeStruct((total, TILE), F32),
            jax.ShapeDtypeStruct((total, width), BF16),
            jax.ShapeDtypeStruct((3, width), F32),
            jax.ShapeDtypeStruct((ff, width // 2), BF16),
            jax.ShapeDtypeStruct((ff, width // 2), BF16),
        ],
        compiler_params=params(),
        name="rows_forward",
    )(half, ctx, xc, xq, cot_c, cot_q, w_output, w_inner, w_outer, after, hidden_bias, gain, shift)


def rows_backward(half, seqs, slots, outer, slope, unit, scale, hidden, ctx, w_output, w_inner, w_outer, gain):
    total, width = outer.shape
    rows = total // seqs
    ff = w_inner.shape[1]
    tiles = 3
    wide = (ff + width) // 2

    def block(n):
        return pl.BlockSpec((rows, n), lambda s, half: (jnp.minimum(s, seqs - 1), 0))

    def by_seq(n):
        return pl.BlockSpec((1, n, width), lambda s, half: (jnp.minimum(s, seqs - 1), 0, 0))

    def grad_block(start):
        return pl.BlockSpec(
            (width, wide // tiles), lambda s, half: (0, jnp.clip(s - start, 0, tiles - 1))
        )

    hbm = pl.BlockSpec(memory_space=pl.ANY)
    return pl.pallas_call(
        rows_backward_kernel,
        grid_spec=pltpu.PrefetchScalarGridSpec(
            num_scalar_prefetch=1,
            grid=(seqs + 2 * tiles,),
            in_specs=[
                block(width), block(ff), block(width), block(TILE),
                full_spec((total, width)), full_spec((total, width)),
                hbm, hbm, hbm, full_spec((2, width)),
            ],
            out_specs=[
                by_seq(rows - slots), by_seq(slots), by_seq(rows),
                full_spec((3, width)), full_spec((1, ff)),
                grad_block(seqs), grad_block(seqs + tiles),
            ],
            scratch_shapes=weight_scratch(width, ff) + [
                pltpu.VMEM((rows, width), F32),
                pltpu.VMEM((total, ff), BF16),
                pltpu.VMEM((total, width), BF16),
                pltpu.VMEM((width, total), BF16),
                pltpu.VMEM((width, total), BF16),
                pltpu.VMEM((3, 8, width), F32),
                pltpu.VMEM((8, ff), F32),
            ],
        ),
        out_shape=[
            jax.ShapeDtypeStruct((seqs, rows - slots, width), F32),
            jax.ShapeDtypeStruct((seqs, slots, width), F32),
            jax.ShapeDtypeStruct((seqs, rows, width), BF16),
            jax.ShapeDtypeStruct((3, width), F32),
            jax.ShapeDtypeStruct((1, ff), F32),
            jax.ShapeDtypeStruct((width, wide), BF16),
            jax.ShapeDtypeStruct((width, wide), BF16),
        ],
        compiler_params=params(),
        name="rows_backward",
    )(half, outer, slope, unit, scale, hidden, ctx, w_output, w_inner, w_outer, gain)


def grad_before_kernel(xc, xq, dq, dk, dv, *rest):
    out = rest[-1]
    length = xc.shape[1]
    wide = dq.shape[2]
    q_sum = k_sum = v_sum = None
    for s in range(xc.shape[0]):
        turned = jnp.concatenate([xc[s], xq[s]], axis=0).T
        q_sum = plus(q_sum, nn(turned, dq[s]))
        k_sum = plus(k_sum, nn(turned[:, :length], dk[s]))
        v_sum = plus(v_sum, nn(turned[:, :length], dv[s]))
    for n, total in enumerate((q_sum, k_sum, v_sum)):
        cols = slice(n * wide, (n + 1) * wide)
        if len(rest) == 3:
            total = total + rest[1][:, cols].astype(F32)
        out[:, cols] = total.astype(BF16)
    if len(rest) == 3:
        out[:, 3 * wide :] = rest[0][...].T.astype(BF16)


def grad_before(xc, xq, dq, dk, dv, vectors=None, got=None):
    seqs, length, width = xc.shape
    slots = xq.shape[1]
    wide = dq.shape[2]
    part = width // 2
    total = 3 * wide
    extra, extra_specs = [], []
    if vectors is not None:
        total += vectors.shape[0]
        extra = [vectors, got]
        extra_specs = [
            pl.BlockSpec((vectors.shape[0], part), lambda i: (0, i)),
            pl.BlockSpec((part, 3 * wide), lambda i: (i, 0)),
        ]
    return pl.pallas_call(
        grad_before_kernel,
        grid=(2,),
        in_specs=[
            pl.BlockSpec((seqs, length, part), lambda i: (0, 0, i)),
            pl.BlockSpec((seqs, slots, part), lambda i: (0, 0, i)),
            full_spec(dq.shape), full_spec(dk.shape), full_spec(dv.shape),
        ] + extra_specs,
        out_specs=pl.BlockSpec((part, total), lambda i: (i, 0)),
        out_shape=jax.ShapeDtypeStruct((width, total), BF16),
        compiler_params=params(),
        name="grad_before",
    )(xc, xq, dq, dk, dv, *extra)


def content_grad_kernel(
    half, first, dq_o, dk_o, dv_o, dq_m, dk_m, dv_m, wq_o, wk_o, wv_o, wq_m, wk_m, wv_m, out,
):
    length = dk_o.shape[1]
    left = [dq_o[0, :length], dk_o[0], dv_o[0], dq_m[0, :length], dk_m[0], dv_m[0]]
    right = [wq_o[...], wk_o[...], wv_o[...], wq_m[...], wk_m[...], wv_m[...]]
    out[0] = first[0] + nt(jnp.concatenate(left, axis=1), jnp.concatenate(right, axis=1))


def slot_grad_kernel(half, first, dq_o, dq_m, wq, out):
    seqs, rows, part = dq_o.shape
    slots = out.shape[1]
    length = rows - slots
    first_half = half[0] == 0
    a, b = wq[:, :part], wq[:, part:]
    w_m, w_o = jnp.where(first_half, a, b), jnp.where(first_half, b, a)
    for s in range(seqs):
        grad = nt(dq_o[s, length:], w_o) + nt(dq_m[s, length:], w_m)
        out[s] = (first[s] + grad).astype(BF16)


def slot_grad(half, first, dq_o, dq_m, wq, slots):
    vmem = pl.BlockSpec(memory_space=pltpu.VMEM)
    return pl.pallas_call(
        slot_grad_kernel,
        in_specs=[pl.BlockSpec(memory_space=pltpu.SMEM)] + [vmem] * 4,
        out_specs=vmem,
        out_shape=jax.ShapeDtypeStruct((dq_o.shape[0], slots, wq.shape[0]), BF16),
        compiler_params=params(),
        name="slot_grad",
    )(half, first, dq_o, dq_m, wq)


def content_grad(half, first, other, mine, wq, wk, wv):
    seqs, rows, part = other[0].shape
    length = other[1].shape[1]
    width = wq.shape[0]

    def by_seq(n):
        return pl.BlockSpec((1, n, part), lambda s, half: (s, 0, 0))

    grads = [by_seq(rows), by_seq(length), by_seq(length)]
    w_other = pl.BlockSpec((width, part), lambda s, half: (0, 1 - half[0]))
    w_mine = pl.BlockSpec((width, part), lambda s, half: (0, half[0]))
    return pl.pallas_call(
        content_grad_kernel,
        grid_spec=pltpu.PrefetchScalarGridSpec(
            num_scalar_prefetch=1,
            grid=(seqs,),
            in_specs=[pl.BlockSpec((1, length, width), lambda s, half: (s, 0, 0))]
            + grads * 2 + [w_other] * 3 + [w_mine] * 3,
            out_specs=pl.BlockSpec((1, length, width), lambda s, half: (s, 0, 0)),
        ),
        out_shape=jax.ShapeDtypeStruct((seqs, length, width), F32),
        compiler_params=params(),
        name="content_grad",
    )(half, first, *other, *mine, wq, wk, wv, wq, wk, wv)


def swap(value, axis, count, stride):
    return lax.ppermute(value, axis, [(i, i ^ stride) for i in range(count)])


def take(value, dim, index):
    return lax.dynamic_index_in_dim(value, index, dim, keepdims=False)


def low_sum(*terms):
    total = None
    for term in terms:
        total = plus(total, term.astype(F32))
    return total.astype(BF16)


def first_kernel(bits, *refs):
    terms, (send_a, send_b, keep_a, keep_b) = refs[:-4], refs[-4:]
    x, y = bits[0], bits[1]
    cut = send_a.shape[2]

    def total(g, row, col, rows):
        out = None
        for term in terms:
            out = plus(out, term[g, row, col, rows].astype(F32))
        return out.astype(BF16)

    for g in range(send_a.shape[0]):
        for n in range(2):
            send_a[g, n] = total(g, n, 1 - x, slice(0, cut))
            keep_a[g, n] = total(g, n, x, slice(0, cut))
            send_b[g, n] = total(g, 1 - y, n, slice(cut, 2 * cut))
            keep_b[g, n] = total(g, y, n, slice(cut, 2 * cut))


def second_kernel(bits, keep_a, keep_b, got_a, got_b, send_a, send_b, left_a, left_b):
    x, y = bits[0], bits[1]

    def total(keep, got, g, n):
        return (keep[g, n].astype(F32) + got[g, n].astype(F32)).astype(BF16)

    for g in range(send_a.shape[0]):
        send_a[g] = total(keep_a, got_a, g, 1 - y)
        left_a[g] = total(keep_a, got_a, g, y)
        send_b[g] = total(keep_b, got_b, g, 1 - x)
        left_b[g] = total(keep_b, got_b, g, x)


def third_kernel(bits, left_a, left_b, got_a, got_b, out):
    cut = left_a.shape[1]
    out[:, :cut] = (left_a[...].astype(F32) + got_a[...].astype(F32)).astype(BF16)
    out[:, cut:] = (left_b[...].astype(F32) + got_b[...].astype(F32)).astype(BF16)


def part_sum_kernel(parts, out):
    total = parts[0].astype(F32)
    for n in range(1, parts.shape[0]):
        total = total + parts[n].astype(F32)
    out[...] = total.astype(BF16)


def staged(kernel, bits, arrays, shapes, name):
    vmem = pl.BlockSpec(memory_space=pltpu.VMEM)
    return pl.pallas_call(
        kernel,
        in_specs=[pl.BlockSpec(memory_space=pltpu.SMEM)] + [vmem] * len(arrays),
        out_specs=[vmem] * len(shapes),
        out_shape=[jax.ShapeDtypeStruct(shape, BF16) for shape in shapes],
        compiler_params=params(),
        name=name,
    )(bits, *arrays)


class Reduction:
    def __init__(self, tok):
        self.tok = tok
        x = lax.axis_index("qry") // 2
        y = lax.axis_index("tok") % 2
        self.x = x
        self.bits = jnp.stack([x, y]).astype(jnp.int32)

    def first_sends(self, *terms):
        rows, cols = terms[0].shape
        deep = rows // self.tok // 2
        shape = (self.tok // 2, 2, 2, deep, cols)
        outs = [(self.tok // 2, 2, deep // 2, cols)] * 4
        *sends, self.keep_a, self.keep_b = staged(
            first_kernel, self.bits, [t.reshape(shape) for t in terms], outs, "first_sums"
        )
        return sends

    def first_moves(self, sends):
        return [swap(sends[0], "qry", 4, 2), swap(sends[1], "tok", self.tok, 1)]

    def second_sends(self, got):
        shape = self.keep_a.shape
        outs = [(shape[0],) + shape[2:]] * 4
        *sends, self.left_a, self.left_b = staged(
            second_kernel, self.bits, [self.keep_a, self.keep_b, *got], outs, "second_sums"
        )
        return sends

    def second_moves(self, sends):
        return [swap(sends[0], "tok", self.tok, 1), swap(sends[1], "qry", 4, 2)]

    def third_sends(self, got):
        rest, deep, cols = self.left_a.shape
        (out,) = staged(
            third_kernel, self.bits, [self.left_a, self.left_b, *got], [(rest, 2 * deep, cols)], "third_sums"
        )
        return out

    def third_moves(self, send):
        if self.tok == 2:
            return send
        groups = [list(range(bit, self.tok, 2)) for bit in range(2)]
        return lax.all_to_all(send, "tok", 0, 0, tiled=True, axis_index_groups=groups)

    def far_sends(self, got):
        self.own = pl.pallas_call(
            part_sum_kernel,
            out_shape=jax.ShapeDtypeStruct(got.shape[1:], BF16),
            name="part_sums",
        )(got)
        return self.own

    def far_moves(self, send):
        return swap(send, "qry", 4, 2)

    def near_sends(self, got):
        low = self.x == 0
        self.own = jnp.concatenate(
            [jnp.where(low, self.own, got), jnp.where(low, got, self.own)], axis=0
        )
        return self.own

    def near_moves(self, send):
        return swap(send, "qry", 4, 1)


def beside(transfers, compute=None, arrays=()):
    moves = [move for move, _ in transfers]
    sends = [send for _, send in transfers]
    sends, arrays = lax.optimization_barrier((sends, tuple(arrays)))
    got = [move(send) for move, send in zip(moves, sends)]
    out = compute(*arrays) if compute is not None else ()
    return lax.optimization_barrier((got, out))


def in_core_order(first, own, got):
    a, b = own[...].astype(F32), got[...].astype(F32)
    return jnp.where(first, a, b), jnp.where(first, b, a)


def place_outer_kernel(core, own, got, outer):
    part = own.shape[1]
    first, second = in_core_order(core[0] == 0, own, got)
    outer[:, :part] = first
    outer[:, part:] = second


def place_inner_kernel(core, own, got, inner, output):
    tiles = 3
    wide, narrow = inner.shape[1] // 2 // tiles, output.shape[1] // 2 // tiles
    for n, half in enumerate(in_core_order(core[0] == 0, own, got)):
        for t in range(tiles):
            at = t * (wide + narrow)
            to = (n * tiles + t) * wide
            inner[:, to : to + wide] = half[:, at : at + wide]
            to = (n * tiles + t) * narrow
            output[:, to : to + narrow] = half[:, at + wide : at + wide + narrow]


def place_before_kernel(core, own, got, query, key, value, vectors):
    part = query.shape[1] // 2
    first, second = in_core_order(core[0] == 0, own, got)
    for n, ref in enumerate((query, key, value)):
        ref[:, :part] = first[:, n * part : (n + 1) * part]
        ref[:, part:] = second[:, n * part : (n + 1) * part]
    vectors[...] = (first[:, 3 * part :] + second[:, 3 * part :]).T


def place_sums(kernel, core, own, got, shapes):
    vmem = pl.BlockSpec(memory_space=pltpu.VMEM)
    return pl.pallas_call(
        kernel,
        in_specs=[pl.BlockSpec(memory_space=pltpu.SMEM), vmem, vmem],
        out_specs=[vmem] * len(shapes),
        out_shape=[jax.ShapeDtypeStruct(shape, F32) for shape in shapes],
        name="place_sums",
    )(core, own, got)


def on_device(
    content_in, query_in, seq_lengths, perm_ranks, w_query, w_key, w_value, w_output, w_inner,
    w_outer, b_before, b_after, b_hidden, norm_gain, norm_shift, rel_table, cot_content, cot_query,
    tok,
):
    seqs, length, width = content_in.shape
    group = lax.axis_index("qry")
    core = group % 2
    other = jnp.reshape(1 - core, (1,)).astype(jnp.int32)
    mine = jnp.reshape(core, (1,)).astype(jnp.int32)
    lengths = lax.dynamic_slice_in_dim(seq_lengths, group * seqs, seqs)
    ranks = lax.dynamic_slice_in_dim(perm_ranks, group * seqs, seqs, 0)

    both = jnp.concatenate([query_in, cot_query], axis=2)
    both = lax.all_to_all(both, "qry", 0, 1, tiled=True)
    xq, cot_q = both[:, :, :width], both[:, :, width:]
    slots = xq.shape[1]
    floor = lengths[:, None] - PRED
    thr_c = jnp.maximum(floor, jnp.minimum(ranks, lengths[:, None]))[:, :, None]
    thr_q = (floor + jnp.arange(slots, dtype=jnp.int32)[None, :])[:, :, None]
    rank_row = ranks[:, None, :]
    place = jnp.arange(512, dtype=jnp.int32)
    one_hot = bucket_of(jnp.where(place < 384, place, place - 512) - 128)
    one_hot = (one_hot[None, :] == jnp.arange(BUCKETS, dtype=jnp.int32)[:, None]).astype(BF16)
    offsets = jnp.dot(rel_table, one_hot, preferred_element_type=F32)[:, None, :]

    ctx, e, rr, q, k, v = attention_forward(
        content_in, xq, w_query, w_key, w_value, b_before, rank_row, thr_c, thr_q, offsets,
        rel_table.astype(F32),
    )
    (out_c, out_q, slope, hidden, unit, scale, outer, sums_f, o_other, o_mine) = rows_forward(
        mine, ctx, content_in, xq, cot_content, cot_q, w_output, w_inner, w_outer, b_after,
        b_hidden[None], norm_gain, norm_shift,
    )
    ff = slope.shape[1]
    share = width // tok
    part = width // 2

    red_i = Reduction(tok)
    red_b = Reduction(tok)

    def to_slots(a):
        return lax.all_to_all(a, "qry", 1, 0, tiled=True)

    def slot_blocks(a):
        a = a.reshape(seqs, 4, slots // 4, width)
        return [take(a, 1, group ^ n) for n in range(4)]

    def slot_moves(blocks):
        return [swap(blocks[n], "qry", 4, n) for n in range(1, 4)]

    def slot_rows(own, got):
        every = jnp.stack([own, *got])
        return jnp.concatenate([take(every, 0, group ^ n) for n in range(4)], axis=0)

    def swap_core(a):
        return swap(a, "qry", 4, 1)

    def over_tok(a):
        return lax.psum_scatter(a, "tok", scatter_dimension=0, tiled=True)

    (got_o,), (first_c, first_q, d_ctx, sums_b, inner_sums, i_other, i_mine) = beside(
        [(swap_core, o_other)],
        lambda a: rows_backward(
            mine, seqs, slots, a, slope, unit, scale, hidden, ctx.reshape(-1, width), w_output,
            w_inner, w_outer, norm_gain,
        ),
        (outer,),
    )
    o_sum = over_tok(o_mine.astype(F32) + got_o.astype(F32))
    (got_i,), back_other = beside(
        [(swap_core, i_other)],
        lambda a: attention_backward(other, q, k, v, e, ctx, a, rr, rank_row, thr_q),
        (d_ctx,),
    )

    def grad_and_backward(dq, dk, dv, cotangent):
        b_other = grad_before(content_in, xq, dq, dk, dv)
        b_other, cotangent = lax.optimization_barrier((b_other, cotangent))
        got = swap_core(b_other)
        return got, attention_backward(mine, q, k, v, e, ctx, cotangent, rr, rank_row, thr_q)

    (got_i, out_q), (got_b, back_mine) = beside(
        [(red_i.first_moves, red_i.first_sends(i_mine, got_i)), (to_slots, out_q)],
        grad_and_backward,
        (*back_other[:3], d_ctx),
    )

    def in_order(a, b, axis):
        return jnp.where(
            core == 0, jnp.concatenate([b, a], axis=axis), jnp.concatenate([a, b], axis=axis)
        )

    table = in_order(back_other[4], back_mine[4], 0)[:, :, :BUCKETS]
    table = jnp.tile(table.reshape(-1, share), (1, tok))
    wide_sums = jnp.swapaxes(inner_sums.reshape(tok, ff // width, share), 0, 1)
    vectors = jnp.concatenate(
        [
            in_order(back_other[3], back_mine[3], 1),
            sums_b[2:], sums_f[2:], sums_b[:1], sums_f[:1], sums_b[1:2], sums_f[1:2],
            wide_sums.reshape(-1, width), table,
        ]
    )
    vectors = jnp.pad(vectors, ((0, TILE - vectors.shape[0]), (0, 0)))
    (got_i,), b_mine = beside(
        [(red_i.second_moves, red_i.second_sends(got_i))],
        lambda a: grad_before(content_in, xq, a, *back_mine[1:3], vectors, got_b),
        (back_mine[0],),
    )
    d_query = slot_grad(mine, first_q, back_other[0], back_mine[0], w_query, slots)
    d_query = slot_blocks(d_query)
    send_i = red_i.third_sends(got_i)
    send_b = red_b.first_sends(b_mine)
    send_i, send_b, d_query, first_c = lax.optimization_barrier(
        (send_i, send_b, d_query, first_c)
    )
    got_i = red_i.third_moves(send_i)
    got_b = red_b.first_moves(send_b)
    got_q = slot_moves(d_query)
    d_content = content_grad(
        mine, first_c, back_other[:3], back_mine[:3], w_query, w_key, w_value
    )
    got_b, d_content = lax.optimization_barrier((got_b, d_content))
    (got_b,), d_query = beside(
        [(red_b.second_moves, red_b.second_sends(got_b))],
        lambda *a: slot_rows(a[0], a[1:]).astype(F32),
        (d_query[0], *got_q),
    )

    def swap_x(a):
        return swap(a, "qry", 4, 2)

    (got_b, got_i, got_o), _ = beside(
        [
            (red_b.third_moves, red_b.third_sends(got_b)),
            (red_i.far_moves, red_i.far_sends(got_i)),
            (swap_x, o_sum.astype(BF16)),
        ],
    )
    o_sum = low_sum(o_sum, got_o)
    (got_b, got_o, got_i), _ = beside(
        [
            (red_b.far_moves, red_b.far_sends(got_b)),
            (swap_core, o_sum),
            (red_i.near_moves, red_i.near_sends(got_i)),
        ]
    )
    (got_b,), ((g_outer,), (g_inner, g_output)) = beside(
        [(red_b.near_moves, red_b.near_sends(got_b))],
        lambda a, b: (
            place_sums(place_outer_kernel, mine, o_sum, a, [(ff // tok, width)]),
            place_sums(place_inner_kernel, mine, red_i.own, b, [(share, ff), (share, width)]),
        ),
        (got_o, got_i),
    )
    g_query, g_key, g_value, vectors = place_sums(
        place_before_kernel, mine, red_b.own, got_b, [(share, width)] * 3 + [(TILE, share)]
    )
    g_hidden = vectors[8 : 8 + ff // width].reshape(-1)
    g_table = vectors[8 + ff // width :].reshape(-1)[: HEADS * BUCKETS].reshape(HEADS, BUCKETS)
    return (
        out_c, out_q, d_content, d_query, g_query, g_key, g_value, g_output, g_inner, g_outer,
        vectors[0:2], vectors[2:4], g_hidden, vectors[4:6], vectors[6:8], g_table,
    )


def solution(mesh):
    rows = P(("tok", "qry"), None, None)
    slots = P("tok", "qry", None)
    return jax.shard_map(
        functools.partial(on_device, tok=mesh.shape["tok"]),
        mesh=mesh,
        in_specs=(rows, slots, P("tok"), P("tok", None)) + (P(),) * 12 + (rows, slots),
        out_specs=(rows, slots, rows, slots)
        + (P("tok", None),) * 6
        + (P(None, "tok"), P(None, "tok"), P("tok"), P(None, "tok"), P(None, "tok"), P()),
        check_vma=False,
    )
```

time: 1370 us -> 323 us (0.24)
  waiting for transfers between devices: 745 us -> 34.1 us
  matrix products: 269 us -> 0.13 us
  Pallas kernels: 0 us -> 204 us
  local copies, waits for them, and re-layouts: 190 us -> 21.7 us
  blocking collectives: 80.5 us -> 0 us
  other arithmetic: 55.1 us -> 11.4 us
  starting transfers between devices: 0.79 us -> 31.8 us
    reduce_scatter x5 -> x1, waiting for transfers between devices: 398 us -> 0.01 us  [over_tok(): return lax.psum_scatter(a, 'tok', scatter_dimension=0, tiled=True)]
    unnamed x22 -> x1, waiting for transfers between devices: 304 us -> 0.02 us
    dot_general x55 -> x1, matrix products: 269 us -> 0.13 us  [on_device(): jnp.dot(rel_table, one_hot, preferred_element_type=F32)[:, None, :]]
    pallas_call x0 -> x20, Pallas kernels: none -> 204 us  [the longest x1 47.8 us: rows_forward(): pl.pallas_call(rows_forward_kernel, grid_spec=pltpu.PrefetchScalarGridSpe...]
    convert_element_type x12 -> x0, local copies, waits for them, and re-layouts: 52.3 us -> none  [the longest x2 29 us: attend_backward(): score_gradient = (attn_probs * centred).astype(jnp.bfloat16)]
    psum x1 -> x0, waiting for transfers between devices: 43 us -> none  [on_device(): lax.psum(all_parts[0].astype(jnp.bfloat16), 'qry').astype(jnp.float32)]
    psum x2 -> x0, blocking collectives: 42.6 us -> none  [the longest x1 36.9 us: on_device(): g_table = lax.psum(table_local, ('tok', 'qry'))]
    while x56 -> x0, local copies, waits for them, and re-layouts: 38.2 us -> none  [the longest x4 25.9 us: per_sequence(): result = lax.map(lambda pieces: function(*pieces), widened)]
  transfers between devices with their start and end apart: 15 -> 25, of which waited for: 9 -> 11; matrix products, arithmetic and copies ran while one was open for 31% -> 4% of each run, Pallas kernels for 0% -> 39%
where the time goes in v1:
time: 323 us; the launch traced here: 318 us
  Pallas kernels  204 us (63%)
  waiting for transfers between devices  34.1 us (11%)
  starting transfers between devices  31.8 us (10%)
  local copies, waits for them, and re-layouts  21.7 us (7%)
  between operations  14.7 us (5%)
  other arithmetic  11.4 us (4%)
    pallas_call x1, Pallas kernels, rows_forward(): pl.pallas_call(rows_forward_kernel, grid_spec=pltpu.PrefetchScalarGridSpe...  47.8 us
    pallas_call x1, Pallas kernels, rows_backward(): pl.pallas_call(rows_backward_kernel, grid_spec=pltpu.PrefetchScalarGridSp...  42.4 us
    pallas_call x2, Pallas kernels, attention_backward(): pl.pallas_call(attention_backward_kernel, grid_spec=pltpu.PrefetchScalarG...  31.3 us
    pallas_call x1, Pallas kernels, attention_forward(): pl.pallas_call(attention_forward_kernel, grid=(seqs, PAIRS), in_specs=[by...  28.2 us
    ppermute x20, waiting for transfers between devices, swap(): return lax.ppermute(value, axis, [(i, i ^ stride) for i in range(count)])  23.7 us
    pallas_call x6, Pallas kernels, staged(): pl.pallas_call(kernel, in_specs=[pl.BlockSpec(memory_space=pltpu.SMEM)] +...  19 us
    ppermute x20, starting transfers between devices, swap(): return lax.ppermute(value, axis, [(i, i ^ stride) for i in range(count)])  14.2 us
    pallas_call x2, Pallas kernels, grad_before(): pl.pallas_call(grad_before_kernel, grid=(2,), in_specs=[pl.BlockSpec((seq...  12.8 us
  transfers between devices with their start and end apart: 25, of which 11 were waited for; matrix products, arithmetic and copies ran while one was open for 4% of the time, Pallas kernels for 39%

profile of v1, /device:TPU:0, one launch (start us, length us, event | category | flops | bytes accessed | tf_op | source)
XLA Modules:
  0.0 318.1 jit_solution(11509767637649143849)
XLA Ops:
  7.2 1.0 copy.53
  8.2 1.0 copy.52
  9.2 0.9 pad_maximum_fusion
  10.1 4.2 %all-to-all-start = ((bf16[8,20,1536]{2,1,0:T(8,128)(2,1)}), bf16[8,20,1536]{2,1,0:T(8,128)(2,1)S(1)}, u32[]{:S(2)}, u32[]{:S(2)}) async-start(bf16[8,20,1536]{2,1,0:T(8,128)(2,1)} %pad_maximum_fusion), calls=%async_computation | async-start | bytes 1179648 | tf_op jit(solution)/shard_map/all_to_all | solution.py:1074
  14.4 0.8 maximum_bitcast_fusion
  15.8 1.0 copy.56.thr_c
  18.8 0.7 iota_add_fusion.thr_q
  19.5 4.4 %all-to-all-done = bf16[8,20,1536]{2,1,0:T(8,128)(2,1)S(1)} async-done(((bf16[8,20,1536]{2,1,0:T(8,128)(2,1)}), bf16[8,20,1536]{2,1,0:T(8,128)(2,1)S(1)}, u32[]{:S(2)}, u32[]{:S(2)}) %all-to-all-start) | async-done | bytes 491552 | tf_op jit(solution)/shard_map/all_to_all | solution.py:1074
  24.6 0.7 copy.62.xq
  25.3 0.7 copy.63.cot_q
  26.0 28.2 %attention_forward.1 = (bf16[2,592,768]{2,1,0:T(8,128)(2,1)}, bf16[2,12,592,512]{3,2,1,0:T(8,128)(2,1)}, f32[2,592,768]{2,1,0:T(8,128)}, bf16[2,592,768]{2,1,0:T...) custom-call(bf16[2,512,768]{2,1,0:T(8,128)(2,1)} %xc.7, bf16[2,80,768]{2,1,0:T(8,128)(2,1)} %copy.62.xq, ...), custom_call_target="tpu_custom_call" | custom-call | tf_op jit(solution)/shard_map/attention_forward/pallas_call | solution.py:197
  54.2 47.8 %rows_forward.1 = (bf16[2,512,768]{2,1,0:T(8,128)(2,1)}, bf16[2,80,768]{2,1,0:T(8,128)(2,1)}, bf16[1184,3072]{1,0:T(8,128)(2,1)}, bf16[1184,768]{1,0:T(8,128)(2,...) custom-call(s32[1]{0:T(128)} %bitcast.half.first.core, ...), custom_call_target="tpu_custom_call" | custom-call | tf_op jit(solution)/shard_map/rows_forward/pallas_call | solution.py:664
  102.1 42.4 %rows_backward.1 = (f32[2,512,768]{2,1,0:T(8,128)}, f32[2,80,768]{2,1,0:T(8,128)}, bf16[2,592,768]{2,1,0:T(8,128)(2,1)}, f32[3,768]{1,0:T(4,128)}, f32[1,3072]{1...) custom-call(s32[1]{0:T(128)} %bitcast.half.first.core, bf16[1184,768]{1,0:T(8,128)(2,1)} %get-tuple-element.157.outer, ...), custom_call_target="tpu_custom_call" | custom-call | tf_op jit(solution)/shard_map/rows_backward/pallas_call | solution.py:722
  144.6 4.2 %convert_add_fusion = f32[3072,384]{1,0:T(8,128)} fusion(bf16[3072,384]{1,0:T(8,128)(2,1)} %collective-permute-done, bf16[3072,384]{1,0:T(8,128)(2,1)S(1)} %copy-done.3), kind=kLoop, calls=%fused_computation | loop fusion | flops 3538944 | bytes 9437184 | tf_op jit(solution)/shard_map/add | solution.py:1129
  149.9 15.8 %attention_backward.2 = (bf16[2,592,384]{2,1,0:T(8,128)(2,1)}, bf16[2,512,384]{2,1,0:T(8,128)(2,1)}, bf16[2,512,384]{2,1,0:T(8,128)(2,1)}, f32[2,384]{1,0:T(2,128)}, f32[3,2,128]{2,1,0:T(2,128)}) custom-call(s32[1]{0:T(128)} %bitcast.11.first, bf16[2,592,768]{2,1,0:T(8,128)(2,1)} %get-tuple-element.173.q, bf16[2,512,768]{2,1,0:T(8,128)(2,1)} %get-tuple-element.174.k, ...), custom_call_target="tpu_custom_call" | custom-call | tf_op jit(solution)/shard_map/attention_backward/pallas_call | solution.py:395
  165.7 1.6 copy-done.1
  167.3 4.8 %first_sums.2 = (bf16[4,2,24,1920]{3,2,1,0:T(8,128)(2,1)}, bf16[4,2,24,1920]{3,2,1,0:T(8,128)(2,1)}, bf16[4,2,24,1920]{3,2,1,0:T(8,128)(2,1)}, bf16[4,2,24,1920]{3,2,1,0:T(8,128)(2,1)}) custom-call(s32[2]{0:T(128)} %pad_add_fusion.bits, bf16[4,2,2,48,1920]{4,3,2,1,0:T(8,128)(2,1)} %bitcast.48, bf16[4,2,2,48,1920]{4,3,2,1,0:T(8,128)(2,1)} %bitcast.49), custom_call_target="tpu_custom_call" | custom-call | tf_op jit(solution)/shard_map/first_sums/pallas_call | solution.py:930
  172.1 6.1 %grad_before.2 = bf16[768,1152]{1,0:T(8,128)(2,1)} custom-call(bf16[2,512,768]{2,1,0:T(8,128)(2,1)} %xc.7, bf16[2,80,768]{2,1,0:T(8,128)(2,1)} %copy.62.xq, bf16[2,592,384]{2,1,0:T(8,128)(2,1)} %get-tuple-element.194.dq.dq_o, bf16[2,512,384]{2,1,0:T(8,128)(2,1)} %get-tuple-element.195.dk.dk_o, bf16[2,512,384]{2,1,0:T(8,128)(2,1)} %get-tuple-element.196.dv.dv_o), custom_call_target="tpu_custom_call" | custom-call | tf_op jit(solution)/shard_map/grad_before/pallas_call | solution.py:794
  178.6 2.2 collective-permute-start.3
  180.8 0.9 copy.58
  181.7 3.4 %all-to-all-start.1 = ((bf16[2,80,768]{2,0,1:T(2,128)(2,1)}), bf16[2,80,768]{2,0,1:T(2,128)(2,1)S(1)}, u32[]{:S(2)}, u32[]{:S(2)}) async-start(bf16[2,80,768]{2,0,1:T(2,128)(2,1)} %copy.58), calls=%async_computation.1 | async-start | bytes 491520 | tf_op jit(solution)/shard_map/all_to_all | solution.py:1102
  185.1 15.6 %attention_backward.3 = (bf16[2,592,384]{2,1,0:T(8,128)(2,1)}, bf16[2,512,384]{2,1,0:T(8,128)(2,1)}, bf16[2,512,384]{2,1,0:T(8,128)(2,1)}, f32[2,384]{1,0:T(2,128)}, f32[3,2,128]{2,1,0:T(2,128)}) custom-call(s32[1]{0:T(128)} %bitcast.half.first.core, bf16[2,592,768]{2,1,0:T(8,128)(2,1)} %get-tuple-element.173.q, bf16[2,512,768]{2,1,0:T(8,128)(2,1)} %get-tuple-element.174.k, ...), custom_call_target="tpu_custom_call" | custom-call | tf_op jit(solution)/shard_map/attention_backward/pallas_call | solution.py:395
  200.9 0.8 all_to_all.39
  201.7 1.4 collective-permute-done.3.got_b
  203.1 3.7 %second_sums.2 = (bf16[4,24,1920]{2,1,0:T(8,128)(2,1)}, bf16[4,24,1920]{2,1,0:T(8,128)(2,1)}, bf16[4,24,1920]{2,1,0:T(8,128)(2,1)}, bf16[4,24,1920]{2,1,0:T(8,128)(2,1)}) custom-call(s32[2]{0:T(128)} %pad_add_fusion.bits, bf16[4,2,24,1920]{3,2,1,0:T(8,128)(2,1)} %get-tuple-element.206.keep_a, bf16[4,2,24,1920]{3,2,1,0:T(8,128)(2,1)} %get-tuple-element.207.keep_b, ...), custom_call_target="tpu_custom_call" | custom-call | tf_op jit(solution)/shard_map/second_sums/pallas_call | solution.py:930
  206.8 0.8 collective-permute-start.5
  207.6 1.6 collective-permute-start.6
  209.7 0.7 reduce.3
  210.8 3.6 %slot_grad.1 = bf16[2,80,768]{2,1,0:T(8,128)(2,1)} custom-call(s32[1]{0:T(128)} %bitcast.half.first.core, f32[2,80,768]{2,1,0:T(8,128)} %get-tuple-element.233.first, bf16[2,592,384]{2,1,0:T(8,128)(2,1)} %get-tuple-element.194.dq.dq_o, bf16[2,592,384]{2,1,0:T(8,128)(2,1)} %get-tuple-element.217.dq.dq_m, bf16[768,768]{1,0:T(8,128)(2,1)} %wq_m.1), custom_call_target="tpu_custom_call" | custom-call | tf_op jit(solution)/shard_map/slot_grad/pallas_call | solution.py:832
  214.4 1.1 copy.61
  215.6 0.8 pad.4.rest_0_
  216.4 6.7 %grad_before.3 = bf16[768,1280]{1,0:T(8,128)(2,1)} custom-call(bf16[2,512,768]{2,1,0:T(8,128)(2,1)} %xc.7, bf16[2,80,768]{2,1,0:T(8,128)(2,1)} %copy.62.xq, bf16[2,592,384]{2,1,0:T(8,128)(2,1)} %get-tuple-element.217.dq.dq_m, bf16[2,512,384]{2,1,0:T(8,128)(2,1)} %get-tuple-element.218.dk.dk_m, bf16[2,512,384]{2,1,0:T(8,128)(2,1)} %get-tuple-element.219.dv.dv_m, ...), custom_call_target="tpu_custom_call" | custom-call | tf_op jit(solution)/shard_map/grad_before/pallas_call | solution.py:794
  223.4 3.3 %first_sums.3 = (bf16[4,2,24,1280]{3,2,1,0:T(8,128)(2,1)}, bf16[4,2,24,1280]{3,2,1,0:T(8,128)(2,1)}, bf16[4,2,24,1280]{3,2,1,0:T(8,128)(2,1)}, bf16[4,2,24,1280]{3,2,1,0:T(8,128)(2,1)}) custom-call(s32[2]{0:T(128)} %pad_add_fusion.bits, bf16[4,2,2,48,1280]{4,3,2,1,0:T(8,128)(2,1)} %bitcast.47), custom_call_target="tpu_custom_call" | custom-call | tf_op jit(solution)/shard_map/first_sums/pallas_call | solution.py:930
  226.6 2.4 third_sums.2
  229.1 6.4 %all-to-all-start.2 = ((bf16[4,48,1920]{2,1,0:T(8,128)(2,1)}), bf16[4,48,1920]{2,1,0:T(8,128)(2,1)S(1)}, u32[]{:S(2)}, u32[]{:S(2)}) async-start(bf16[4,48,1920]{2,1,0:T(8,128)(2,1)} %third_sums.2), calls=%async_computation.2 | async-start | bytes 1474560 | tf_op jit(solution)/shard_map/all_to_all | solution.py:983
  235.6 0.7 collective-permute-start.8
  236.4 1.3 collective-permute-start.10
  238.3 8.8 %content_grad.1 = f32[2,512,768]{2,1,0:T(8,128)} custom-call(s32[1]{0:T(128)} %bitcast.half.first.core, f32[2,512,768]{2,1,0:T(8,128)} %get-tuple-element.237.first, bf16[2,592,384]{2,1,0:T(8,128)(2,1)} %get-tuple-element.194.dq.dq_o, bf16[2,512,384]{2,1,0:T(8,128)(2,1)} %get-tuple-element.195.dk.dk_o, bf16[2,512,384]{2,1,0:T(8,128)(2,1)} %get-tuple-element.196.dv.dv_o, ...), custom_call_target="tpu_custom_call" | custom-call | tf_op jit(solution)/shard_map/content_grad/pallas_call | solution.py:853
  247.3 4.8 %collective-permute-done.8.got_b = bf16[4,2,24,1280]{3,2,1,0:T(8,128)(2,1)S(1)} collective-permute-done((bf16[4,2,24,1280]{3,2,1,0:T(8,128)(2,1)S(1)}, bf16[4,2,24,1280]{3,2,1,0:T(8,128)(2,1)S(1)}, u32[]{:S(2)}, u32[]{:S(2)}) %collective-permute-start.8) | collective-permute-done | bytes 491552 | tf_op jit(solution)/shard_map/ppermute | solution.py:869
  252.0 0.8 copy-done.13
  252.8 2.6 second_sums.3
  255.8 1.7 collective-permute-start.13
  258.1 1.1 maximum_convert_fusion
  259.2 3.4 %collective-permute-done.12.got_a = bf16[4,24,1280]{2,1,0:T(8,128)(2,1)S(1)} collective-permute-done((bf16[4,24,1280]{2,1,0:T(8,128)(2,1)}, bf16[4,24,1280]{2,1,0:T(8,128)(2,1)S(1)}, u32[]{:S(2)}, u32[]{:S(2)}) %collective-permute-start.12) | collective-permute-done | bytes 245792 | tf_op jit(solution)/shard_map/ppermute | solution.py:869
  263.4 2.2 third_sums.3
  265.6 4.8 %all-to-all-done.2.parts = bf16[4,48,1920]{2,1,0:T(8,128)(2,1)S(1)} async-done(((bf16[4,48,1920]{2,1,0:T(8,128)(2,1)}), bf16[4,48,1920]{2,1,0:T(8,128)(2,1)S(1)}, u32[]{:S(2)}, u32[]{:S(2)}) %all-to-all-start.2) | async-done | bytes 737312 | tf_op jit(solution)/shard_map/all_to_all | solution.py:983
  270.4 0.9 copy-done
  271.3 1.9 part_sums.2
  273.2 1.2 convert_element_type.85
  274.4 3.5 %all-to-all-start.3 = ((bf16[4,48,1280]{2,1,0:T(8,128)(2,1)}), bf16[4,48,1280]{2,1,0:T(8,128)(2,1)S(1)}, u32[]{:S(2)}, u32[]{:S(2)}) async-start(bf16[4,48,1280]{2,1,0:T(8,128)(2,1)} %third_sums.3), calls=%async_computation.4 | async-start | bytes 983040 | tf_op jit(solution)/shard_map/all_to_all | solution.py:983
  278.5 1.4 collective-permute-start.14
  279.9 9.7 %collective-permute-done.14 = bf16[48,1920]{1,0:T(8,128)(2,1)S(1)} collective-permute-done((bf16[48,1920]{1,0:T(8,128)(2,1)S(1)}, bf16[48,1920]{1,0:T(8,128)(2,1)S(1)}, u32[]{:S(2)}, u32[]{:S(2)}) %collective-permute-start.14) | collective-permute-done | bytes 184352 | tf_op jit(solution)/shard_map/ppermute | solution.py:869
  289.6 1.3 all-to-all-done.3.parts
  290.9 0.8 copy-done.4
  291.7 1.7 part_sums.3
  294.3 1.1 collective-permute-start.16
  295.4 4.1 %collective-permute-done.16 = bf16[48,1280]{1,0:T(8,128)(2,1)S(1)} collective-permute-done((bf16[48,1280]{1,0:T(8,128)(2,1)S(1)}, bf16[48,1280]{1,0:T(8,128)(2,1)S(1)}, u32[]{:S(2)}, u32[]{:S(2)}) %collective-permute-start.16) | collective-permute-done | bytes 122912 | tf_op jit(solution)/shard_map/ppermute | solution.py:869
  300.2 2.2 place_sums.3
  302.4 2.4 place_sums.4
  304.8 0.7 copy-done.18
  305.5 2.0 place_sums.5
  307.5 1.4 fusion.8
  309.0 0.8 fusion.7
  310.4 0.7 reshape.150
  (123 shorter events, 12.1 us)
Async XLA Ops:
  7.2 7.1 %copy-start.31 = (s32[8]{0:T(128)S(1)}, s32[8]{0:T(128)}, u32[]{:S(2)}) copy-start(s32[8]{0:T(128)} %param.20) | copy-start | bytes 100
  8.2 8.6 %copy-start.22 = (bf16[12,32]{1,0:T(8,128)(2,1)S(1)}, bf16[12,32]{1,0:T(8,128)(2,1)}, u32[]{:S(2)}) copy-start(bf16[12,32]{1,0:T(8,128)(2,1)} %param.33) | copy-start | bytes 2308
  8.2 10.0 %copy-start.26 = (bf16[3072]{0:T(1024)(128)(2,1)S(1)}, bf16[3072]{0:T(1024)(128)(2,1)}, u32[]{:S(2)}) copy-start(bf16[3072]{0:T(1024)(128)(2,1)} %param.30) | copy-start | bytes 18436
  10.1 13.8 %all-to-all-start = ((bf16[8,20,1536]{2,1,0:T(8,128)(2,1)}), bf16[8,20,1536]{2,1,0:T(8,128)(2,1)S(1)}, u32[]{:S(2)}, u32[]{:S(2)}) async-start(bf16[8,20,1536]{2,1,0:T(8,128)(2,1)} %pad_maximum_fusion), calls=%async_computation | async-start | bytes 1179648 | tf_op jit(solution)/shard_map/all_to_all | solution.py:1074
  14.3 258.9 %reduce-scatter.2.cloned.1.call-start = ((), (), s32[]{:S(2)}) async-start(), calls=%async_computation.5 | async-start | bytes 5308416 | tf_op jit(solution)/shard_map/reduce_scatter | solution.py:1119
  102.0 42.5 %collective-permute-start = (bf16[3072,384]{1,0:T(8,128)(2,1)}, bf16[3072,384]{1,0:T(8,128)(2,1)}, u32[]{:S(2)}, u32[]{:S(2)}) collective-permute-start(bf16[3072,384]{1,0:T(8,128)(2,1)} %get-tuple-element.156), channel_id=1, source_target_pairs={{0,1},{1,0},{2,3},{3,2},{4,5},{5,4},{6,7},{7,6},{8,9},{9,8},{10,11... | collective-permute-start | bytes 7077896 | tf_op jit(solution)/shard_map/ppermute | solution.py:869
  102.1 42.5 %copy-start.3 = (bf16[3072,384]{1,0:T(8,128)(2,1)S(1)}, bf16[3072,384]{1,0:T(8,128)(2,1)}, u32[]{:S(2)}) copy-start(bf16[3072,384]{1,0:T(8,128)(2,1)} %get-tuple-element.261) | copy-start | bytes 7077892
  148.8 16.9 %collective-permute-start.1 = (bf16[768,1920]{1,0:T(8,128)(2,1)}, bf16[768,1920]{1,0:T(8,128)(2,1)S(1)}, u32[]{:S(2)}, u32[]{:S(2)}) collective-permute-start(bf16[768,1920]{1,0:T(8,128)(2,1)} %get-tuple-element.172), channel_id=1, source_target_pairs={{0,1},{1,0},{2,3},{3,2},{4,5},{5,4},{6,7},{7,6},{8,9},{9,8},{10,11... | collective-permute-start | bytes 8847368 | tf_op jit(solution)/shard_map/ppermute | solution.py:869
  165.7 1.6 copy-start.1
  172.1 8.7 %copy-start.19 = (bf16[2,80,768]{2,1,0:T(8,128)(2,1)S(1)}, bf16[2,80,768]{2,1,0:T(8,128)(2,1)}, u32[]{:S(2)}) copy-start(bf16[2,80,768]{2,1,0:T(8,128)(2,1)} %get-tuple-element.193) | copy-start | bytes 737284
  178.2 24.8 %collective-permute-start.4 = (bf16[768,1152]{1,0:T(8,128)(2,1)}, bf16[768,1152]{1,0:T(8,128)(2,1)S(1)}, u32[]{:S(2)}, u32[]{:S(2)}) collective-permute-start(bf16[768,1152]{1,0:T(8,128)(2,1)} %grad_before.2), channel_id=1, source_target_pairs={{0,1},{1,0},{2,3},{3,2},{4,5},{5,4},{6,7},{7,6},{8,9},{9,8},{10,11... | collective-permute-start | bytes 5308424 | tf_op jit(solution)/shard_map/ppermute | solution.py:869
  178.2 23.5 %collective-permute-start.2 = (bf16[4,2,24,1920]{3,2,1,0:T(8,128)(2,1)}, bf16[4,2,24,1920]{3,2,1,0:T(8,128)(2,1)S(1)}, u32[]{:S(2)}, u32[]{:S(2)}) collective-permute-start(bf16[4,2,24,1920]{3,2,1,0:T(8,128)(2,1)} %get-tuple-element.191), channel_id=1, source_target_pairs={{0,2},{1,3},{2,0},{3,1},{4,6},{5,7},{6,4},{7,5},{8,10},{9,11},{10,... | collective-permute-start | bytes 2211848 | tf_op jit(solution)/shard_map/ppermute | solution.py:869
  178.6 24.5 %collective-permute-start.3 = (bf16[4,2,24,1920]{3,2,1,0:T(8,128)(2,1)}, bf16[4,2,24,1920]{3,2,1,0:T(8,128)(2,1)}, u32[]{:S(2)}, u32[]{:S(2)}) collective-permute-start(bf16[4,2,24,1920]{3,2,1,0:T(8,128)(2,1)} %get-tuple-element.192), channel_id=1, source_target_pairs={{0,4},{4,0},{8,12},{12,8},{16,20},{20,16},{24,28},{28,24},{1,5},{5... | collective-permute-start | bytes 2211848 | tf_op jit(solution)/shard_map/ppermute | solution.py:869
  181.7 19.0 %all-to-all-start.1 = ((bf16[2,80,768]{2,0,1:T(2,128)(2,1)}), bf16[2,80,768]{2,0,1:T(2,128)(2,1)S(1)}, u32[]{:S(2)}, u32[]{:S(2)}) async-start(bf16[2,80,768]{2,0,1:T(2,128)(2,1)} %copy.58), calls=%async_computation.1 | async-start | bytes 491520 | tf_op jit(solution)/shard_map/all_to_all | solution.py:1102
  200.9 8.3 %copy-start.24 = (f32[3,768]{1,0:T(4,128)S(1)}, f32[3,768]{1,0:T(4,128)}, u32[]{:S(2)}) copy-start(f32[3,768]{1,0:T(4,128)} %get-tuple-element.223) | copy-start | bytes 27652
  200.9 8.3 %copy-start.25 = (f32[3,768]{1,0:T(4,128)S(1)}, f32[3,768]{1,0:T(4,128)}, u32[]{:S(2)}) copy-start(f32[3,768]{1,0:T(4,128)} %get-tuple-element.222) | copy-start | bytes 27652
  200.9 8.8 %copy-start.23 = (f32[1,3072]{1,0:T(1,128)S(1)}, f32[1,3072]{1,0:T(1,128)}, u32[]{:S(2)}) copy-start(f32[1,3072]{1,0:T(1,128)} %get-tuple-element.224) | copy-start | bytes 36868
  200.9 9.7 %copy-start.28 = (f32[3,2,128]{2,1,0:T(2,128)S(1)}, f32[3,2,128]{2,1,0:T(2,128)}, u32[]{:S(2)}) copy-start(f32[3,2,128]{2,1,0:T(2,128)} %get-tuple-element.226) | copy-start | bytes 9220
  200.9 9.7 %copy-start.30 = (f32[3,2,128]{2,1,0:T(2,128)S(1)}, f32[3,2,128]{2,1,0:T(2,128)}, u32[]{:S(2)}) copy-start(f32[3,2,128]{2,1,0:T(2,128)} %get-tuple-element.225) | copy-start | bytes 9220
  201.7 1.4 copy-start.10
  203.1 11.3 %copy-start.5 = (bf16[768,1152]{1,0:T(8,128)(2,1)}, bf16[768,1152]{1,0:T(8,128)(2,1)S(1)}, u32[]{:S(2)}) copy-start(bf16[768,1152]{1,0:T(8,128)(2,1)S(1)} %collective-permute-done.4.rest_1_) | copy-start | bytes 5308420
  206.8 16.5 %collective-permute-start.5 = (bf16[4,24,1920]{2,1,0:T(8,128)(2,1)}, bf16[4,24,1920]{2,1,0:T(8,128)(2,1)S(1)}, u32[]{:S(2)}, u32[]{:S(2)}) collective-permute-start(bf16[4,24,1920]{2,1,0:T(8,128)(2,1)} %get-tuple-element.215), channel_id=1, source_target_pairs={{0,4},{4,0},{8,12},{12,8},{16,20},{20,16},{24,28},{28,24},{1,5},{5... | collective-permute-start | bytes 1105928 | tf_op jit(solution)/shard_map/ppermute | solution.py:869
  207.6 15.7 %collective-permute-start.6 = (bf16[4,24,1920]{2,1,0:T(8,128)(2,1)}, bf16[4,24,1920]{2,1,0:T(8,128)(2,1)S(1)}, u32[]{:S(2)}, u32[]{:S(2)}) collective-permute-start(bf16[4,24,1920]{2,1,0:T(8,128)(2,1)} %get-tuple-element.216), channel_id=1, source_target_pairs={{0,2},{1,3},{2,0},{3,1},{4,6},{5,7},{6,4},{7,5},{8,10},{9,11},{10,... | collective-permute-start | bytes 1105928 | tf_op jit(solution)/shard_map/ppermute | solution.py:869
  210.8 4.7 %copy-start.27 = (f32[2,384]{1,0:T(2,128)S(1)}, f32[2,384]{1,0:T(2,128)}, u32[]{:S(2)}) copy-start(f32[2,384]{1,0:T(2,128)} %get-tuple-element.221) | copy-start | bytes 9220
  210.8 4.7 %copy-start.29 = (f32[2,384]{1,0:T(2,128)S(1)}, f32[2,384]{1,0:T(2,128)}, u32[]{:S(2)}) copy-start(f32[2,384]{1,0:T(2,128)} %get-tuple-element.220) | copy-start | bytes 9220
  223.3 3.3 %copy-start.14 = (bf16[4,24,1920]{2,1,0:T(8,128)(2,1)}, bf16[4,24,1920]{2,1,0:T(8,128)(2,1)S(1)}, u32[]{:S(2)}) copy-start(bf16[4,24,1920]{2,1,0:T(8,128)(2,1)S(1)} %collective-permute-done.5.got_a) | copy-start | bytes 1105924
  223.4 3.3 %copy-start.15 = (bf16[4,24,1920]{2,1,0:T(8,128)(2,1)}, bf16[4,24,1920]{2,1,0:T(8,128)(2,1)S(1)}, u32[]{:S(2)}) copy-start(bf16[4,24,1920]{2,1,0:T(8,128)(2,1)S(1)} %collective-permute-done.6.got_b) | copy-start | bytes 1105924
  226.6 9.0 %copy-start.32 = (bf16[4,2,24,1280]{3,2,1,0:T(8,128)(2,1)S(1)}, bf16[4,2,24,1280]{3,2,1,0:T(8,128)(2,1)}, u32[]{:S(2)}) copy-start(bf16[4,2,24,1280]{3,2,1,0:T(8,128)(2,1)} %get-tuple-element.236) | copy-start | bytes 1474564
  229.1 41.4 %all-to-all-start.2 = ((bf16[4,48,1920]{2,1,0:T(8,128)(2,1)}), bf16[4,48,1920]{2,1,0:T(8,128)(2,1)S(1)}, u32[]{:S(2)}, u32[]{:S(2)}) async-start(bf16[4,48,1920]{2,1,0:T(8,128)(2,1)} %third_sums.2), calls=%async_computation.2 | async-start | bytes 1474560 | tf_op jit(solution)/shard_map/all_to_all | solution.py:983
  235.5 11.8 %collective-permute-start.7 = (bf16[4,2,24,1280]{3,2,1,0:T(8,128)(2,1)}, bf16[4,2,24,1280]{3,2,1,0:T(8,128)(2,1)S(1)}, u32[]{:S(2)}, u32[]{:S(2)}) collective-permute-start(bf16[4,2,24,1280]{3,2,1,0:T(8,128)(2,1)} %get-tuple-element.235), channel_id=1, source_target_pairs={{0,2},{1,3},{2,0},{3,1},{4,6},{5,7},{6,4},{7,5},{8,10},{9,11},{10,... | collective-permute-start | bytes 1474568 | tf_op jit(solution)/shard_map/ppermute | solution.py:869
  235.6 16.4 %collective-permute-start.8 = (bf16[4,2,24,1280]{3,2,1,0:T(8,128)(2,1)S(1)}, bf16[4,2,24,1280]{3,2,1,0:T(8,128)(2,1)S(1)}, u32[]{:S(2)}, u32[]{:S(2)}) collective-permute-start(bf16[4,2,24,1280]{3,2,1,0:T(8,128)(2,1)S(1)} %copy-done.32), channel_id=1, source_target_pairs={{0,4},{4,0},{8,12},{12,8},{16,20},{20,16},{24,28},{28,24},{1,5},{5... | collective-permute-start | bytes 1474568 | tf_op jit(solution)/shard_map/ppermute | solution.py:869
  236.4 19.0 %collective-permute-start.9 = (bf16[2,20,768]{2,0,1:T(2,128)(2,1)S(1)}, bf16[2,20,768]{2,0,1:T(2,128)(2,1)S(1)}, u32[]{:S(2)}, u32[]{:S(2)}) collective-permute-start(bf16[2,20,768]{2,0,1:T(2,128)(2,1)S(1)} %get-tuple-element.246), channel_id=1, source_target_pairs={{0,1},{1,0},{2,3},{3,2},{4,5},{5,4},{6,7},{7,6},{8,9},{9,8},{10,11... | collective-permute-start | bytes 184328 | tf_op jit(solution)/shard_map/ppermute | solution.py:869
  236.4 19.0 %collective-permute-start.10 = (bf16[2,20,768]{2,0,1:T(2,128)(2,1)S(1)}, bf16[2,20,768]{2,0,1:T(2,128)(2,1)S(1)}, u32[]{:S(2)}, u32[]{:S(2)}) collective-permute-start(bf16[2,20,768]{2,0,1:T(2,128)(2,1)S(1)} %get-tuple-element.247), channel_id=1, source_target_pairs={{0,2},{1,3},{2,0},{3,1},{4,6},{5,7},{6,4},{7,5},{8,10},{9,11},{10,... | collective-permute-start | bytes 184328 | tf_op jit(solution)/shard_map/ppermute | solution.py:869
  237.7 17.7 %collective-permute-start.11 = (bf16[2,20,768]{2,0,1:T(2,128)(2,1)S(1)}, bf16[2,20,768]{2,0,1:T(2,128)(2,1)S(1)}, u32[]{:S(2)}, u32[]{:S(2)}) collective-permute-start(bf16[2,20,768]{2,0,1:T(2,128)(2,1)S(1)} %get-tuple-element.248), channel_id=1, source_target_pairs={{0,3},{1,2},{2,1},{3,0},{4,7},{5,6},{6,5},{7,4},{8,11},{9,10},{10,... | collective-permute-start | bytes 184328 | tf_op jit(solution)/shard_map/ppermute | solution.py:869
  247.3 4.8 %copy-start.12 = (bf16[4,2,24,1280]{3,2,1,0:T(8,128)(2,1)}, bf16[4,2,24,1280]{3,2,1,0:T(8,128)(2,1)S(1)}, u32[]{:S(2)}) copy-start(bf16[4,2,24,1280]{3,2,1,0:T(8,128)(2,1)S(1)} %collective-permute-done.7.got_a) | copy-start | bytes 1474564
  252.0 0.8 copy-start.13
  255.4 7.2 %collective-permute-start.12 = (bf16[4,24,1280]{2,1,0:T(8,128)(2,1)}, bf16[4,24,1280]{2,1,0:T(8,128)(2,1)S(1)}, u32[]{:S(2)}, u32[]{:S(2)}) collective-permute-start(bf16[4,24,1280]{2,1,0:T(8,128)(2,1)} %get-tuple-element.249), channel_id=1, source_target_pairs={{0,4},{4,0},{8,12},{12,8},{16,20},{20,16},{24,28},{28,24},{1,5},{5... | collective-permute-start | bytes 737288 | tf_op jit(solution)/shard_map/ppermute | solution.py:869
  255.8 6.9 %collective-permute-start.13 = (bf16[4,24,1280]{2,1,0:T(8,128)(2,1)}, bf16[4,24,1280]{2,1,0:T(8,128)(2,1)S(1)}, u32[]{:S(2)}, u32[]{:S(2)}) collective-permute-start(bf16[4,24,1280]{2,1,0:T(8,128)(2,1)} %get-tuple-element.250), channel_id=1, source_target_pairs={{0,2},{1,3},{2,0},{3,1},{4,6},{5,7},{6,4},{7,5},{8,10},{9,11},{10,... | collective-permute-start | bytes 737288 | tf_op jit(solution)/shard_map/ppermute | solution.py:869
  262.6 0.7 copy-start.20
  262.7 0.7 copy-start.21
  270.4 0.9 copy-start
  273.2 5.3 %copy-start.9 = (bf16[48,1920]{1,0:T(8,128)(2,1)S(1)}, bf16[48,1920]{1,0:T(8,128)(2,1)}, u32[]{:S(2)}) copy-start(bf16[48,1920]{1,0:T(8,128)(2,1)} %part_sums.2) | copy-start | bytes 552964
  273.2 20.3 %copy-start.2 = (f32[384,384]{1,0:T(8,128)S(1)}, f32[384,384]{1,0:T(8,128)}, u32[]{:S(2)}) copy-start(f32[384,384]{1,0:T(8,128)} %reduce-scatter.2.cloned.1.call-done) | copy-start | bytes 1769476
  274.4 16.5 %all-to-all-start.3 = ((bf16[4,48,1280]{2,1,0:T(8,128)(2,1)}), bf16[4,48,1280]{2,1,0:T(8,128)(2,1)S(1)}, u32[]{:S(2)}, u32[]{:S(2)}) async-start(bf16[4,48,1280]{2,1,0:T(8,128)(2,1)} %third_sums.3), calls=%async_computation.4 | async-start | bytes 983040 | tf_op jit(solution)/shard_map/all_to_all | solution.py:983
  277.8 11.8 %collective-permute-start.15 = (bf16[384,384]{1,0:T(8,128)(2,1)S(1)}, bf16[384,384]{1,0:T(8,128)(2,1)S(1)}, u32[]{:S(2)}, u32[]{:S(2)}) collective-permute-start(bf16[384,384]{1,0:T(8,128)(2,1)S(1)} %convert_element_type.85), channel_id=1, source_target_pairs={{0,2},{1,3},{2,0},{3,1},{4,6},{5,7},{6,4},{7,5},{8,10},{9,11},{10,... | collective-permute-start | bytes 884744 | tf_op jit(solution)/shard_map/ppermute | solution.py:869
  278.5 11.1 %collective-permute-start.14 = (bf16[48,1920]{1,0:T(8,128)(2,1)S(1)}, bf16[48,1920]{1,0:T(8,128)(2,1)S(1)}, u32[]{:S(2)}, u32[]{:S(2)}) collective-permute-start(bf16[48,1920]{1,0:T(8,128)(2,1)S(1)} %copy-done.9), channel_id=1, source_target_pairs={{0,2},{1,3},{2,0},{3,1},{4,6},{5,7},{6,4},{7,5},{8,10},{9,11},{10,... | collective-permute-start | bytes 552968 | tf_op jit(solution)/shard_map/ppermute | solution.py:869
  290.9 0.8 copy-start.4
  293.4 0.9 copy-start.11
  293.5 8.9 %copy-start.6 = (bf16[96,1920]{1,0:T(8,128)(2,1)}, bf16[96,1920]{1,0:T(8,128)(2,1)S(1)}, u32[]{:S(2)}) copy-start(bf16[96,1920]{1,0:T(8,128)(2,1)S(1)} %pad_maximum_fusion.1.own) | copy-start | bytes 1105924
  293.6 6.1 %copy-start.7 = (bf16[384,384]{1,0:T(8,128)(2,1)}, bf16[384,384]{1,0:T(8,128)(2,1)S(1)}, u32[]{:S(2)}) copy-start(bf16[384,384]{1,0:T(8,128)(2,1)S(1)} %add_convert_fusion.own) | copy-start | bytes 884740
  293.6 5.9 %collective-permute-start.18 = (bf16[96,1920]{1,0:T(8,128)(2,1)S(1)}, bf16[96,1920]{1,0:T(8,128)(2,1)S(1)}, u32[]{:S(2)}, u32[]{:S(2)}) collective-permute-start(bf16[96,1920]{1,0:T(8,128)(2,1)S(1)} %pad_maximum_fusion.1.own), channel_id=1, source_target_pairs={{0,1},{1,0},{2,3},{3,2},{4,5},{5,4},{6,7},{7,6},{8,9},{9,8},{10,11... | collective-permute-start | bytes 1105928 | tf_op jit(solution)/shard_map/ppermute | solution.py:869
  293.7 5.8 %collective-permute-start.17 = (bf16[384,384]{1,0:T(8,128)(2,1)S(1)}, bf16[384,384]{1,0:T(8,128)(2,1)S(1)}, u32[]{:S(2)}, u32[]{:S(2)}) collective-permute-start(bf16[384,384]{1,0:T(8,128)(2,1)S(1)} %add_convert_fusion.own), channel_id=1, source_target_pairs={{0,1},{1,0},{2,3},{3,2},{4,5},{5,4},{6,7},{7,6},{8,9},{9,8},{10,11... | collective-permute-start | bytes 884744 | tf_op jit(solution)/shard_map/ppermute | solution.py:869
  294.3 5.2 %collective-permute-start.16 = (bf16[48,1280]{1,0:T(8,128)(2,1)S(1)}, bf16[48,1280]{1,0:T(8,128)(2,1)S(1)}, u32[]{:S(2)}, u32[]{:S(2)}) collective-permute-start(bf16[48,1280]{1,0:T(8,128)(2,1)S(1)} %copy-done.11), channel_id=1, source_target_pairs={{0,2},{1,3},{2,0},{3,1},{4,6},{5,7},{6,4},{7,5},{8,10},{9,11},{10,... | collective-permute-start | bytes 368648 | tf_op jit(solution)/shard_map/ppermute | solution.py:869
  299.5 0.7 copy-start.17
  299.5 2.9 copy-start.16
  299.6 5.2 %copy-start.8 = (bf16[96,1280]{1,0:T(8,128)(2,1)}, bf16[96,1280]{1,0:T(8,128)(2,1)S(1)}, u32[]{:S(2)}) copy-start(bf16[96,1280]{1,0:T(8,128)(2,1)S(1)} %pad_maximum_fusion.3.own) | copy-start | bytes 737284
  299.6 5.2 %collective-permute-start.19 = (bf16[96,1280]{1,0:T(8,128)(2,1)S(1)}, bf16[96,1280]{1,0:T(8,128)(2,1)S(1)}, u32[]{:S(2)}, u32[]{:S(2)}) collective-permute-start(bf16[96,1280]{1,0:T(8,128)(2,1)S(1)} %pad_maximum_fusion.3.own), channel_id=1, source_target_pairs={{0,1},{1,0},{2,3},{3,2},{4,5},{5,4},{6,7},{7,6},{8,9},{9,8},{10,11... | collective-permute-start | bytes 737288 | tf_op jit(solution)/shard_map/ppermute | solution.py:869
  304.8 0.7 copy-start.18
Sparse Core Ops, SparseCore 0:
  148.9 122.9 reduce-scatter.1

commit v2 on v1

--- a/solution.py
+++ b/solution.py
@@ -81,25 +81,47 @@
     return term if total is None else total + term
 
 
+Q_SCALE = 0.125 * LOG2E
+
+
+def project_kernel(xc, wq, wk, wv, before, q_out, k_out, v_out):
+    x = xc[0]
+    bias = before[...].astype(F32)
+    q_out[0] = ((nn(x, wq[...]) + bias[0:1]) * Q_SCALE).astype(BF16)
+    k_out[0] = nn(x, wk[...]).astype(BF16)
+    v_out[0] = (nn(x, wv[...]) + bias[1:2]).astype(BF16)
+
+
+def project(xc, wq, wk, wv, before):
+    seqs, length, width = xc.shape
+    rows = pl.BlockSpec((1, length // 2, width), lambda s, i: (s, i, 0))
+    weight = full_spec((width, width))
+    return pl.pallas_call(
+        project_kernel,
+        grid=(seqs, 2),
+        in_specs=[rows, weight, weight, weight, full_spec((2, width))],
+        out_specs=[rows] * 3,
+        out_shape=[jax.ShapeDtypeStruct(xc.shape, BF16)] * 3,
+        compiler_params=params(),
+        name="project",
+    )(xc, wq, wk, wv, before)
+
+
 def attention_forward_kernel(
-    xc, xq, wq, wk, wv, before, rank_row, thr_c, thr_q, offsets, table,
-    ctx_out, e_out, rr_out, q_out, k_out, v_out, mask, s_buf,
+    q_in, k_in, v_in, xq, wq, before, rank_row, thr_c, thr_q, offsets, table,
+    ctx_out, e_out, rr_out, q_out, mask, s_buf,
 ):
     pair = pl.program_id(1)
-    length = xc.shape[1]
+    length = q_in.shape[1]
     slots = xq.shape[1]
     total = length + slots
     tiles = length // TILE
 
     @pl.when(pair == 0)
     def _():
-        scale = 0.125 * LOG2E
-        x = xc[0]
-        bias = before[...].astype(F32)
-        q_out[0, :length] = ((nn(x, wq[...]) + bias[0:1]) * scale).astype(BF16)
-        k_out[0] = nn(x, wk[...]).astype(BF16)
-        v_out[0] = (nn(x, wv[...]) + bias[1:2]).astype(BF16)
-        q_out[0, length:] = ((nn(xq[0], wq[...]) + bias[0:1]) * scale).astype(BF16)
+        bias = before[...].astype(F32)[0:1]
+        q_out[0, :length] = q_in[0]
+        q_out[0, length:] = ((nn(xq[0], wq[...]) + bias) * Q_SCALE).astype(BF16)
         ranks = rank_row[0]
         for i in range(tiles):
             rows = slice(i * TILE, (i + 1) * TILE)
@@ -110,8 +132,8 @@
         mask[length:] = jnp.where(ranks < thr_q[0], 0.0, NEG)
 
     cols = pl.ds(pl.multiple_of(pair * TILE, TILE), TILE)
-    k_pair = k_out[0, :, cols]
-    v_pair = v_out[0, :, cols]
+    k_pair = k_in[0, :, cols]
+    v_pair = v_in[0, :, cols]
     q_pair = q_out[0, :, cols]
     lane = lax.broadcasted_iota(jnp.int32, (1, TILE), 1)
     block_of, row_of = slot_position(rank_row[0], thr_q[0], length)
@@ -185,8 +207,8 @@
     attend(*work[-1])
 
 
-def attention_forward(xc, xq, wq, wk, wv, before, rank_row, thr_c, thr_q, offsets, table):
-    seqs, length, width = xc.shape
+def attention_forward(q, k, v, xq, wq, before, rank_row, thr_c, thr_q, offsets, table):
+    seqs, length, width = q.shape
     slots = xq.shape[1]
     rows = length + slots
 
@@ -199,9 +221,9 @@
         grid=(seqs, PAIRS),
         in_specs=[
             by_seq((length, width)),
+            by_seq((length, width)),
+            by_seq((length, width)),
             by_seq((slots, width)),
-            full_spec((width, width)),
-            full_spec((width, width)),
             full_spec((width, width)),
             full_spec((2, width)),
             by_seq((1, length)),
@@ -215,21 +237,17 @@
             pl.BlockSpec((1, 2, rows, length), lambda s, p: (s, p, 0, 0)),
             by_pair,
             by_seq((rows, width)),
-            by_seq((length, width)),
-            by_seq((length, width)),
         ],
         out_shape=[
             jax.ShapeDtypeStruct((seqs, rows, width), BF16),
             jax.ShapeDtypeStruct((seqs, HEADS, rows, length), BF16),
             jax.ShapeDtypeStruct((seqs, rows, width), F32),
             jax.ShapeDtypeStruct((seqs, rows, width), BF16),
-            jax.ShapeDtypeStruct((seqs, length, width), BF16),
-            jax.ShapeDtypeStruct((seqs, length, width), BF16),
         ],
         scratch_shapes=[pltpu.VMEM((rows, length), F32), pltpu.VMEM((2, rows, length), F32)],
         compiler_params=params(),
         name="attention_forward",
-    )(xc, xq, wq, wk, wv, before, rank_row, thr_c, thr_q, offsets, table)
+    )(q, k, v, xq, wq, before, rank_row, thr_c, thr_q, offsets, table)
 
 
 def attention_backward_kernel(
@@ -481,8 +499,8 @@
 
 
 def rows_forward_kernel(
-    half, ctx, xc, xq, cot_c, cot_q, w_output, w_inner, w_outer, after, hidden_bias, gain, shift,
-    out_c, out_q, slope_out, hidden_out, unit_out, scale_out, outer_out, sums, grad_other, grad_mine,
+    ctx, xc, xq, cot_c, cot_q, w_output, w_inner, w_outer, after, hidden_bias, gain, shift,
+    out_c, out_q, slope_out, hidden_out, unit_out, scale_out, outer_out, sums, grad_out,
     wo, wi, wu, sems, acc, act, outer, sums_acc,
 ):
     step = pl.program_id(0)
@@ -551,11 +569,7 @@
     @pl.when(step >= seqs)
     def _():
         cols = pl.ds(pl.multiple_of((step - seqs) * GRAD_TILE, GRAD_TILE), GRAD_TILE)
-        grad = tn(act[:, cols], outer[...]).astype(BF16)
-        part = grad.shape[1] // 2
-        first = half[0] == 0
-        grad_mine[...] = jnp.where(first, grad[:, :part], grad[:, part:])
-        grad_other[...] = jnp.where(first, grad[:, part:], grad[:, :part])
+        grad_out[...] = tn(act[:, cols], outer[...]).astype(BF16)
 
 
 def rows_backward_kernel(
@@ -644,7 +658,7 @@
 
 
 def rows_forward(
-    half, ctx, xc, xq, cot_c, cot_q, w_output, w_inner, w_outer, after, hidden_bias, gain, shift
+    ctx, xc, xq, cot_c, cot_q, w_output, w_inner, w_outer, after, hidden_bias, gain, shift
 ):
     seqs, rows, width = ctx.shape
     length, slots = xc.shape[1], xq.shape[1]
@@ -652,19 +666,19 @@
     total = seqs * rows
 
     def by_seq(n):
-        return pl.BlockSpec((1, n, width), lambda s, half: (jnp.minimum(s, seqs - 1), 0, 0))
+        return pl.BlockSpec((1, n, width), lambda s: (jnp.minimum(s, seqs - 1), 0, 0))
 
     def block(n):
-        return pl.BlockSpec((rows, n), lambda s, half: (jnp.minimum(s, seqs - 1), 0))
+        return pl.BlockSpec((rows, n), lambda s: (jnp.minimum(s, seqs - 1), 0))
 
     grad_block = pl.BlockSpec(
-        (GRAD_TILE, width // 2), lambda s, half: (jnp.maximum(s - seqs, 0), 0)
+        (GRAD_TILE, width), lambda s: (jnp.maximum(s - seqs, 0), 0)
     )
     hbm = pl.BlockSpec(memory_space=pl.ANY)
     return pl.pallas_call(
         rows_forward_kernel,
         grid_spec=pltpu.PrefetchScalarGridSpec(
-            num_scalar_prefetch=1,
+            num_scalar_prefetch=0,
             grid=(seqs + ff // GRAD_TILE,),
             in_specs=[
             by_seq(rows), by_seq(length), by_seq(slots), by_seq(length), by_seq(slots),
@@ -674,7 +688,7 @@
         out_specs=[
             by_seq(length), by_seq(slots), block(ff), block(width),
             block(width), block(TILE), block(width), full_spec((3, width)),
-            grad_block, grad_block,
+            grad_block,
         ],
         scratch_shapes=weight_scratch(width, ff) + [
             pltpu.VMEM((rows, width), F32),
@@ -692,12 +706,11 @@
             jax.ShapeDtypeStruct((total, TILE), F32),
             jax.ShapeDtypeStruct((total, width), BF16),
             jax.ShapeDtypeStruct((3, width), F32),
-            jax.ShapeDtypeStruct((ff, width // 2), BF16),
-            jax.ShapeDtypeStruct((ff, width // 2), BF16),
+            jax.ShapeDtypeStruct((ff, width), BF16),
         ],
         compiler_params=params(),
         name="rows_forward",
-    )(half, ctx, xc, xq, cot_c, cot_q, w_output, w_inner, w_outer, after, hidden_bias, gain, shift)
+    )(ctx, xc, xq, cot_c, cot_q, w_output, w_inner, w_outer, after, hidden_bias, gain, shift)
 
 
 def rows_backward(half, seqs, slots, outer, slope, unit, scale, hidden, ctx, w_output, w_inner, w_outer, gain):
@@ -806,63 +819,46 @@
     )(xc, xq, dq, dk, dv, *extra)
 
 
-def content_grad_kernel(
-    half, first, dq_o, dk_o, dv_o, dq_m, dk_m, dv_m, wq_o, wk_o, wv_o, wq_m, wk_m, wv_m, out,
+def input_grad_kernel(
+    half, first_c, first_q, dq_o, dk_o, dv_o, dq_m, dk_m, dv_m, wq_o, wk_o, wv_o, wq_m, wk_m, wv_m,
+    out_c, out_q,
 ):
     length = dk_o.shape[1]
     left = [dq_o[0, :length], dk_o[0], dv_o[0], dq_m[0, :length], dk_m[0], dv_m[0]]
     right = [wq_o[...], wk_o[...], wv_o[...], wq_m[...], wk_m[...], wv_m[...]]
-    out[0] = first[0] + nt(jnp.concatenate(left, axis=1), jnp.concatenate(right, axis=1))
-
-
-def slot_grad_kernel(half, first, dq_o, dq_m, wq, out):
-    seqs, rows, part = dq_o.shape
-    slots = out.shape[1]
-    length = rows - slots
-    first_half = half[0] == 0
-    a, b = wq[:, :part], wq[:, part:]
-    w_m, w_o = jnp.where(first_half, a, b), jnp.where(first_half, b, a)
-    for s in range(seqs):
-        grad = nt(dq_o[s, length:], w_o) + nt(dq_m[s, length:], w_m)
-        out[s] = (first[s] + grad).astype(BF16)
-
-
-def slot_grad(half, first, dq_o, dq_m, wq, slots):
-    vmem = pl.BlockSpec(memory_space=pltpu.VMEM)
-    return pl.pallas_call(
-        slot_grad_kernel,
-        in_specs=[pl.BlockSpec(memory_space=pltpu.SMEM)] + [vmem] * 4,
-        out_specs=vmem,
-        out_shape=jax.ShapeDtypeStruct((dq_o.shape[0], slots, wq.shape[0]), BF16),
-        compiler_params=params(),
-        name="slot_grad",
-    )(half, first, dq_o, dq_m, wq)
-
-
-def content_grad(half, first, other, mine, wq, wk, wv):
+    out_c[0] = first_c[0] + nt(jnp.concatenate(left, axis=1), jnp.concatenate(right, axis=1))
+    dq = jnp.concatenate([dq_o[0, length:], dq_m[0, length:]], axis=1)
+    wq = jnp.concatenate([wq_o[...], wq_m[...]], axis=1)
+    out_q[0] = (first_q[0] + nt(dq, wq)).astype(BF16)
+
+
+def input_grad(half, first_c, first_q, other, mine, wq, wk, wv):
     seqs, rows, part = other[0].shape
     length = other[1].shape[1]
     width = wq.shape[0]
 
-    def by_seq(n):
-        return pl.BlockSpec((1, n, part), lambda s, half: (s, 0, 0))
-
-    grads = [by_seq(rows), by_seq(length), by_seq(length)]
+    def by_seq(n, cols):
+        return pl.BlockSpec((1, n, cols), lambda s, half: (s, 0, 0))
+
+    grads = [by_seq(rows, part), by_seq(length, part), by_seq(length, part)]
+    firsts = [by_seq(length, width), by_seq(rows - length, width)]
     w_other = pl.BlockSpec((width, part), lambda s, half: (0, 1 - half[0]))
     w_mine = pl.BlockSpec((width, part), lambda s, half: (0, half[0]))
     return pl.pallas_call(
-        content_grad_kernel,
+        input_grad_kernel,
         grid_spec=pltpu.PrefetchScalarGridSpec(
             num_scalar_prefetch=1,
             grid=(seqs,),
-            in_specs=[pl.BlockSpec((1, length, width), lambda s, half: (s, 0, 0))]
-            + grads * 2 + [w_other] * 3 + [w_mine] * 3,
-            out_specs=pl.BlockSpec((1, length, width), lambda s, half: (s, 0, 0)),
+            in_specs=firsts + grads * 2 + [w_other] * 3 + [w_mine] * 3,
+            out_specs=firsts,
         ),
-        out_shape=jax.ShapeDtypeStruct((seqs, length, width), F32),
+        out_shape=[
+            jax.ShapeDtypeStruct((seqs, length, width), F32),
+            jax.ShapeDtypeStruct((seqs, rows - length, width), BF16),
+        ],
         compiler_params=params(),
-        name="content_grad",
-    )(half, first, *other, *mine, wq, wk, wv, wq, wk, wv)
+        name="input_grad",
+    )(half, first_c, first_q, *other, *mine, wq, wk, wv, wq, wk, wv)
 
 
 def swap(value, axis, count, stride):
@@ -1071,7 +1067,10 @@
     ranks = lax.dynamic_slice_in_dim(perm_ranks, group * seqs, seqs, 0)
 
     both = jnp.concatenate([query_in, cot_query], axis=2)
-    both = lax.all_to_all(both, "qry", 0, 1, tiled=True)
+    (both,), (q_content, k, v) = beside(
+        [(lambda a: lax.all_to_all(a, "qry", 0, 1, tiled=True), both)],
+        lambda: project(content_in, w_query, w_key, w_value, b_before),
+    )
     xq, cot_q = both[:, :, :width], both[:, :, width:]
     slots = xq.shape[1]
     floor = lengths[:, None] - PRED
@@ -1083,12 +1082,12 @@
     one_hot = (one_hot[None, :] == jnp.arange(BUCKETS, dtype=jnp.int32)[:, None]).astype(BF16)
     offsets = jnp.dot(rel_table, one_hot, preferred_element_type=F32)[:, None, :]
 
-    ctx, e, rr, q, k, v = attention_forward(
-        content_in, xq, w_query, w_key, w_value, b_before, rank_row, thr_c, thr_q, offsets,
+    ctx, e, rr, q = attention_forward(
+        q_content, k, v, xq, w_query, b_before, rank_row, thr_c, thr_q, offsets,
         rel_table.astype(F32),
     )
-    (out_c, out_q, slope, hidden, unit, scale, outer, sums_f, o_other, o_mine) = rows_forward(
-        mine, ctx, content_in, xq, cot_content, cot_q, w_output, w_inner, w_outer, b_after,
+    (out_c, out_q, slope, hidden, unit, scale, outer, sums_f, g_outer) = rows_forward(
+        ctx, content_in, xq, cot_content, cot_q, w_output, w_inner, w_outer, b_after,
         b_hidden[None], norm_gain, norm_shift,
     )
     ff = slope.shape[1]
@@ -1098,11 +1097,8 @@
     red_i = Reduction(tok)
     red_b = Reduction(tok)
 
-    def to_slots(a):
-        return lax.all_to_all(a, "qry", 1, 0, tiled=True)
-
     def slot_blocks(a):
-        a = a.reshape(seqs, 4, slots // 4, width)
+        a = a.reshape(seqs, 4, slots // 4, a.shape[2])
         return [take(a, 1, group ^ n) for n in range(4)]
 
     def slot_moves(blocks):
@@ -1118,15 +1114,11 @@
     def over_tok(a):
         return lax.psum_scatter(a, "tok", scatter_dimension=0, tiled=True)
 
-    (got_o,), (first_c, first_q, d_ctx, sums_b, inner_sums, i_other, i_mine) = beside(
-        [(swap_core, o_other)],
-        lambda a: rows_backward(
-            mine, seqs, slots, a, slope, unit, scale, hidden, ctx.reshape(-1, width), w_output,
-            w_inner, w_outer, norm_gain,
-        ),
-        (outer,),
-    )
-    o_sum = over_tok(o_mine.astype(F32) + got_o.astype(F32))
+    o_sum = over_tok(g_outer)
+    first_c, first_q, d_ctx, sums_b, inner_sums, i_other, i_mine = rows_backward(
+        mine, seqs, slots, outer, slope, unit, scale, hidden, ctx.reshape(-1, width), w_output,
+        w_inner, w_outer, norm_gain,
+    )
     (got_i,), back_other = beside(
         [(swap_core, i_other)],
         lambda a: attention_backward(other, q, k, v, e, ctx, a, rr, rank_row, thr_q),
@@ -1139,8 +1131,8 @@
         got = swap_core(b_other)
         return got, attention_backward(mine, q, k, v, e, ctx, cotangent, rr, rank_row, thr_q)
 
-    (got_i, out_q), (got_b, back_mine) = beside(
-        [(red_i.first_moves, red_i.first_sends(i_mine, got_i)), (to_slots, out_q)],
+    (got_i,), (got_b, back_mine) = beside(
+        [(red_i.first_moves, red_i.first_sends(i_mine, got_i))],
         grad_and_backward,
         (*back_other[:3], d_ctx),
     )
@@ -1161,49 +1153,53 @@
         ]
     )
     vectors = jnp.pad(vectors, ((0, TILE - vectors.shape[0]), (0, 0)))
-    (got_i,), b_mine = beside(
-        [(red_i.second_moves, red_i.second_sends(got_i))],
+    o_parts = o_sum.reshape(ff // tok, 2, part)
+    (got_i, got_o), b_mine = beside(
+        [
+            (red_i.second_moves, red_i.second_sends(got_i)),
+            (swap_core, take(o_parts, 1, 1 - core)),
+        ],
         lambda a: grad_before(content_in, xq, a, *back_mine[1:3], vectors, got_b),
         (back_mine[0],),
     )
-    d_query = slot_grad(mine, first_q, back_other[0], back_mine[0], w_query, slots)
-    d_query = slot_blocks(d_query)
+    o_sum = low_sum(take(o_parts, 1, core), got_o)
     send_i = red_i.third_sends(got_i)
     send_b = red_b.first_sends(b_mine)
-    send_i, send_b, d_query, first_c = lax.optimization_barrier(
-        (send_i, send_b, d_query, first_c)
-    )
+    send_i, send_b, first_c = lax.optimization_barrier((send_i, send_b, first_c))
     got_i = red_i.third_moves(send_i)
     got_b = red_b.first_moves(send_b)
-    got_q = slot_moves(d_query)
-    d_content = content_grad(
-        mine, first_c, back_other[:3], back_mine[:3], w_query, w_key, w_value
-    )
-    got_b, d_content = lax.optimization_barrier((got_b, d_content))
-    (got_b,), d_query = beside(
+    d_content, d_query = input_grad(
+        mine, first_c, first_q, back_other[:3], back_mine[:3], w_query, w_key, w_value
+    )
+    got_b, d_content, d_query = lax.optimization_barrier((got_b, d_content, d_query))
+    (got_b,), rows_q = beside(
         [(red_b.second_moves, red_b.second_sends(got_b))],
-        lambda *a: slot_rows(a[0], a[1:]).astype(F32),
-        (d_query[0], *got_q),
+        lambda *a: slot_blocks(jnp.concatenate(a, axis=2)),
+        (out_q, d_query),
     )
 
     def swap_x(a):
         return swap(a, "qry", 4, 2)
 
-    (got_b, got_i, got_o), _ = beside(
+    (got_b, got_i, got_o, got_q), _ = beside(
         [
             (red_b.third_moves, red_b.third_sends(got_b)),
             (red_i.far_moves, red_i.far_sends(got_i)),
-            (swap_x, o_sum.astype(BF16)),
+            (swap_x, o_sum),
+            (slot_moves, rows_q),
         ],
     )
     o_sum = low_sum(o_sum, got_o)
-    (got_b, got_o, got_i), _ = beside(
+    (got_b, got_o, got_i), rows_q = beside(
         [
             (red_b.far_moves, red_b.far_sends(got_b)),
             (swap_core, o_sum),
             (red_i.near_moves, red_i.near_sends(got_i)),
-        ]
-    )
+        ],
+        lambda *a: slot_rows(a[0], a[1:]),
+        (rows_q[0], *got_q),
+    )
+    out_q, d_query = rows_q[:, :, :width], rows_q[:, :, width:].astype(F32)
     (got_b,), ((g_outer,), (g_inner, g_output)) = beside(
         [(red_b.near_moves, red_b.near_sends(got_b))],
         lambda a, b: (

time: 323 us -> 309 us (0.957)
  waiting for transfers between devices: 34.1 us -> 26.6 us
  other arithmetic: 11.4 us -> 6.98 us
    all_to_all x2, waiting for transfers between devices: 6.07 us -> 0.01 us  [third_moves(): lax.all_to_all(send, 'tok', 0, 0, tiled=True, axis_index_groups=groups)]
    pallas_call x2, Pallas kernels: 12.4 us -> 16.9 us  [the longest x1 9.55 us: input_grad(): pl.pallas_call(input_grad_kernel, grid_spec=pltpu.PrefetchScalarGridSpec(...]
    all_to_all x2 -> x1, waiting for transfers between devices: 4.36 us -> 0.01 us  [on_device(): lax.all_to_all(a, 'qry', 0, 1, tiled=True)]
    add x1 -> x0, other arithmetic: 4.23 us -> none  [on_device(): o_sum = over_tok(o_mine.astype(F32) + got_o.astype(F32))]
    pallas_call x1, Pallas kernels: 28.2 us -> 24.4 us  [attention_forward(): pl.pallas_call(attention_forward_kernel, grid=(seqs, PAIRS), in_specs=[by...]
    all_to_all x2 -> x1, starting transfers between devices: 7.6 us -> 4.21 us  [on_device(): lax.all_to_all(a, 'qry', 0, 1, tiled=True)]
    unnamed x70 -> x69, local copies, waits for them, and re-layouts: 9.62 us -> 9.73 us
  transfers between devices with their start and end apart: 25 -> 24, of which waited for: 11 -> 8; matrix products, arithmetic and copies ran while one was open for 4% -> 4% of each run, Pallas kernels for 39% -> 39%
where the time goes in v2:
time: 309 us; the launch traced here: 305 us
  Pallas kernels  204 us (66%)
  starting transfers between devices  30.9 us (10%)
  waiting for transfers between devices  26.6 us (9%)
  local copies, waits for them, and re-layouts  22 us (7%)
  between operations  14.8 us (5%)
  other arithmetic  6.98 us (2%)
    pallas_call x1, Pallas kernels, rows_forward(): pl.pallas_call(rows_forward_kernel, grid_spec=pltpu.PrefetchScalarGridSpe...  47.8 us
    pallas_call x1, Pallas kernels, rows_backward(): pl.pallas_call(rows_backward_kernel, grid_spec=pltpu.PrefetchScalarGridSp...  42.3 us
    pallas_call x2, Pallas kernels, attention_backward(): pl.pallas_call(attention_backward_kernel, grid_spec=pltpu.PrefetchScalarG...  31.3 us
    ppermute x20, waiting for transfers between devices, swap(): return lax.ppermute(value, axis, [(i, i ^ stride) for i in range(count)])  26.5 us
    pallas_call x1, Pallas kernels, attention_forward(): pl.pallas_call(attention_forward_kernel, grid=(seqs, PAIRS), in_specs=[by...  24.4 us
    pallas_call x6, Pallas kernels, staged(): pl.pallas_call(kernel, in_specs=[pl.BlockSpec(memory_space=pltpu.SMEM)] +...  18.1 us
    ppermute x20, starting transfers between devices, swap(): return lax.ppermute(value, axis, [(i, i ^ stride) for i in range(count)])  16.7 us
    pallas_call x2, Pallas kernels, grad_before(): pl.pallas_call(grad_before_kernel, grid=(2,), in_specs=[pl.BlockSpec((seq...  12.8 us
  transfers between devices with their start and end apart: 24, of which 8 were waited for; matrix products, arithmetic and copies ran while one was open for 4% of the time, Pallas kernels for 39%

profile of v2, /device:TPU:0, one launch (start us, length us, event | category | flops | bytes accessed | tf_op | source)
XLA Modules:
  0.0 305.2 jit_solution(16087785565840775535)
XLA Ops:
  7.2 1.0 copy.45
  8.2 1.0 copy.46
  9.2 0.9 pad_maximum_fusion
  10.1 4.2 %all-to-all-start = ((bf16[8,20,1536]{2,1,0:T(8,128)(2,1)}), bf16[8,20,1536]{2,1,0:T(8,128)(2,1)S(1)}, u32[]{:S(2)}, u32[]{:S(2)}) async-start(bf16[8,20,1536]{2,1,0:T(8,128)(2,1)} %pad_maximum_fusion), calls=%async_computation | async-start | bytes 1179648 | tf_op jit(solution)/shard_map/all_to_all | solution.py:1071
  14.4 0.8 maximum_bitcast_fusion
  17.7 1.0 copy.49.thr_c
  18.8 7.3 %project.1 = (bf16[2,512,768]{2,1,0:T(8,128)(2,1)}, bf16[2,512,768]{2,1,0:T(8,128)(2,1)}, bf16[2,512,768]{2,1,0:T(8,128)(2,1)}) custom-call(bf16[2,512,768]{2,1,0:T(8,128)(2,1)} %xc.7, bf16[768,768]{1,0:T(8,128)(2,1)} %wq_m.1, bf16[768,768]{1,0:T(8,128)(2,1)} %wk_m.1, bf16[768,768]{1,0:T(8,128)(2,1)} %wv_m.1, bf16[2,768]{1,0:T(2,128)(2,1)} %before.3), custom_call_target="tpu_custom_call" | custom-call | tf_op jit(solution)/shard_map/project/pallas_call | solution.py:99
  26.1 0.7 iota_add_fusion.thr_q
  27.3 0.8 fusion.7
  28.1 24.4 %attention_forward.1 = (bf16[2,592,768]{2,1,0:T(8,128)(2,1)}, bf16[2,12,592,512]{3,2,1,0:T(8,128)(2,1)}, f32[2,592,768]{2,1,0:T(8,128)}, bf16[2,592,768]{2,1,0:T(8,128)(2,1)}) custom-call(bf16[2,512,768]{2,1,0:T(8,128)(2,1)} %get-tuple-element.160.q_in, bf16[2,512,768]{2,1,0:T(8,128)(2,1)} %get-tuple-element.161.k_in.k, ...), custom_call_target="tpu_custom_call" | custom-call | tf_op jit(solution)/shard_map/attention_forward/pallas_call | solution.py:219
  52.5 47.8 %rows_forward.1 = (bf16[2,512,768]{2,1,0:T(8,128)(2,1)}, bf16[2,80,768]{2,1,0:T(8,128)(2,1)}, bf16[1184,3072]{1,0:T(8,128)(2,1)}, bf16[1184,768]{1,0:T(8,128)(2,...) custom-call(bf16[2,592,768]{2,1,0:T(8,128)(2,1)} %get-tuple-element., ...), custom_call_target="tpu_custom_call" | custom-call | tf_op jit(solution)/shard_map/rows_forward/pallas_call | solution.py:678
  100.4 42.3 %rows_backward.1 = (f32[2,512,768]{2,1,0:T(8,128)}, f32[2,80,768]{2,1,0:T(8,128)}, bf16[2,592,768]{2,1,0:T(8,128)(2,1)}, f32[3,768]{1,0:T(4,128)}, f32[1,3072]{1...) custom-call(s32[1]{0:T(128)} %bitcast.7.half.first.core, bf16[1184,768]{1,0:T(8,128)(2,1)} %get-tuple-element.166.outer, ...), custom_call_target="tpu_custom_call" | custom-call | tf_op jit(solution)/shard_map/rows_backward/pallas_call | solution.py:735
  143.8 15.8 %attention_backward.2 = (bf16[2,592,384]{2,1,0:T(8,128)(2,1)}, bf16[2,512,384]{2,1,0:T(8,128)(2,1)}, bf16[2,512,384]{2,1,0:T(8,128)(2,1)}, f32[2,384]{1,0:T(2,128)}, f32[3,2,128]{2,1,0:T(2,128)}) custom-call(s32[1]{0:T(128)} %bitcast.10.first, bf16[2,592,768]{2,1,0:T(8,128)(2,1)} %get-tuple-element.175.q, bf16[2,512,768]{2,1,0:T(8,128)(2,1)} %get-tuple-element.161.k_in.k, ...), custom_call_target="tpu_custom_call" | custom-call | tf_op jit(solution)/shard_map/attention_backward/pallas_call | solution.py:413
  159.6 1.6 copy-done.1
  161.2 4.7 %first_sums.2 = (bf16[4,2,24,1920]{3,2,1,0:T(8,128)(2,1)}, bf16[4,2,24,1920]{3,2,1,0:T(8,128)(2,1)}, bf16[4,2,24,1920]{3,2,1,0:T(8,128)(2,1)}, bf16[4,2,24,1920]{3,2,1,0:T(8,128)(2,1)}) custom-call(s32[2]{0:T(128)} %pad_add_fusion.bits, bf16[4,2,2,48,1920]{4,3,2,1,0:T(8,128)(2,1)} %bitcast.48, bf16[4,2,2,48,1920]{4,3,2,1,0:T(8,128)(2,1)} %bitcast.49), custom_call_target="tpu_custom_call" | custom-call | tf_op jit(solution)/shard_map/first_sums/pallas_call | solution.py:926
  165.9 6.1 %grad_before.2 = bf16[768,1152]{1,0:T(8,128)(2,1)} custom-call(bf16[2,512,768]{2,1,0:T(8,128)(2,1)} %xc.7, bf16[2,80,768]{2,1,0:T(8,128)(2,1)} %get-tuple-element.315.xq, bf16[2,592,384]{2,1,0:T(8,128)(2,1)} %get-tuple-element.194.dq.dq_o, bf16[2,512,384]{2,1,0:T(8,128)(2,1)} %get-tuple-element.195.dk.dk_o, bf16[2,512,384]{2,1,0:T(8,128)(2,1)} %get-tuple-element.196.dv.dv_o), custom_call_target="tpu_custom_call" | custom-call | tf_op jit(solution)/shard_map/grad_before/pallas_call | solution.py:807
  172.1 2.2 collective-permute-start.1
  174.2 2.0 collective-permute-start.2
  176.2 15.6 %attention_backward.3 = (bf16[2,592,384]{2,1,0:T(8,128)(2,1)}, bf16[2,512,384]{2,1,0:T(8,128)(2,1)}, bf16[2,512,384]{2,1,0:T(8,128)(2,1)}, f32[2,384]{1,0:T(2,128)}, f32[3,2,128]{2,1,0:T(2,128)}) custom-call(s32[1]{0:T(128)} %bitcast.7.half.first.core, bf16[2,592,768]{2,1,0:T(8,128)(2,1)} %get-tuple-element.175.q, ...), custom_call_target="tpu_custom_call" | custom-call | tf_op jit(solution)/shard_map/attention_backward/pallas_call | solution.py:413
  191.8 7.5 %collective-permute-done.2.got_b = bf16[4,2,24,1920]{3,2,1,0:T(8,128)(2,1)S(1)} collective-permute-done((bf16[4,2,24,1920]{3,2,1,0:T(8,128)(2,1)}, bf16[4,2,24,1920]{3,2,1,0:T(8,128)(2,1)S(1)}, u32[]{:S(2)}, u32[]{:S(2)}) %collective-permute-start.2) | collective-permute-done | bytes 737312 | tf_op jit(solution)/shard_map/ppermute | solution.py:865
  199.3 0.9 copy-done.9
  200.2 3.1 %second_sums.2 = (bf16[4,24,1920]{2,1,0:T(8,128)(2,1)}, bf16[4,24,1920]{2,1,0:T(8,128)(2,1)}, bf16[4,24,1920]{2,1,0:T(8,128)(2,1)}, bf16[4,24,1920]{2,1,0:T(8,128)(2,1)}) custom-call(s32[2]{0:T(128)} %pad_add_fusion.bits, bf16[4,2,24,1920]{3,2,1,0:T(8,128)(2,1)} %get-tuple-element.185.keep_a, bf16[4,2,24,1920]{3,2,1,0:T(8,128)(2,1)} %get-tuple-element.186.keep_b, ...), custom_call_target="tpu_custom_call" | custom-call | tf_op jit(solution)/shard_map/second_sums/pallas_call | solution.py:926
  203.3 1.5 copy.51
  205.2 1.2 collective-permute-start.4
  206.4 1.0 collective-permute-start.5
  207.9 0.7 reduce.3
  209.0 0.8 pad.4.rest_0_
  209.8 6.7 %grad_before.3 = bf16[768,1280]{1,0:T(8,128)(2,1)} custom-call(bf16[2,512,768]{2,1,0:T(8,128)(2,1)} %xc.7, bf16[2,80,768]{2,1,0:T(8,128)(2,1)} %get-tuple-element.315.xq, bf16[2,592,384]{2,1,0:T(8,128)(2,1)} %get-tuple-element.214.dq.dq_m, bf16[2,512,384]{2,1,0:T(8,128)(2,1)} %get-tuple-element.215.dk.dk_m, bf16[2,512,384]{2,1,0:T(8,128)(2,1)} %get-tuple-element.216.dv.dv_m, ...), custom_call_target="tpu_custom_call" | custom-call | tf_op jit(solution)/shard_map/grad_before/pallas_call | solution.py:807
  217.0 3.1 %first_sums.3 = (bf16[4,2,24,1280]{3,2,1,0:T(8,128)(2,1)}, bf16[4,2,24,1280]{3,2,1,0:T(8,128)(2,1)}, bf16[4,2,24,1280]{3,2,1,0:T(8,128)(2,1)}, bf16[4,2,24,1280]{3,2,1,0:T(8,128)(2,1)}) custom-call(s32[2]{0:T(128)} %pad_add_fusion.bits, bf16[4,2,2,48,1280]{4,3,2,1,0:T(8,128)(2,1)} %bitcast.47), custom_call_target="tpu_custom_call" | custom-call | tf_op jit(solution)/shard_map/first_sums/pallas_call | solution.py:926
  220.2 2.4 third_sums.2
  222.5 5.0 %all-to-all-start.1 = ((bf16[4,48,1920]{2,1,0:T(8,128)(2,1)}), bf16[4,48,1920]{2,1,0:T(8,128)(2,1)S(1)}, u32[]{:S(2)}, u32[]{:S(2)}) async-start(bf16[4,48,1920]{2,1,0:T(8,128)(2,1)} %third_sums.2), calls=%async_computation.2 | async-start | bytes 1474560 | tf_op jit(solution)/shard_map/all_to_all | solution.py:979
  227.6 1.2 collective-permute-start.7
  228.7 0.9 collective-permute-start.8
  229.8 9.5 %input_grad.1 = (f32[2,512,768]{2,1,0:T(8,128)}, bf16[2,80,768]{2,1,0:T(8,128)(2,1)}) custom-call(s32[1]{0:T(128)} %bitcast.7.half.first.core, f32[2,512,768]{2,1,0:T(8,128)} %get-tuple-element.237.first_c, f32[2,80,768]{2,1,0:T(8,128)} %get-tuple-element.238.first_q, bf16[2,592,384]{2,1,0:T(8,128)(2,1)} %get-tuple-element.194.dq.dq_o, ...), custom_call_target="tpu_custom_call" | custom-call | tf_op jit(solution)/shard_map/input_grad/pallas_call | solution.py:847
  239.5 0.9 collective-permute-done.7.got_a
  241.8 2.6 second_sums.3
  244.4 1.2 collective-permute-start.9
  245.6 0.8 collective-permute-start.10
  247.3 3.5 %collective-permute-done.9.got_a = bf16[4,24,1280]{2,1,0:T(8,128)(2,1)S(1)} collective-permute-done((bf16[4,24,1280]{2,1,0:T(8,128)(2,1)}, bf16[4,24,1280]{2,1,0:T(8,128)(2,1)S(1)}, u32[]{:S(2)}, u32[]{:S(2)}) %collective-permute-start.9) | collective-permute-done | bytes 245792 | tf_op jit(solution)/shard_map/ppermute | solution.py:865
  250.8 1.2 collective-permute-done.10.got_b
  252.0 0.7 copy-done.19
  252.7 2.2 third_sums.3
  254.9 0.9 copy-done
  255.8 1.9 part_sums.2
  257.7 4.9 %all-to-all-start.2 = ((bf16[4,48,1280]{2,1,0:T(8,128)(2,1)}), bf16[4,48,1280]{2,1,0:T(8,128)(2,1)S(1)}, u32[]{:S(2)}, u32[]{:S(2)}) async-start(bf16[4,48,1280]{2,1,0:T(8,128)(2,1)} %third_sums.3), calls=%async_computation.3 | async-start | bytes 983040 | tf_op jit(solution)/shard_map/all_to_all | solution.py:979
  262.6 0.8 collective-permute-start.12
  263.4 1.3 collective-permute-start.11
  264.6 0.8 collective-permute-start.14
  265.4 1.1 collective-permute-start.15
  266.5 9.6 %collective-permute-done.14 = bf16[2,20,1536]{2,0,1:T(2,128)(2,1)S(1)} collective-permute-done((bf16[2,20,1536]{2,0,1:T(2,128)(2,1)S(1)}, bf16[2,20,1536]{2,0,1:T(2,128)(2,1)S(1)}, u32[]{:S(2)}, u32[]{:S(2)}) %collective-permute-start.14) | collective-permute-done | bytes 122912 | tf_op jit(solution)/shard_map/ppermute | solution.py:865
  276.2 0.8 copy-done.2
  276.9 1.7 part_sums.3
  278.9 0.7 copy-done.10
  279.6 0.9 collective-permute-start.16
  280.4 0.7 collective-permute-start.17
  281.1 0.9 pad_maximum_fusion.2
  283.0 2.6 collective-permute-done.16
  286.3 2.2 place_sums.3
  288.5 2.4 place_sums.4
  290.9 0.9 slice_convert_fusion
  291.8 0.7 copy-done.17
  292.5 2.0 place_sums.5
  294.5 1.4 fusion.9
  295.9 0.8 fusion.8
  (123 shorter events, 12.0 us)
Async XLA Ops:
  7.2 7.1 %copy-start.31 = (s32[8]{0:T(128)S(1)}, s32[8]{0:T(128)}, u32[]{:S(2)}) copy-start(s32[8]{0:T(128)} %param.20) | copy-start | bytes 100
  7.2 8.6 %copy-start.22 = (bf16[12,32]{1,0:T(8,128)(2,1)S(1)}, bf16[12,32]{1,0:T(8,128)(2,1)}, u32[]{:S(2)}) copy-start(bf16[12,32]{1,0:T(8,128)(2,1)} %param.33) | copy-start | bytes 2308
  7.2 9.2 %copy-start.26 = (bf16[3072]{0:T(1024)(128)(2,1)S(1)}, bf16[3072]{0:T(1024)(128)(2,1)}, u32[]{:S(2)}) copy-start(bf16[3072]{0:T(1024)(128)(2,1)} %param.30) | copy-start | bytes 18436
  10.1 16.8 %all-to-all-start = ((bf16[8,20,1536]{2,1,0:T(8,128)(2,1)}), bf16[8,20,1536]{2,1,0:T(8,128)(2,1)S(1)}, u32[]{:S(2)}, u32[]{:S(2)}) async-start(bf16[8,20,1536]{2,1,0:T(8,128)(2,1)} %pad_maximum_fusion), calls=%async_computation | async-start | bytes 1179648 | tf_op jit(solution)/shard_map/all_to_all | solution.py:1071
  14.3 189.0 %reduce-scatter.2.cloned.1.call-start = ((), (), s32[]{:S(2)}) async-start(), calls=%async_computation.4 | async-start | bytes 5308416 | tf_op jit(solution)/shard_map/reduce_scatter | solution.py:1115
  142.6 16.9 %collective-permute-start = (bf16[768,1920]{1,0:T(8,128)(2,1)}, bf16[768,1920]{1,0:T(8,128)(2,1)S(1)}, u32[]{:S(2)}, u32[]{:S(2)}) collective-permute-start(bf16[768,1920]{1,0:T(8,128)(2,1)} %get-tuple-element.174), channel_id=1, source_target_pairs={{0,1},{1,0},{2,3},{3,2},{4,5},{5,4},{6,7},{7,6},{8,9},{9,8},{10,11... | collective-permute-start | bytes 8847368 | tf_op jit(solution)/shard_map/ppermute | solution.py:865
  159.6 1.6 copy-start.1
  165.9 10.3 %copy-start.25 = (f32[3,768]{1,0:T(4,128)S(1)}, f32[3,768]{1,0:T(4,128)}, u32[]{:S(2)}) copy-start(f32[3,768]{1,0:T(4,128)} %get-tuple-element.220) | copy-start | bytes 27652
  172.0 27.3 %collective-permute-start.3 = (bf16[768,1152]{1,0:T(8,128)(2,1)}, bf16[768,1152]{1,0:T(8,128)(2,1)S(1)}, u32[]{:S(2)}, u32[]{:S(2)}) collective-permute-start(bf16[768,1152]{1,0:T(8,128)(2,1)} %grad_before.2), channel_id=1, source_target_pairs={{0,1},{1,0},{2,3},{3,2},{4,5},{5,4},{6,7},{7,6},{8,9},{9,8},{10,11... | collective-permute-start | bytes 5308424 | tf_op jit(solution)/shard_map/ppermute | solution.py:865
  172.1 19.7 %collective-permute-start.1 = (bf16[4,2,24,1920]{3,2,1,0:T(8,128)(2,1)}, bf16[4,2,24,1920]{3,2,1,0:T(8,128)(2,1)S(1)}, u32[]{:S(2)}, u32[]{:S(2)}) collective-permute-start(bf16[4,2,24,1920]{3,2,1,0:T(8,128)(2,1)} %get-tuple-element.192), channel_id=1, source_target_pairs={{0,2},{1,3},{2,0},{3,1},{4,6},{5,7},{6,4},{7,5},{8,10},{9,11},{10,... | collective-permute-start | bytes 2211848 | tf_op jit(solution)/shard_map/ppermute | solution.py:865
  174.2 25.1 %collective-permute-start.2 = (bf16[4,2,24,1920]{3,2,1,0:T(8,128)(2,1)}, bf16[4,2,24,1920]{3,2,1,0:T(8,128)(2,1)S(1)}, u32[]{:S(2)}, u32[]{:S(2)}) collective-permute-start(bf16[4,2,24,1920]{3,2,1,0:T(8,128)(2,1)} %get-tuple-element.193), channel_id=1, source_target_pairs={{0,4},{4,0},{8,12},{12,8},{16,20},{20,16},{24,28},{28,24},{1,5},{5... | collective-permute-start | bytes 2211848 | tf_op jit(solution)/shard_map/ppermute | solution.py:865
  191.8 7.5 %copy-start.8 = (bf16[4,2,24,1920]{3,2,1,0:T(8,128)(2,1)}, bf16[4,2,24,1920]{3,2,1,0:T(8,128)(2,1)S(1)}, u32[]{:S(2)}) copy-start(bf16[4,2,24,1920]{3,2,1,0:T(8,128)(2,1)S(1)} %collective-permute-done.1.got_a) | copy-start | bytes 2211844
  199.3 0.9 copy-start.9
  199.3 5.5 %copy-start.3 = (bf16[768,1152]{1,0:T(8,128)(2,1)}, bf16[768,1152]{1,0:T(8,128)(2,1)S(1)}, u32[]{:S(2)}) copy-start(bf16[768,1152]{1,0:T(8,128)(2,1)S(1)} %collective-permute-done.3.rest_1_) | copy-start | bytes 5308420
  203.2 3.1 %copy-start.32 = (bf16[4,24,1920]{2,1,0:T(8,128)(2,1)S(1)}, bf16[4,24,1920]{2,1,0:T(8,128)(2,1)}, u32[]{:S(2)}) copy-start(bf16[4,24,1920]{2,1,0:T(8,128)(2,1)} %get-tuple-element.212) | copy-start | bytes 1105924
  203.3 4.1 %copy-start.24 = (f32[3,768]{1,0:T(4,128)S(1)}, f32[3,768]{1,0:T(4,128)}, u32[]{:S(2)}) copy-start(f32[3,768]{1,0:T(4,128)} %get-tuple-element.219) | copy-start | bytes 27652
  203.3 4.6 %copy-start.23 = (f32[1,3072]{1,0:T(1,128)S(1)}, f32[1,3072]{1,0:T(1,128)}, u32[]{:S(2)}) copy-start(f32[1,3072]{1,0:T(1,128)} %get-tuple-element.221) | copy-start | bytes 36868
  203.3 5.5 %copy-start.28 = (f32[3,2,128]{2,1,0:T(2,128)S(1)}, f32[3,2,128]{2,1,0:T(2,128)}, u32[]{:S(2)}) copy-start(f32[3,2,128]{2,1,0:T(2,128)} %get-tuple-element.223) | copy-start | bytes 9220
  203.3 5.5 %copy-start.30 = (f32[3,2,128]{2,1,0:T(2,128)S(1)}, f32[3,2,128]{2,1,0:T(2,128)}, u32[]{:S(2)}) copy-start(f32[3,2,128]{2,1,0:T(2,128)} %get-tuple-element.222) | copy-start | bytes 9220
  203.3 5.7 %copy-start.27 = (f32[2,384]{1,0:T(2,128)S(1)}, f32[2,384]{1,0:T(2,128)}, u32[]{:S(2)}) copy-start(f32[2,384]{1,0:T(2,128)} %get-tuple-element.218) | copy-start | bytes 9220
  203.3 5.6 %copy-start.29 = (f32[2,384]{1,0:T(2,128)S(1)}, f32[2,384]{1,0:T(2,128)}, u32[]{:S(2)}) copy-start(f32[2,384]{1,0:T(2,128)} %get-tuple-element.217) | copy-start | bytes 9220
  205.1 11.5 %collective-permute-start.6 = (bf16[384,384]{1,0:T(8,128)(2,1)S(1)}, bf16[384,384]{1,0:T(8,128)(2,1)S(1)}, u32[]{:S(2)}, u32[]{:S(2)}) collective-permute-start(bf16[384,384]{1,0:T(8,128)(2,1)S(1)} %bitcast.55), channel_id=1, source_target_pairs={{0,1},{1,0},{2,3},{3,2},{4,5},{5,4},{6,7},{7,6},{8,9},{9,8},{10,11... | collective-permute-start | bytes 884744 | tf_op jit(solution)/shard_map/ppermute | solution.py:865
  205.2 11.4 %collective-permute-start.4 = (bf16[4,24,1920]{2,1,0:T(8,128)(2,1)}, bf16[4,24,1920]{2,1,0:T(8,128)(2,1)S(1)}, u32[]{:S(2)}, u32[]{:S(2)}) collective-permute-start(bf16[4,24,1920]{2,1,0:T(8,128)(2,1)} %get-tuple-element.211), channel_id=1, source_target_pairs={{0,4},{4,0},{8,12},{12,8},{16,20},{20,16},{24,28},{28,24},{1,5},{5... | collective-permute-start | bytes 1105928 | tf_op jit(solution)/shard_map/ppermute | solution.py:865
  206.4 10.7 %collective-permute-start.5 = (bf16[4,24,1920]{2,1,0:T(8,128)(2,1)S(1)}, bf16[4,24,1920]{2,1,0:T(8,128)(2,1)S(1)}, u32[]{:S(2)}, u32[]{:S(2)}) collective-permute-start(bf16[4,24,1920]{2,1,0:T(8,128)(2,1)S(1)} %copy-done.32), channel_id=1, source_target_pairs={{0,2},{1,3},{2,0},{3,1},{4,6},{5,7},{6,4},{7,5},{8,10},{9,11},{10,... | collective-permute-start | bytes 1105928 | tf_op jit(solution)/shard_map/ppermute | solution.py:865
  216.6 3.6 %copy-start.13 = (bf16[4,24,1920]{2,1,0:T(8,128)(2,1)}, bf16[4,24,1920]{2,1,0:T(8,128)(2,1)S(1)}, u32[]{:S(2)}) copy-start(bf16[4,24,1920]{2,1,0:T(8,128)(2,1)S(1)} %collective-permute-done.4.got_a) | copy-start | bytes 1105924
  217.0 3.1 %copy-start.14 = (bf16[4,24,1920]{2,1,0:T(8,128)(2,1)}, bf16[4,24,1920]{2,1,0:T(8,128)(2,1)S(1)}, u32[]{:S(2)}) copy-start(bf16[4,24,1920]{2,1,0:T(8,128)(2,1)S(1)} %collective-permute-done.5.got_b) | copy-start | bytes 1105924
  222.5 32.4 %all-to-all-start.1 = ((bf16[4,48,1920]{2,1,0:T(8,128)(2,1)}), bf16[4,48,1920]{2,1,0:T(8,128)(2,1)S(1)}, u32[]{:S(2)}, u32[]{:S(2)}) async-start(bf16[4,48,1920]{2,1,0:T(8,128)(2,1)} %third_sums.2), calls=%async_computation.2 | async-start | bytes 1474560 | tf_op jit(solution)/shard_map/all_to_all | solution.py:979
  227.6 12.8 %collective-permute-start.7 = (bf16[4,2,24,1280]{3,2,1,0:T(8,128)(2,1)}, bf16[4,2,24,1280]{3,2,1,0:T(8,128)(2,1)S(1)}, u32[]{:S(2)}, u32[]{:S(2)}) collective-permute-start(bf16[4,2,24,1280]{3,2,1,0:T(8,128)(2,1)} %get-tuple-element.235), channel_id=1, source_target_pairs={{0,2},{1,3},{2,0},{3,1},{4,6},{5,7},{6,4},{7,5},{8,10},{9,11},{10,... | collective-permute-start | bytes 1474568 | tf_op jit(solution)/shard_map/ppermute | solution.py:865
  228.7 12.3 %collective-permute-start.8 = (bf16[4,2,24,1280]{3,2,1,0:T(8,128)(2,1)}, bf16[4,2,24,1280]{3,2,1,0:T(8,128)(2,1)S(1)}, u32[]{:S(2)}, u32[]{:S(2)}) collective-permute-start(bf16[4,2,24,1280]{3,2,1,0:T(8,128)(2,1)} %get-tuple-element.236), channel_id=1, source_target_pairs={{0,4},{4,0},{8,12},{12,8},{16,20},{20,16},{24,28},{28,24},{1,5},{5... | collective-permute-start | bytes 1474568 | tf_op jit(solution)/shard_map/ppermute | solution.py:865
  239.4 7.0 %copy-start.20 = (bf16[2,80,768]{2,1,0:T(8,128)(2,1)S(1)}, bf16[2,80,768]{2,1,0:T(8,128)(2,1)}, u32[]{:S(2)}) copy-start(bf16[2,80,768]{2,1,0:T(8,128)(2,1)} %get-tuple-element.251) | copy-start | bytes 737284
  239.4 7.0 %copy-start.21 = (bf16[2,80,768]{2,1,0:T(8,128)(2,1)S(1)}, bf16[2,80,768]{2,1,0:T(8,128)(2,1)}, u32[]{:S(2)}) copy-start(bf16[2,80,768]{2,1,0:T(8,128)(2,1)} %get-tuple-element.252) | copy-start | bytes 737284
  240.4 0.8 copy-start.11
  241.0 0.8 copy-start.12
  244.4 6.4 %collective-permute-start.9 = (bf16[4,24,1280]{2,1,0:T(8,128)(2,1)}, bf16[4,24,1280]{2,1,0:T(8,128)(2,1)S(1)}, u32[]{:S(2)}, u32[]{:S(2)}) collective-permute-start(bf16[4,24,1280]{2,1,0:T(8,128)(2,1)} %get-tuple-element.249), channel_id=1, source_target_pairs={{0,4},{4,0},{8,12},{12,8},{16,20},{20,16},{24,28},{28,24},{1,5},{5... | collective-permute-start | bytes 737288 | tf_op jit(solution)/shard_map/ppermute | solution.py:865
  245.6 6.4 %collective-permute-start.10 = (bf16[4,24,1280]{2,1,0:T(8,128)(2,1)}, bf16[4,24,1280]{2,1,0:T(8,128)(2,1)S(1)}, u32[]{:S(2)}, u32[]{:S(2)}) collective-permute-start(bf16[4,24,1280]{2,1,0:T(8,128)(2,1)} %get-tuple-element.250), channel_id=1, source_target_pairs={{0,2},{1,3},{2,0},{3,1},{4,6},{5,7},{6,4},{7,5},{8,10},{9,11},{10,... | collective-permute-start | bytes 737288 | tf_op jit(solution)/shard_map/ppermute | solution.py:865
  250.8 1.2 copy-start.18
  252.0 0.7 copy-start.19
  254.9 0.9 copy-start
  257.7 21.1 %copy-start.7 = (bf16[48,1920]{1,0:T(8,128)(2,1)S(1)}, bf16[48,1920]{1,0:T(8,128)(2,1)}, u32[]{:S(2)}) copy-start(bf16[48,1920]{1,0:T(8,128)(2,1)} %part_sums.2) | copy-start | bytes 552964
  257.7 18.5 %all-to-all-start.2 = ((bf16[4,48,1280]{2,1,0:T(8,128)(2,1)}), bf16[4,48,1280]{2,1,0:T(8,128)(2,1)S(1)}, u32[]{:S(2)}, u32[]{:S(2)}) async-start(bf16[4,48,1280]{2,1,0:T(8,128)(2,1)} %third_sums.3), calls=%async_computation.3 | async-start | bytes 983040 | tf_op jit(solution)/shard_map/all_to_all | solution.py:979
  262.6 13.5 %collective-permute-start.12 = (bf16[384,384]{1,0:T(8,128)(2,1)S(1)}, bf16[384,384]{1,0:T(8,128)(2,1)S(1)}, u32[]{:S(2)}, u32[]{:S(2)}) collective-permute-start(bf16[384,384]{1,0:T(8,128)(2,1)S(1)} %fusion), channel_id=1, source_target_pairs={{0,2},{1,3},{2,0},{3,1},{4,6},{5,7},{6,4},{7,5},{8,10},{9,11},{10,... | collective-permute-start | bytes 884744 | tf_op jit(solution)/shard_map/ppermute | solution.py:865
  263.4 12.8 %collective-permute-start.11 = (bf16[48,1920]{1,0:T(8,128)(2,1)}, bf16[48,1920]{1,0:T(8,128)(2,1)S(1)}, u32[]{:S(2)}, u32[]{:S(2)}) collective-permute-start(bf16[48,1920]{1,0:T(8,128)(2,1)} %part_sums.2), channel_id=1, source_target_pairs={{0,2},{1,3},{2,0},{3,1},{4,6},{5,7},{6,4},{7,5},{8,10},{9,11},{10,... | collective-permute-start | bytes 552968 | tf_op jit(solution)/shard_map/ppermute | solution.py:865
  264.6 1.9 collective-permute-start.13
  264.6 11.5 %collective-permute-start.14 = (bf16[2,20,1536]{2,0,1:T(2,128)(2,1)S(1)}, bf16[2,20,1536]{2,0,1:T(2,128)(2,1)S(1)}, u32[]{:S(2)}, u32[]{:S(2)}) collective-permute-start(bf16[2,20,1536]{2,0,1:T(2,128)(2,1)S(1)} %get-tuple-element.265), channel_id=1, source_target_pairs={{0,2},{1,3},{2,0},{3,1},{4,6},{5,7},{6,4},{7,5},{8,10},{9,11},{10,... | collective-permute-start | bytes 368648 | tf_op jit(solution)/shard_map/ppermute | solution.py:865
  265.4 10.7 %collective-permute-start.15 = (bf16[2,20,1536]{2,0,1:T(2,128)(2,1)S(1)}, bf16[2,20,1536]{2,0,1:T(2,128)(2,1)S(1)}, u32[]{:S(2)}, u32[]{:S(2)}) collective-permute-start(bf16[2,20,1536]{2,0,1:T(2,128)(2,1)S(1)} %get-tuple-element.266), channel_id=1, source_target_pairs={{0,3},{1,2},{2,1},{3,0},{4,7},{5,6},{6,5},{7,4},{8,11},{9,10},{10,... | collective-permute-start | bytes 368648 | tf_op jit(solution)/shard_map/ppermute | solution.py:865
  276.2 0.8 copy-start.2
  278.7 0.9 copy-start.10
  278.8 4.2 %copy-start.5 = (bf16[384,384]{1,0:T(8,128)(2,1)}, bf16[384,384]{1,0:T(8,128)(2,1)S(1)}, u32[]{:S(2)}) copy-start(bf16[384,384]{1,0:T(8,128)(2,1)S(1)} %add_convert_fusion.own) | copy-start | bytes 884740
  279.6 6.1 %copy-start.4 = (bf16[96,1920]{1,0:T(8,128)(2,1)}, bf16[96,1920]{1,0:T(8,128)(2,1)S(1)}, u32[]{:S(2)}) copy-start(bf16[96,1920]{1,0:T(8,128)(2,1)S(1)} %pad_maximum_fusion.4.own) | copy-start | bytes 1105924
  279.6 6.0 %collective-permute-start.16 = (bf16[48,1280]{1,0:T(8,128)(2,1)S(1)}, bf16[48,1280]{1,0:T(8,128)(2,1)S(1)}, u32[]{:S(2)}, u32[]{:S(2)}) collective-permute-start(bf16[48,1280]{1,0:T(8,128)(2,1)S(1)} %copy-done.10), channel_id=1, source_target_pairs={{0,2},{1,3},{2,0},{3,1},{4,6},{5,7},{6,4},{7,5},{8,10},{9,11},{10,... | collective-permute-start | bytes 368648 | tf_op jit(solution)/shard_map/ppermute | solution.py:865
  280.4 5.2 %collective-permute-start.17 = (bf16[384,384]{1,0:T(8,128)(2,1)S(1)}, bf16[384,384]{1,0:T(8,128)(2,1)S(1)}, u32[]{:S(2)}, u32[]{:S(2)}) collective-permute-start(bf16[384,384]{1,0:T(8,128)(2,1)S(1)} %add_convert_fusion.own), channel_id=1, source_target_pairs={{0,1},{1,0},{2,3},{3,2},{4,5},{5,4},{6,7},{7,6},{8,9},{9,8},{10,11... | collective-permute-start | bytes 884744 | tf_op jit(solution)/shard_map/ppermute | solution.py:865
  281.1 4.5 %collective-permute-start.18 = (bf16[96,1920]{1,0:T(8,128)(2,1)S(1)}, bf16[96,1920]{1,0:T(8,128)(2,1)S(1)}, u32[]{:S(2)}, u32[]{:S(2)}) collective-permute-start(bf16[96,1920]{1,0:T(8,128)(2,1)S(1)} %pad_maximum_fusion.4.own), channel_id=1, source_target_pairs={{0,1},{1,0},{2,3},{3,2},{4,5},{5,4},{6,7},{7,6},{8,9},{9,8},{10,11... | collective-permute-start | bytes 1105928 | tf_op jit(solution)/shard_map/ppermute | solution.py:865
  285.6 0.7 copy-start.16
  285.6 2.9 copy-start.15
  285.7 6.1 %copy-start.6 = (bf16[96,1280]{1,0:T(8,128)(2,1)}, bf16[96,1280]{1,0:T(8,128)(2,1)S(1)}, u32[]{:S(2)}) copy-start(bf16[96,1280]{1,0:T(8,128)(2,1)S(1)} %pad_maximum_fusion.5.own) | copy-start | bytes 737284
  285.7 6.1 %collective-permute-start.19 = (bf16[96,1280]{1,0:T(8,128)(2,1)S(1)}, bf16[96,1280]{1,0:T(8,128)(2,1)S(1)}, u32[]{:S(2)}, u32[]{:S(2)}) collective-permute-start(bf16[96,1280]{1,0:T(8,128)(2,1)S(1)} %pad_maximum_fusion.5.own), channel_id=1, source_target_pairs={{0,1},{1,0},{2,3},{3,2},{4,5},{5,4},{6,7},{7,6},{8,9},{9,8},{10,11... | collective-permute-start | bytes 737288 | tf_op jit(solution)/shard_map/ppermute | solution.py:865
  291.8 0.7 copy-start.17
Sparse Core Ops, SparseCore 0:
  100.5 102.2 reduce-scatter.1

commit v3 on v2

--- a/solution.py
+++ b/solution.py
@@ -27,7 +27,7 @@
 BACK_STEP = 256
 SUB = 64
 CHUNK = 768
-GRAD_TILE = 512
+GRAD_TILE = 1024
 
 
 def nn(a, b):
@@ -535,13 +535,14 @@
         acc[...] = hidden + after_f[1:2]
         for n in range(wi.shape[1] // CHUNK):
             part = slice(n * CHUNK, (n + 1) * CHUNK)
-            ready(1 + 2 * n)
+            if n == 0:
+                for number in range(1, len(copies)):
+                    ready(number)
             u = nn(low, wi[:, part]) + hidden_bias[:, part].astype(F32)
             phi, density = normal_parts(u)
             active = (u * phi).astype(BF16)
             act[pl.ds(at, rows), part] = active
             slope_out[:, part] = (phi + u * density * INV_ROOT).astype(BF16)
-            ready(2 + 2 * n)
             acc[...] += nn(active, wu[part, :])
         unit2, scale2 = norm_parts(acc[...])
         out = (unit2 * gain_f[1:2] + shift_f[1:2]).astype(BF16)
@@ -601,13 +602,14 @@
         chunks = ff // CHUNK
         for n in range(chunks):
             part = slice(n * CHUNK, (n + 1) * CHUNK)
-            ready(2 * n)
+            if n % 2 == 0:
+                for number in range(2 * n, min(2 * n + 4, 2 * chunks)):
+                    ready(number)
             d_act = nt(outer[...], wu[part, :])
             d_inner = (d_act * slope[:, part].astype(F32)).astype(BF16)
             inner[pl.ds(at, rows), part] = d_inner
             term = column_sum(d_inner.astype(F32))
             inner_acc[:, part] += term
-            ready(2 * n + 1)
             acc[...] += nt(d_inner, wi[:, part])
         inner_sums[...] = jnp.sum(inner_acc[...], axis=0, keepdims=True)
         unit1 = unit[...].astype(F32)
@@ -1033,13 +1035,17 @@
             output[:, to : to + narrow] = half[:, at + wide : at + wide + narrow]
 
 
-def place_before_kernel(core, own, got, query, key, value, vectors):
+def place_before_kernel(core, own, got, query, key, value, *vectors):
     part = query.shape[1] // 2
     first, second = in_core_order(core[0] == 0, own, got)
     for n, ref in enumerate((query, key, value)):
         ref[:, :part] = first[:, n * part : (n + 1) * part]
         ref[:, part:] = second[:, n * part : (n + 1) * part]
-    vectors[...] = (first[:, 3 * part :] + second[:, 3 * part :]).T
+    every = (first[:, 3 * part :] + second[:, 3 * part :]).T
+    at = 0
+    for ref in vectors:
+        ref[...] = every[at : at + ref.shape[0]]
+        at += ref.shape[0]
 
 
 def place_sums(kernel, core, own, got, shapes):
@@ -1208,14 +1214,17 @@
         ),
         (got_o, got_i),
     )
-    g_query, g_key, g_value, vectors = place_sums(
-        place_before_kernel, mine, red_b.own, got_b, [(share, width)] * 3 + [(TILE, share)]
-    )
-    g_hidden = vectors[8 : 8 + ff // width].reshape(-1)
-    g_table = vectors[8 + ff // width :].reshape(-1)[: HEADS * BUCKETS].reshape(HEADS, BUCKETS)
+    pair = (2, share)
+    (
+        g_query, g_key, g_value, g_before, g_after, g_gain, g_shift, g_hidden, g_table,
+    ) = place_sums(
+        place_before_kernel, mine, red_b.own, got_b,
+        [(share, width)] * 3 + [pair] * 4
+        + [(ff // width, share), (HEADS * BUCKETS // share, share)],
+    )
     return (
         out_c, out_q, d_content, d_query, g_query, g_key, g_value, g_output, g_inner, g_outer,
-        vectors[0:2], vectors[2:4], g_hidden, vectors[4:6], vectors[6:8], g_table,
+        g_before, g_after, g_hidden.reshape(-1), g_gain, g_shift, g_table.reshape(HEADS, BUCKETS),
     )
 
 

time: 309 us -> 302 us (0.977)
  Pallas kernels: 204 us -> 194 us
    pallas_call x1, Pallas kernels: 47.8 us -> 41.6 us  [rows_forward(): pl.pallas_call(rows_forward_kernel, grid_spec=pltpu.PrefetchScalarGridSpe...]
    pallas_call x1, Pallas kernels: 42.3 us -> 38.6 us  [rows_backward(): pl.pallas_call(rows_backward_kernel, grid_spec=pltpu.PrefetchScalarGridSp...]
    reduce_scatter x1, waiting for transfers between devices: 0.02 us -> 3.26 us  [over_tok(): return lax.psum_scatter(a, 'tok', scatter_dimension=0, tiled=True)]
  transfers between devices with their start and end apart: 24 -> 24, of which waited for: 8 -> 9; matrix products, arithmetic and copies ran while one was open for 4% -> 4% of each run, Pallas kernels for 39% -> 39%
where the time goes in v3:
time: 302 us; the launch traced here: 297 us
  Pallas kernels  194 us (64%)
  starting transfers between devices  30.9 us (10%)
  waiting for transfers between devices  28.9 us (10%)
  local copies, waits for them, and re-layouts  21.1 us (7%)
  between operations  14.7 us (5%)
  other arithmetic  6.97 us (2%)
    pallas_call x1, Pallas kernels, rows_forward(): pl.pallas_call(rows_forward_kernel, grid_spec=pltpu.PrefetchScalarGridSpe...  41.6 us
    pallas_call x1, Pallas kernels, rows_backward(): pl.pallas_call(rows_backward_kernel, grid_spec=pltpu.PrefetchScalarGridSp...  38.6 us
    pallas_call x2, Pallas kernels, attention_backward(): pl.pallas_call(attention_backward_kernel, grid_spec=pltpu.PrefetchScalarG...  31.5 us
    ppermute x20, waiting for transfers between devices, swap(): return lax.ppermute(value, axis, [(i, i ^ stride) for i in range(count)])  25.6 us
    pallas_call x1, Pallas kernels, attention_forward(): pl.pallas_call(attention_forward_kernel, grid=(seqs, PAIRS), in_specs=[by...  24.4 us
    pallas_call x6, Pallas kernels, staged(): pl.pallas_call(kernel, in_specs=[pl.BlockSpec(memory_space=pltpu.SMEM)] +...  18.3 us
    ppermute x20, starting transfers between devices, swap(): return lax.ppermute(value, axis, [(i, i ^ stride) for i in range(count)])  18.2 us
    pallas_call x2, Pallas kernels, grad_before(): pl.pallas_call(grad_before_kernel, grid=(2,), in_specs=[pl.BlockSpec((seq...  12.8 us
  transfers between devices with their start and end apart: 24, of which 9 were waited for; matrix products, arithmetic and copies ran while one was open for 4% of the time, Pallas kernels for 39%

profile of v3, /device:TPU:0, one launch (start us, length us, event | category | flops | bytes accessed | tf_op | source)
XLA Modules:
  0.0 297.0 jit_solution(539621831354048805)
XLA Ops:
  7.2 1.0 copy.45
  8.2 1.0 copy.46
  9.2 0.9 pad_maximum_fusion
  10.1 4.2 %all-to-all-start = ((bf16[8,20,1536]{2,1,0:T(8,128)(2,1)}), bf16[8,20,1536]{2,1,0:T(8,128)(2,1)S(1)}, u32[]{:S(2)}, u32[]{:S(2)}) async-start(bf16[8,20,1536]{2,1,0:T(8,128)(2,1)} %pad_maximum_fusion), calls=%async_computation | async-start | bytes 1179648 | tf_op jit(solution)/shard_map/all_to_all | solution.py:1077
  14.4 0.8 maximum_bitcast_fusion
  17.8 1.0 copy.49.thr_c
  18.8 7.3 %project.1 = (bf16[2,512,768]{2,1,0:T(8,128)(2,1)}, bf16[2,512,768]{2,1,0:T(8,128)(2,1)}, bf16[2,512,768]{2,1,0:T(8,128)(2,1)}) custom-call(bf16[2,512,768]{2,1,0:T(8,128)(2,1)} %xc.7, bf16[768,768]{1,0:T(8,128)(2,1)} %wq_m.1, bf16[768,768]{1,0:T(8,128)(2,1)} %wk_m.1, bf16[768,768]{1,0:T(8,128)(2,1)} %wv_m.1, bf16[2,768]{1,0:T(2,128)(2,1)} %before.3), custom_call_target="tpu_custom_call" | custom-call | tf_op jit(solution)/shard_map/project/pallas_call | solution.py:99
  26.1 0.7 iota_add_fusion.thr_q
  27.3 0.8 fusion.7
  28.1 24.4 %attention_forward.1 = (bf16[2,592,768]{2,1,0:T(8,128)(2,1)}, bf16[2,12,592,512]{3,2,1,0:T(8,128)(2,1)}, f32[2,592,768]{2,1,0:T(8,128)}, bf16[2,592,768]{2,1,0:T(8,128)(2,1)}) custom-call(bf16[2,512,768]{2,1,0:T(8,128)(2,1)} %get-tuple-element.165.q_in, bf16[2,512,768]{2,1,0:T(8,128)(2,1)} %get-tuple-element.166.k_in.k, ...), custom_call_target="tpu_custom_call" | custom-call | tf_op jit(solution)/shard_map/attention_forward/pallas_call | solution.py:219
  52.5 41.6 %rows_forward.1 = (bf16[2,512,768]{2,1,0:T(8,128)(2,1)}, bf16[2,80,768]{2,1,0:T(8,128)(2,1)}, bf16[1184,3072]{1,0:T(8,128)(2,1)}, bf16[1184,768]{1,0:T(8,128)(2,...) custom-call(bf16[2,592,768]{2,1,0:T(8,128)(2,1)} %get-tuple-element., ...), custom_call_target="tpu_custom_call" | custom-call | tf_op jit(solution)/shard_map/rows_forward/pallas_call | solution.py:680
  94.2 38.6 %rows_backward.1 = (f32[2,512,768]{2,1,0:T(8,128)}, f32[2,80,768]{2,1,0:T(8,128)}, bf16[2,592,768]{2,1,0:T(8,128)(2,1)}, f32[3,768]{1,0:T(4,128)}, f32[1,3072]{1...) custom-call(s32[1]{0:T(128)} %bitcast.7.half.first.core, bf16[1184,768]{1,0:T(8,128)(2,1)} %get-tuple-element.171.outer, ...), custom_call_target="tpu_custom_call" | custom-call | tf_op jit(solution)/shard_map/rows_backward/pallas_call | solution.py:737
  133.9 16.0 %attention_backward.2 = (bf16[2,592,384]{2,1,0:T(8,128)(2,1)}, bf16[2,512,384]{2,1,0:T(8,128)(2,1)}, bf16[2,512,384]{2,1,0:T(8,128)(2,1)}, f32[2,384]{1,0:T(2,128)}, f32[3,2,128]{2,1,0:T(2,128)}) custom-call(s32[1]{0:T(128)} %bitcast.10.first, bf16[2,592,768]{2,1,0:T(8,128)(2,1)} %get-tuple-element.180.q, bf16[2,512,768]{2,1,0:T(8,128)(2,1)} %get-tuple-element.166.k_in.k, ...), custom_call_target="tpu_custom_call" | custom-call | tf_op jit(solution)/shard_map/attention_backward/pallas_call | solution.py:413
  149.9 1.6 copy-done.1
  151.5 4.8 %first_sums.2 = (bf16[4,2,24,1920]{3,2,1,0:T(8,128)(2,1)}, bf16[4,2,24,1920]{3,2,1,0:T(8,128)(2,1)}, bf16[4,2,24,1920]{3,2,1,0:T(8,128)(2,1)}, bf16[4,2,24,1920]{3,2,1,0:T(8,128)(2,1)}) custom-call(s32[2]{0:T(128)} %pad_add_fusion.bits, bf16[4,2,2,48,1920]{4,3,2,1,0:T(8,128)(2,1)} %bitcast.48, bf16[4,2,2,48,1920]{4,3,2,1,0:T(8,128)(2,1)} %bitcast.49), custom_call_target="tpu_custom_call" | custom-call | tf_op jit(solution)/shard_map/first_sums/pallas_call | solution.py:928
  156.3 6.0 %grad_before.2 = bf16[768,1152]{1,0:T(8,128)(2,1)} custom-call(bf16[2,512,768]{2,1,0:T(8,128)(2,1)} %xc.7, bf16[2,80,768]{2,1,0:T(8,128)(2,1)} %get-tuple-element.325.xq, bf16[2,592,384]{2,1,0:T(8,128)(2,1)} %get-tuple-element.199.dq.dq_o, bf16[2,512,384]{2,1,0:T(8,128)(2,1)} %get-tuple-element.200.dk.dk_o, bf16[2,512,384]{2,1,0:T(8,128)(2,1)} %get-tuple-element.201.dv.dv_o), custom_call_target="tpu_custom_call" | custom-call | tf_op jit(solution)/shard_map/grad_before/pallas_call | solution.py:809
  162.4 2.2 collective-permute-start.1
  164.6 1.9 collective-permute-start.2
  166.5 15.5 %attention_backward.3 = (bf16[2,592,384]{2,1,0:T(8,128)(2,1)}, bf16[2,512,384]{2,1,0:T(8,128)(2,1)}, bf16[2,512,384]{2,1,0:T(8,128)(2,1)}, f32[2,384]{1,0:T(2,128)}, f32[3,2,128]{2,1,0:T(2,128)}) custom-call(s32[1]{0:T(128)} %bitcast.7.half.first.core, bf16[2,592,768]{2,1,0:T(8,128)(2,1)} %get-tuple-element.180.q, ...), custom_call_target="tpu_custom_call" | custom-call | tf_op jit(solution)/shard_map/attention_backward/pallas_call | solution.py:413
  182.1 7.6 %collective-permute-done.2.got_b = bf16[4,2,24,1920]{3,2,1,0:T(8,128)(2,1)S(1)} collective-permute-done((bf16[4,2,24,1920]{3,2,1,0:T(8,128)(2,1)}, bf16[4,2,24,1920]{3,2,1,0:T(8,128)(2,1)S(1)}, u32[]{:S(2)}, u32[]{:S(2)}) %collective-permute-start.2) | collective-permute-done | bytes 737312 | tf_op jit(solution)/shard_map/ppermute | solution.py:867
  189.7 0.9 copy-done.9
  190.5 3.1 %second_sums.2 = (bf16[4,24,1920]{2,1,0:T(8,128)(2,1)}, bf16[4,24,1920]{2,1,0:T(8,128)(2,1)}, bf16[4,24,1920]{2,1,0:T(8,128)(2,1)}, bf16[4,24,1920]{2,1,0:T(8,128)(2,1)}) custom-call(s32[2]{0:T(128)} %pad_add_fusion.bits, bf16[4,2,24,1920]{3,2,1,0:T(8,128)(2,1)} %get-tuple-element.190.keep_a, bf16[4,2,24,1920]{3,2,1,0:T(8,128)(2,1)} %get-tuple-element.191.keep_b, ...), custom_call_target="tpu_custom_call" | custom-call | tf_op jit(solution)/shard_map/second_sums/pallas_call | solution.py:928
  193.7 3.3 %reduce-scatter.2.cloned.1.call-done = bf16[384,768]{1,0:T(8,128)(2,1)} async-done(((bf16[3072,768]{1,0:T(8,128)(2,1)}), bf16[384,768]{1,0:T(8,128)(2,1)}) %reduce-scatter.2.cloned.1.call-update) | async-done | bytes 589840 | tf_op jit(solution)/shard_map/reduce_scatter | solution.py:1121
  197.0 1.4 copy.51
  199.3 1.5 collective-permute-start.5
  201.3 0.7 reduce.3
  202.5 0.8 pad.4.rest_0_
  203.3 6.7 %grad_before.3 = bf16[768,1280]{1,0:T(8,128)(2,1)} custom-call(bf16[2,512,768]{2,1,0:T(8,128)(2,1)} %xc.7, bf16[2,80,768]{2,1,0:T(8,128)(2,1)} %get-tuple-element.325.xq, bf16[2,592,384]{2,1,0:T(8,128)(2,1)} %get-tuple-element.219.dq.dq_m, bf16[2,512,384]{2,1,0:T(8,128)(2,1)} %get-tuple-element.220.dk.dk_m, bf16[2,512,384]{2,1,0:T(8,128)(2,1)} %get-tuple-element.221.dv.dv_m, ...), custom_call_target="tpu_custom_call" | custom-call | tf_op jit(solution)/shard_map/grad_before/pallas_call | solution.py:809
  210.0 3.2 %first_sums.3 = (bf16[4,2,24,1280]{3,2,1,0:T(8,128)(2,1)}, bf16[4,2,24,1280]{3,2,1,0:T(8,128)(2,1)}, bf16[4,2,24,1280]{3,2,1,0:T(8,128)(2,1)}, bf16[4,2,24,1280]{3,2,1,0:T(8,128)(2,1)}) custom-call(s32[2]{0:T(128)} %pad_add_fusion.bits, bf16[4,2,2,48,1280]{4,3,2,1,0:T(8,128)(2,1)} %bitcast.47), custom_call_target="tpu_custom_call" | custom-call | tf_op jit(solution)/shard_map/first_sums/pallas_call | solution.py:928
  213.3 2.4 third_sums.2
  215.6 3.7 %all-to-all-start.1 = ((bf16[4,48,1920]{2,1,0:T(8,128)(2,1)}), bf16[4,48,1920]{2,1,0:T(8,128)(2,1)S(1)}, u32[]{:S(2)}, u32[]{:S(2)}) async-start(bf16[4,48,1920]{2,1,0:T(8,128)(2,1)} %third_sums.2), calls=%async_computation.2 | async-start | bytes 1474560 | tf_op jit(solution)/shard_map/all_to_all | solution.py:981
  219.3 1.4 collective-permute-start.7
  220.8 1.4 collective-permute-start.8
  222.4 9.6 %input_grad.1 = (f32[2,512,768]{2,1,0:T(8,128)}, bf16[2,80,768]{2,1,0:T(8,128)(2,1)}) custom-call(s32[1]{0:T(128)} %bitcast.7.half.first.core, f32[2,512,768]{2,1,0:T(8,128)} %get-tuple-element.242.first_c, f32[2,80,768]{2,1,0:T(8,128)} %get-tuple-element.243.first_q, bf16[2,592,384]{2,1,0:T(8,128)(2,1)} %get-tuple-element.199.dq.dq_o, ...), custom_call_target="tpu_custom_call" | custom-call | tf_op jit(solution)/shard_map/input_grad/pallas_call | solution.py:849
  232.6 0.9 collective-permute-done.8.got_b
  233.5 0.8 copy-done.12
  234.2 2.6 second_sums.3
  236.8 1.1 collective-permute-start.9
  237.9 1.3 collective-permute-start.10
  240.1 3.2 %collective-permute-done.9.got_a = bf16[4,24,1280]{2,1,0:T(8,128)(2,1)S(1)} collective-permute-done((bf16[4,24,1280]{2,1,0:T(8,128)(2,1)}, bf16[4,24,1280]{2,1,0:T(8,128)(2,1)S(1)}, u32[]{:S(2)}, u32[]{:S(2)}) %collective-permute-start.9) | collective-permute-done | bytes 245792 | tf_op jit(solution)/shard_map/ppermute | solution.py:867
  243.3 1.0 collective-permute-done.10.got_b
  244.4 0.7 copy-done.19
  245.1 2.2 third_sums.3
  247.3 0.9 copy-done
  248.2 1.9 part_sums.2
  250.0 4.8 %all-to-all-start.2 = ((bf16[4,48,1280]{2,1,0:T(8,128)(2,1)}), bf16[4,48,1280]{2,1,0:T(8,128)(2,1)S(1)}, u32[]{:S(2)}, u32[]{:S(2)}) async-start(bf16[4,48,1280]{2,1,0:T(8,128)(2,1)} %third_sums.3), calls=%async_computation.3 | async-start | bytes 983040 | tf_op jit(solution)/shard_map/all_to_all | solution.py:981
  254.9 1.3 collective-permute-start.12
  256.2 0.7 collective-permute-start.11
  256.9 1.3 collective-permute-start.14
  258.8 9.9 %collective-permute-done.14 = bf16[2,20,1536]{2,0,1:T(2,128)(2,1)S(1)} collective-permute-done((bf16[2,20,1536]{2,0,1:T(2,128)(2,1)S(1)}, bf16[2,20,1536]{2,0,1:T(2,128)(2,1)S(1)}, u32[]{:S(2)}, u32[]{:S(2)}) %collective-permute-start.14) | collective-permute-done | bytes 122912 | tf_op jit(solution)/shard_map/ppermute | solution.py:867
  268.8 0.8 copy-done.2
  269.6 1.7 part_sums.3
  271.5 0.7 copy-done.10
  272.2 1.2 collective-permute-start.16
  273.4 0.8 collective-permute-start.17
  274.3 0.9 pad_maximum_fusion.2
  276.1 2.3 collective-permute-done.16
  279.1 2.2 place_sums.3
  281.3 2.4 place_sums.4
  283.7 0.9 slice_convert_fusion
  284.6 0.7 copy-done.17
  285.3 2.0 place_sums.5
  287.3 1.3 reshape.152
  288.7 1.3 reshape.153
  (121 shorter events, 10.6 us)
Async XLA Ops:
  7.2 7.1 %copy-start.31 = (s32[8]{0:T(128)S(1)}, s32[8]{0:T(128)}, u32[]{:S(2)}) copy-start(s32[8]{0:T(128)} %param.20) | copy-start | bytes 100
  7.2 8.6 %copy-start.22 = (bf16[12,32]{1,0:T(8,128)(2,1)S(1)}, bf16[12,32]{1,0:T(8,128)(2,1)}, u32[]{:S(2)}) copy-start(bf16[12,32]{1,0:T(8,128)(2,1)} %param.33) | copy-start | bytes 2308
  7.2 9.2 %copy-start.26 = (bf16[3072]{0:T(1024)(128)(2,1)S(1)}, bf16[3072]{0:T(1024)(128)(2,1)}, u32[]{:S(2)}) copy-start(bf16[3072]{0:T(1024)(128)(2,1)} %param.30) | copy-start | bytes 18436
  10.1 16.8 %all-to-all-start = ((bf16[8,20,1536]{2,1,0:T(8,128)(2,1)}), bf16[8,20,1536]{2,1,0:T(8,128)(2,1)S(1)}, u32[]{:S(2)}, u32[]{:S(2)}) async-start(bf16[8,20,1536]{2,1,0:T(8,128)(2,1)} %pad_maximum_fusion), calls=%async_computation | async-start | bytes 1179648 | tf_op jit(solution)/shard_map/all_to_all | solution.py:1077
  14.3 182.7 %reduce-scatter.2.cloned.1.call-start = ((), (), s32[]{:S(2)}) async-start(), calls=%async_computation.4 | async-start | bytes 5308416 | tf_op jit(solution)/shard_map/reduce_scatter | solution.py:1121
  132.7 17.1 %collective-permute-start = (bf16[768,1920]{1,0:T(8,128)(2,1)}, bf16[768,1920]{1,0:T(8,128)(2,1)S(1)}, u32[]{:S(2)}, u32[]{:S(2)}) collective-permute-start(bf16[768,1920]{1,0:T(8,128)(2,1)} %get-tuple-element.179), channel_id=1, source_target_pairs={{0,1},{1,0},{2,3},{3,2},{4,5},{5,4},{6,7},{7,6},{8,9},{9,8},{10,11... | collective-permute-start | bytes 8847368 | tf_op jit(solution)/shard_map/ppermute | solution.py:867
  149.9 1.6 copy-start.1
  156.3 10.2 %copy-start.25 = (f32[3,768]{1,0:T(4,128)S(1)}, f32[3,768]{1,0:T(4,128)}, u32[]{:S(2)}) copy-start(f32[3,768]{1,0:T(4,128)} %get-tuple-element.225) | copy-start | bytes 27652
  162.4 27.3 %collective-permute-start.3 = (bf16[768,1152]{1,0:T(8,128)(2,1)}, bf16[768,1152]{1,0:T(8,128)(2,1)S(1)}, u32[]{:S(2)}, u32[]{:S(2)}) collective-permute-start(bf16[768,1152]{1,0:T(8,128)(2,1)} %grad_before.2), channel_id=1, source_target_pairs={{0,1},{1,0},{2,3},{3,2},{4,5},{5,4},{6,7},{7,6},{8,9},{9,8},{10,11... | collective-permute-start | bytes 5308424 | tf_op jit(solution)/shard_map/ppermute | solution.py:867
  162.4 19.6 %collective-permute-start.1 = (bf16[4,2,24,1920]{3,2,1,0:T(8,128)(2,1)}, bf16[4,2,24,1920]{3,2,1,0:T(8,128)(2,1)S(1)}, u32[]{:S(2)}, u32[]{:S(2)}) collective-permute-start(bf16[4,2,24,1920]{3,2,1,0:T(8,128)(2,1)} %get-tuple-element.197), channel_id=1, source_target_pairs={{0,2},{1,3},{2,0},{3,1},{4,6},{5,7},{6,4},{7,5},{8,10},{9,11},{10,... | collective-permute-start | bytes 2211848 | tf_op jit(solution)/shard_map/ppermute | solution.py:867
  164.6 25.0 %collective-permute-start.2 = (bf16[4,2,24,1920]{3,2,1,0:T(8,128)(2,1)}, bf16[4,2,24,1920]{3,2,1,0:T(8,128)(2,1)S(1)}, u32[]{:S(2)}, u32[]{:S(2)}) collective-permute-start(bf16[4,2,24,1920]{3,2,1,0:T(8,128)(2,1)} %get-tuple-element.198), channel_id=1, source_target_pairs={{0,4},{4,0},{8,12},{12,8},{16,20},{20,16},{24,28},{28,24},{1,5},{5... | collective-permute-start | bytes 2211848 | tf_op jit(solution)/shard_map/ppermute | solution.py:867
  182.1 7.6 %copy-start.8 = (bf16[4,2,24,1920]{3,2,1,0:T(8,128)(2,1)}, bf16[4,2,24,1920]{3,2,1,0:T(8,128)(2,1)S(1)}, u32[]{:S(2)}) copy-start(bf16[4,2,24,1920]{3,2,1,0:T(8,128)(2,1)S(1)} %collective-permute-done.1.got_a) | copy-start | bytes 2211844
  189.7 0.9 copy-start.9
  189.7 8.7 %copy-start.3 = (bf16[768,1152]{1,0:T(8,128)(2,1)}, bf16[768,1152]{1,0:T(8,128)(2,1)S(1)}, u32[]{:S(2)}) copy-start(bf16[768,1152]{1,0:T(8,128)(2,1)S(1)} %collective-permute-done.3.rest_1_) | copy-start | bytes 5308420
  193.6 5.7 %copy-start.32 = (bf16[4,24,1920]{2,1,0:T(8,128)(2,1)S(1)}, bf16[4,24,1920]{2,1,0:T(8,128)(2,1)}, u32[]{:S(2)}) copy-start(bf16[4,24,1920]{2,1,0:T(8,128)(2,1)} %get-tuple-element.217) | copy-start | bytes 1105924
  193.6 7.2 %copy-start.24 = (f32[3,768]{1,0:T(4,128)S(1)}, f32[3,768]{1,0:T(4,128)}, u32[]{:S(2)}) copy-start(f32[3,768]{1,0:T(4,128)} %get-tuple-element.224) | copy-start | bytes 27652
  193.6 7.7 %copy-start.23 = (f32[1,3072]{1,0:T(1,128)S(1)}, f32[1,3072]{1,0:T(1,128)}, u32[]{:S(2)}) copy-start(f32[1,3072]{1,0:T(1,128)} %get-tuple-element.226) | copy-start | bytes 36868
  193.6 8.5 %copy-start.28 = (f32[3,2,128]{2,1,0:T(2,128)S(1)}, f32[3,2,128]{2,1,0:T(2,128)}, u32[]{:S(2)}) copy-start(f32[3,2,128]{2,1,0:T(2,128)} %get-tuple-element.228) | copy-start | bytes 9220
  193.7 8.5 %copy-start.30 = (f32[3,2,128]{2,1,0:T(2,128)S(1)}, f32[3,2,128]{2,1,0:T(2,128)}, u32[]{:S(2)}) copy-start(f32[3,2,128]{2,1,0:T(2,128)} %get-tuple-element.227) | copy-start | bytes 9220
  193.7 8.7 %copy-start.27 = (f32[2,384]{1,0:T(2,128)S(1)}, f32[2,384]{1,0:T(2,128)}, u32[]{:S(2)}) copy-start(f32[2,384]{1,0:T(2,128)} %get-tuple-element.223) | copy-start | bytes 9220
  193.7 8.7 %copy-start.29 = (f32[2,384]{1,0:T(2,128)S(1)}, f32[2,384]{1,0:T(2,128)}, u32[]{:S(2)}) copy-start(f32[2,384]{1,0:T(2,128)} %get-tuple-element.222) | copy-start | bytes 9220
  198.6 11.4 %collective-permute-start.6 = (bf16[384,384]{1,0:T(8,128)(2,1)S(1)}, bf16[384,384]{1,0:T(8,128)(2,1)S(1)}, u32[]{:S(2)}, u32[]{:S(2)}) collective-permute-start(bf16[384,384]{1,0:T(8,128)(2,1)S(1)} %bitcast.55), channel_id=1, source_target_pairs={{0,1},{1,0},{2,3},{3,2},{4,5},{5,4},{6,7},{7,6},{8,9},{9,8},{10,11... | collective-permute-start | bytes 884744 | tf_op jit(solution)/shard_map/ppermute | solution.py:867
  198.7 11.3 %collective-permute-start.4 = (bf16[4,24,1920]{2,1,0:T(8,128)(2,1)}, bf16[4,24,1920]{2,1,0:T(8,128)(2,1)S(1)}, u32[]{:S(2)}, u32[]{:S(2)}) collective-permute-start(bf16[4,24,1920]{2,1,0:T(8,128)(2,1)} %get-tuple-element.216), channel_id=1, source_target_pairs={{0,4},{4,0},{8,12},{12,8},{16,20},{20,16},{24,28},{28,24},{1,5},{5... | collective-permute-start | bytes 1105928 | tf_op jit(solution)/shard_map/ppermute | solution.py:867
  199.3 10.7 %collective-permute-start.5 = (bf16[4,24,1920]{2,1,0:T(8,128)(2,1)S(1)}, bf16[4,24,1920]{2,1,0:T(8,128)(2,1)S(1)}, u32[]{:S(2)}, u32[]{:S(2)}) collective-permute-start(bf16[4,24,1920]{2,1,0:T(8,128)(2,1)S(1)} %copy-done.32), channel_id=1, source_target_pairs={{0,2},{1,3},{2,0},{3,1},{4,6},{5,7},{6,4},{7,5},{8,10},{9,11},{10,... | collective-permute-start | bytes 1105928 | tf_op jit(solution)/shard_map/ppermute | solution.py:867
  210.0 3.3 %copy-start.13 = (bf16[4,24,1920]{2,1,0:T(8,128)(2,1)}, bf16[4,24,1920]{2,1,0:T(8,128)(2,1)S(1)}, u32[]{:S(2)}) copy-start(bf16[4,24,1920]{2,1,0:T(8,128)(2,1)S(1)} %collective-permute-done.4.got_a) | copy-start | bytes 1105924
  210.0 3.3 %copy-start.14 = (bf16[4,24,1920]{2,1,0:T(8,128)(2,1)}, bf16[4,24,1920]{2,1,0:T(8,128)(2,1)S(1)}, u32[]{:S(2)}) copy-start(bf16[4,24,1920]{2,1,0:T(8,128)(2,1)S(1)} %collective-permute-done.5.got_b) | copy-start | bytes 1105924
  215.6 31.7 %all-to-all-start.1 = ((bf16[4,48,1920]{2,1,0:T(8,128)(2,1)}), bf16[4,48,1920]{2,1,0:T(8,128)(2,1)S(1)}, u32[]{:S(2)}, u32[]{:S(2)}) async-start(bf16[4,48,1920]{2,1,0:T(8,128)(2,1)} %third_sums.2), calls=%async_computation.2 | async-start | bytes 1474560 | tf_op jit(solution)/shard_map/all_to_all | solution.py:981
  219.3 13.3 %collective-permute-start.7 = (bf16[4,2,24,1280]{3,2,1,0:T(8,128)(2,1)}, bf16[4,2,24,1280]{3,2,1,0:T(8,128)(2,1)S(1)}, u32[]{:S(2)}, u32[]{:S(2)}) collective-permute-start(bf16[4,2,24,1280]{3,2,1,0:T(8,128)(2,1)} %get-tuple-element.240), channel_id=1, source_target_pairs={{0,2},{1,3},{2,0},{3,1},{4,6},{5,7},{6,4},{7,5},{8,10},{9,11},{10,... | collective-permute-start | bytes 1474568 | tf_op jit(solution)/shard_map/ppermute | solution.py:867
  220.8 12.7 %collective-permute-start.8 = (bf16[4,2,24,1280]{3,2,1,0:T(8,128)(2,1)}, bf16[4,2,24,1280]{3,2,1,0:T(8,128)(2,1)S(1)}, u32[]{:S(2)}, u32[]{:S(2)}) collective-permute-start(bf16[4,2,24,1280]{3,2,1,0:T(8,128)(2,1)} %get-tuple-element.241), channel_id=1, source_target_pairs={{0,4},{4,0},{8,12},{12,8},{16,20},{20,16},{24,28},{28,24},{1,5},{5... | collective-permute-start | bytes 1474568 | tf_op jit(solution)/shard_map/ppermute | solution.py:867
  231.9 7.2 %copy-start.20 = (bf16[2,80,768]{2,1,0:T(8,128)(2,1)S(1)}, bf16[2,80,768]{2,1,0:T(8,128)(2,1)}, u32[]{:S(2)}) copy-start(bf16[2,80,768]{2,1,0:T(8,128)(2,1)} %get-tuple-element.256) | copy-start | bytes 737284
  231.9 7.2 %copy-start.21 = (bf16[2,80,768]{2,1,0:T(8,128)(2,1)S(1)}, bf16[2,80,768]{2,1,0:T(8,128)(2,1)}, u32[]{:S(2)}) copy-start(bf16[2,80,768]{2,1,0:T(8,128)(2,1)} %get-tuple-element.257) | copy-start | bytes 737284
  232.6 0.9 copy-start.11
  233.5 0.8 copy-start.12
  236.8 6.5 %collective-permute-start.9 = (bf16[4,24,1280]{2,1,0:T(8,128)(2,1)}, bf16[4,24,1280]{2,1,0:T(8,128)(2,1)S(1)}, u32[]{:S(2)}, u32[]{:S(2)}) collective-permute-start(bf16[4,24,1280]{2,1,0:T(8,128)(2,1)} %get-tuple-element.254), channel_id=1, source_target_pairs={{0,4},{4,0},{8,12},{12,8},{16,20},{20,16},{24,28},{28,24},{1,5},{5... | collective-permute-start | bytes 737288 | tf_op jit(solution)/shard_map/ppermute | solution.py:867
  237.9 6.5 %collective-permute-start.10 = (bf16[4,24,1280]{2,1,0:T(8,128)(2,1)}, bf16[4,24,1280]{2,1,0:T(8,128)(2,1)S(1)}, u32[]{:S(2)}, u32[]{:S(2)}) collective-permute-start(bf16[4,24,1280]{2,1,0:T(8,128)(2,1)} %get-tuple-element.255), channel_id=1, source_target_pairs={{0,2},{1,3},{2,0},{3,1},{4,6},{5,7},{6,4},{7,5},{8,10},{9,11},{10,... | collective-permute-start | bytes 737288 | tf_op jit(solution)/shard_map/ppermute | solution.py:867
  243.3 1.1 copy-start.18
  244.4 0.7 copy-start.19
  247.3 0.9 copy-start
  250.0 21.4 %copy-start.7 = (bf16[48,1920]{1,0:T(8,128)(2,1)S(1)}, bf16[48,1920]{1,0:T(8,128)(2,1)}, u32[]{:S(2)}) copy-start(bf16[48,1920]{1,0:T(8,128)(2,1)} %part_sums.2) | copy-start | bytes 552964
  250.0 18.7 %all-to-all-start.2 = ((bf16[4,48,1280]{2,1,0:T(8,128)(2,1)}), bf16[4,48,1280]{2,1,0:T(8,128)(2,1)S(1)}, u32[]{:S(2)}, u32[]{:S(2)}) async-start(bf16[4,48,1280]{2,1,0:T(8,128)(2,1)} %third_sums.3), calls=%async_computation.3 | async-start | bytes 983040 | tf_op jit(solution)/shard_map/all_to_all | solution.py:981
  254.9 13.9 %collective-permute-start.12 = (bf16[384,384]{1,0:T(8,128)(2,1)S(1)}, bf16[384,384]{1,0:T(8,128)(2,1)S(1)}, u32[]{:S(2)}, u32[]{:S(2)}) collective-permute-start(bf16[384,384]{1,0:T(8,128)(2,1)S(1)} %fusion), channel_id=1, source_target_pairs={{0,2},{1,3},{2,0},{3,1},{4,6},{5,7},{6,4},{7,5},{8,10},{9,11},{10,... | collective-permute-start | bytes 884744 | tf_op jit(solution)/shard_map/ppermute | solution.py:867
  256.2 12.6 %collective-permute-start.11 = (bf16[48,1920]{1,0:T(8,128)(2,1)}, bf16[48,1920]{1,0:T(8,128)(2,1)S(1)}, u32[]{:S(2)}, u32[]{:S(2)}) collective-permute-start(bf16[48,1920]{1,0:T(8,128)(2,1)} %part_sums.2), channel_id=1, source_target_pairs={{0,2},{1,3},{2,0},{3,1},{4,6},{5,7},{6,4},{7,5},{8,10},{9,11},{10,... | collective-permute-start | bytes 552968 | tf_op jit(solution)/shard_map/ppermute | solution.py:867
  256.9 1.9 collective-permute-start.13
  256.9 11.8 %collective-permute-start.14 = (bf16[2,20,1536]{2,0,1:T(2,128)(2,1)S(1)}, bf16[2,20,1536]{2,0,1:T(2,128)(2,1)S(1)}, u32[]{:S(2)}, u32[]{:S(2)}) collective-permute-start(bf16[2,20,1536]{2,0,1:T(2,128)(2,1)S(1)} %get-tuple-element.270), channel_id=1, source_target_pairs={{0,2},{1,3},{2,0},{3,1},{4,6},{5,7},{6,4},{7,5},{8,10},{9,11},{10,... | collective-permute-start | bytes 368648 | tf_op jit(solution)/shard_map/ppermute | solution.py:867
  258.2 10.6 %collective-permute-start.15 = (bf16[2,20,1536]{2,0,1:T(2,128)(2,1)S(1)}, bf16[2,20,1536]{2,0,1:T(2,128)(2,1)S(1)}, u32[]{:S(2)}, u32[]{:S(2)}) collective-permute-start(bf16[2,20,1536]{2,0,1:T(2,128)(2,1)S(1)} %get-tuple-element.271), channel_id=1, source_target_pairs={{0,3},{1,2},{2,1},{3,0},{4,7},{5,6},{6,5},{7,4},{8,11},{9,10},{10,... | collective-permute-start | bytes 368648 | tf_op jit(solution)/shard_map/ppermute | solution.py:867
  268.8 0.8 copy-start.2
  271.3 0.9 copy-start.10
  271.4 4.7 %copy-start.5 = (bf16[384,384]{1,0:T(8,128)(2,1)}, bf16[384,384]{1,0:T(8,128)(2,1)S(1)}, u32[]{:S(2)}) copy-start(bf16[384,384]{1,0:T(8,128)(2,1)S(1)} %add_convert_fusion.own) | copy-start | bytes 884740
  272.2 6.2 %copy-start.4 = (bf16[96,1920]{1,0:T(8,128)(2,1)}, bf16[96,1920]{1,0:T(8,128)(2,1)S(1)}, u32[]{:S(2)}) copy-start(bf16[96,1920]{1,0:T(8,128)(2,1)S(1)} %pad_maximum_fusion.4.own) | copy-start | bytes 1105924
  272.2 6.2 %collective-permute-start.16 = (bf16[48,1280]{1,0:T(8,128)(2,1)S(1)}, bf16[48,1280]{1,0:T(8,128)(2,1)S(1)}, u32[]{:S(2)}, u32[]{:S(2)}) collective-permute-start(bf16[48,1280]{1,0:T(8,128)(2,1)S(1)} %copy-done.10), channel_id=1, source_target_pairs={{0,2},{1,3},{2,0},{3,1},{4,6},{5,7},{6,4},{7,5},{8,10},{9,11},{10,... | collective-permute-start | bytes 368648 | tf_op jit(solution)/shard_map/ppermute | solution.py:867
  273.4 5.0 %collective-permute-start.17 = (bf16[384,384]{1,0:T(8,128)(2,1)S(1)}, bf16[384,384]{1,0:T(8,128)(2,1)S(1)}, u32[]{:S(2)}, u32[]{:S(2)}) collective-permute-start(bf16[384,384]{1,0:T(8,128)(2,1)S(1)} %add_convert_fusion.own), channel_id=1, source_target_pairs={{0,1},{1,0},{2,3},{3,2},{4,5},{5,4},{6,7},{7,6},{8,9},{9,8},{10,11... | collective-permute-start | bytes 884744 | tf_op jit(solution)/shard_map/ppermute | solution.py:867
  274.2 4.1 %collective-permute-start.18 = (bf16[96,1920]{1,0:T(8,128)(2,1)S(1)}, bf16[96,1920]{1,0:T(8,128)(2,1)S(1)}, u32[]{:S(2)}, u32[]{:S(2)}) collective-permute-start(bf16[96,1920]{1,0:T(8,128)(2,1)S(1)} %pad_maximum_fusion.4.own), channel_id=1, source_target_pairs={{0,1},{1,0},{2,3},{3,2},{4,5},{5,4},{6,7},{7,6},{8,9},{9,8},{10,11... | collective-permute-start | bytes 1105928 | tf_op jit(solution)/shard_map/ppermute | solution.py:867
  278.4 0.7 copy-start.16
  278.4 2.9 copy-start.15
  278.5 6.1 %copy-start.6 = (bf16[96,1280]{1,0:T(8,128)(2,1)}, bf16[96,1280]{1,0:T(8,128)(2,1)S(1)}, u32[]{:S(2)}) copy-start(bf16[96,1280]{1,0:T(8,128)(2,1)S(1)} %pad_maximum_fusion.5.own) | copy-start | bytes 737284
  278.5 6.1 %collective-permute-start.19 = (bf16[96,1280]{1,0:T(8,128)(2,1)S(1)}, bf16[96,1280]{1,0:T(8,128)(2,1)S(1)}, u32[]{:S(2)}, u32[]{:S(2)}) collective-permute-start(bf16[96,1280]{1,0:T(8,128)(2,1)S(1)} %pad_maximum_fusion.5.own), channel_id=1, source_target_pairs={{0,1},{1,0},{2,3},{3,2},{4,5},{5,4},{6,7},{7,6},{8,9},{9,8},{10,11... | collective-permute-start | bytes 737288 | tf_op jit(solution)/shard_map/ppermute | solution.py:867
  284.6 0.7 copy-start.17
Sparse Core Ops, SparseCore 0:
  94.3 102.6 reduce-scatter.1

commit v4 on v3

--- a/solution.py
+++ b/solution.py
@@ -94,11 +94,11 @@
 
 def project(xc, wq, wk, wv, before):
     seqs, length, width = xc.shape
-    rows = pl.BlockSpec((1, length // 2, width), lambda s, i: (s, i, 0))
+    rows = pl.BlockSpec((1, length, width), lambda s: (s, 0, 0))
     weight = full_spec((width, width))
     return pl.pallas_call(
         project_kernel,
-        grid=(seqs, 2),
+        grid=(seqs,),
         in_specs=[rows, weight, weight, weight, full_spec((2, width))],
         out_specs=[rows] * 3,
         out_shape=[jax.ShapeDtypeStruct(xc.shape, BF16)] * 3,

time: 302 us -> 302 us (level)
  no operation moved by 1% of the time
where the time goes in v4:
time: 302 us; the launch traced here: 297 us
  Pallas kernels  194 us (64%)
  starting transfers between devices  30.8 us (10%)
  waiting for transfers between devices  29 us (10%)
  local copies, waits for them, and re-layouts  21.1 us (7%)
  between operations  14.7 us (5%)
  other arithmetic  6.97 us (2%)
    pallas_call x1, Pallas kernels, rows_forward(): pl.pallas_call(rows_forward_kernel, grid_spec=pltpu.PrefetchScalarGridSpe...  41.6 us
    pallas_call x1, Pallas kernels, rows_backward(): pl.pallas_call(rows_backward_kernel, grid_spec=pltpu.PrefetchScalarGridSp...  38.6 us
    pallas_call x2, Pallas kernels, attention_backward(): pl.pallas_call(attention_backward_kernel, grid_spec=pltpu.PrefetchScalarG...  31.5 us
    ppermute x20, waiting for transfers between devices, swap(): return lax.ppermute(value, axis, [(i, i ^ stride) for i in range(count)])  25.6 us
    pallas_call x1, Pallas kernels, attention_forward(): pl.pallas_call(attention_forward_kernel, grid=(seqs, PAIRS), in_specs=[by...  24.4 us
    pallas_call x6, Pallas kernels, staged(): pl.pallas_call(kernel, in_specs=[pl.BlockSpec(memory_space=pltpu.SMEM)] +...  18.3 us
    ppermute x20, starting transfers between devices, swap(): return lax.ppermute(value, axis, [(i, i ^ stride) for i in range(count)])  18.1 us
    pallas_call x2, Pallas kernels, grad_before(): pl.pallas_call(grad_before_kernel, grid=(2,), in_specs=[pl.BlockSpec((seq...  12.8 us
  transfers between devices with their start and end apart: 24, of which 9 were waited for; matrix products, arithmetic and copies ran while one was open for 4% of the time, Pallas kernels for 39%

profile of v4, /device:TPU:0, one launch (start us, length us, event | category | flops | bytes accessed | tf_op | source)
XLA Modules:
  0.0 296.9 jit_solution(6159460524770002648)
XLA Ops:
  7.2 1.0 copy.45
  8.2 1.0 copy.46
  9.2 0.9 pad_maximum_fusion
  10.1 4.2 %all-to-all-start = ((bf16[8,20,1536]{2,1,0:T(8,128)(2,1)}), bf16[8,20,1536]{2,1,0:T(8,128)(2,1)S(1)}, u32[]{:S(2)}, u32[]{:S(2)}) async-start(bf16[8,20,1536]{2,1,0:T(8,128)(2,1)} %pad_maximum_fusion), calls=%async_computation | async-start | bytes 1179648 | tf_op jit(solution)/shard_map/all_to_all | solution.py:1077
  14.4 0.8 maximum_bitcast_fusion
  17.8 1.0 copy.49.thr_c
  18.8 7.2 %project.1 = (bf16[2,512,768]{2,1,0:T(8,128)(2,1)}, bf16[2,512,768]{2,1,0:T(8,128)(2,1)}, bf16[2,512,768]{2,1,0:T(8,128)(2,1)}) custom-call(bf16[2,512,768]{2,1,0:T(8,128)(2,1)} %xc.7, bf16[768,768]{1,0:T(8,128)(2,1)} %wq_m.1, bf16[768,768]{1,0:T(8,128)(2,1)} %wk_m.1, bf16[768,768]{1,0:T(8,128)(2,1)} %wv_m.1, bf16[2,768]{1,0:T(2,128)(2,1)} %before.3), custom_call_target="tpu_custom_call" | custom-call | tf_op jit(solution)/shard_map/project/pallas_call | solution.py:99
  26.0 0.7 iota_add_fusion.thr_q
  27.1 0.8 fusion.7
  27.9 24.4 %attention_forward.1 = (bf16[2,592,768]{2,1,0:T(8,128)(2,1)}, bf16[2,12,592,512]{3,2,1,0:T(8,128)(2,1)}, f32[2,592,768]{2,1,0:T(8,128)}, bf16[2,592,768]{2,1,0:T(8,128)(2,1)}) custom-call(bf16[2,512,768]{2,1,0:T(8,128)(2,1)} %get-tuple-element.165.q_in, bf16[2,512,768]{2,1,0:T(8,128)(2,1)} %get-tuple-element.166.k_in.k, ...), custom_call_target="tpu_custom_call" | custom-call | tf_op jit(solution)/shard_map/attention_forward/pallas_call | solution.py:219
  52.3 41.6 %rows_forward.1 = (bf16[2,512,768]{2,1,0:T(8,128)(2,1)}, bf16[2,80,768]{2,1,0:T(8,128)(2,1)}, bf16[1184,3072]{1,0:T(8,128)(2,1)}, bf16[1184,768]{1,0:T(8,128)(2,...) custom-call(bf16[2,592,768]{2,1,0:T(8,128)(2,1)} %get-tuple-element., ...), custom_call_target="tpu_custom_call" | custom-call | tf_op jit(solution)/shard_map/rows_forward/pallas_call | solution.py:680
  94.0 38.6 %rows_backward.1 = (f32[2,512,768]{2,1,0:T(8,128)}, f32[2,80,768]{2,1,0:T(8,128)}, bf16[2,592,768]{2,1,0:T(8,128)(2,1)}, f32[3,768]{1,0:T(4,128)}, f32[1,3072]{1...) custom-call(s32[1]{0:T(128)} %bitcast.7.half.first.core, bf16[1184,768]{1,0:T(8,128)(2,1)} %get-tuple-element.171.outer, ...), custom_call_target="tpu_custom_call" | custom-call | tf_op jit(solution)/shard_map/rows_backward/pallas_call | solution.py:737
  133.7 16.0 %attention_backward.2 = (bf16[2,592,384]{2,1,0:T(8,128)(2,1)}, bf16[2,512,384]{2,1,0:T(8,128)(2,1)}, bf16[2,512,384]{2,1,0:T(8,128)(2,1)}, f32[2,384]{1,0:T(2,128)}, f32[3,2,128]{2,1,0:T(2,128)}) custom-call(s32[1]{0:T(128)} %bitcast.10.first, bf16[2,592,768]{2,1,0:T(8,128)(2,1)} %get-tuple-element.180.q, bf16[2,512,768]{2,1,0:T(8,128)(2,1)} %get-tuple-element.166.k_in.k, ...), custom_call_target="tpu_custom_call" | custom-call | tf_op jit(solution)/shard_map/attention_backward/pallas_call | solution.py:413
  149.7 1.6 copy-done.1
  151.3 4.8 %first_sums.2 = (bf16[4,2,24,1920]{3,2,1,0:T(8,128)(2,1)}, bf16[4,2,24,1920]{3,2,1,0:T(8,128)(2,1)}, bf16[4,2,24,1920]{3,2,1,0:T(8,128)(2,1)}, bf16[4,2,24,1920]{3,2,1,0:T(8,128)(2,1)}) custom-call(s32[2]{0:T(128)} %pad_add_fusion.bits, bf16[4,2,2,48,1920]{4,3,2,1,0:T(8,128)(2,1)} %bitcast.48, bf16[4,2,2,48,1920]{4,3,2,1,0:T(8,128)(2,1)} %bitcast.49), custom_call_target="tpu_custom_call" | custom-call | tf_op jit(solution)/shard_map/first_sums/pallas_call | solution.py:928
  156.2 6.0 %grad_before.2 = bf16[768,1152]{1,0:T(8,128)(2,1)} custom-call(bf16[2,512,768]{2,1,0:T(8,128)(2,1)} %xc.7, bf16[2,80,768]{2,1,0:T(8,128)(2,1)} %get-tuple-element.325.xq, bf16[2,592,384]{2,1,0:T(8,128)(2,1)} %get-tuple-element.199.dq.dq_o, bf16[2,512,384]{2,1,0:T(8,128)(2,1)} %get-tuple-element.200.dk.dk_o, bf16[2,512,384]{2,1,0:T(8,128)(2,1)} %get-tuple-element.201.dv.dv_o), custom_call_target="tpu_custom_call" | custom-call | tf_op jit(solution)/shard_map/grad_before/pallas_call | solution.py:809
  162.3 2.2 collective-permute-start.1
  164.5 1.9 collective-permute-start.2
  166.4 15.5 %attention_backward.3 = (bf16[2,592,384]{2,1,0:T(8,128)(2,1)}, bf16[2,512,384]{2,1,0:T(8,128)(2,1)}, bf16[2,512,384]{2,1,0:T(8,128)(2,1)}, f32[2,384]{1,0:T(2,128)}, f32[3,2,128]{2,1,0:T(2,128)}) custom-call(s32[1]{0:T(128)} %bitcast.7.half.first.core, bf16[2,592,768]{2,1,0:T(8,128)(2,1)} %get-tuple-element.180.q, ...), custom_call_target="tpu_custom_call" | custom-call | tf_op jit(solution)/shard_map/attention_backward/pallas_call | solution.py:413
  181.9 7.6 %collective-permute-done.2.got_b = bf16[4,2,24,1920]{3,2,1,0:T(8,128)(2,1)S(1)} collective-permute-done((bf16[4,2,24,1920]{3,2,1,0:T(8,128)(2,1)}, bf16[4,2,24,1920]{3,2,1,0:T(8,128)(2,1)S(1)}, u32[]{:S(2)}, u32[]{:S(2)}) %collective-permute-start.2) | collective-permute-done | bytes 737312 | tf_op jit(solution)/shard_map/ppermute | solution.py:867
  189.5 0.9 copy-done.9
  190.4 3.1 %second_sums.2 = (bf16[4,24,1920]{2,1,0:T(8,128)(2,1)}, bf16[4,24,1920]{2,1,0:T(8,128)(2,1)}, bf16[4,24,1920]{2,1,0:T(8,128)(2,1)}, bf16[4,24,1920]{2,1,0:T(8,128)(2,1)}) custom-call(s32[2]{0:T(128)} %pad_add_fusion.bits, bf16[4,2,24,1920]{3,2,1,0:T(8,128)(2,1)} %get-tuple-element.190.keep_a, bf16[4,2,24,1920]{3,2,1,0:T(8,128)(2,1)} %get-tuple-element.191.keep_b, ...), custom_call_target="tpu_custom_call" | custom-call | tf_op jit(solution)/shard_map/second_sums/pallas_call | solution.py:928
  193.5 3.3 %reduce-scatter.2.cloned.1.call-done = bf16[384,768]{1,0:T(8,128)(2,1)} async-done(((bf16[3072,768]{1,0:T(8,128)(2,1)}), bf16[384,768]{1,0:T(8,128)(2,1)}) %reduce-scatter.2.cloned.1.call-update) | async-done | bytes 589840 | tf_op jit(solution)/shard_map/reduce_scatter | solution.py:1121
  196.8 1.4 copy.51
  199.2 1.5 collective-permute-start.5
  201.2 0.7 reduce.3
  202.4 0.8 pad.4.rest_0_
  203.2 6.7 %grad_before.3 = bf16[768,1280]{1,0:T(8,128)(2,1)} custom-call(bf16[2,512,768]{2,1,0:T(8,128)(2,1)} %xc.7, bf16[2,80,768]{2,1,0:T(8,128)(2,1)} %get-tuple-element.325.xq, bf16[2,592,384]{2,1,0:T(8,128)(2,1)} %get-tuple-element.219.dq.dq_m, bf16[2,512,384]{2,1,0:T(8,128)(2,1)} %get-tuple-element.220.dk.dk_m, bf16[2,512,384]{2,1,0:T(8,128)(2,1)} %get-tuple-element.221.dv.dv_m, ...), custom_call_target="tpu_custom_call" | custom-call | tf_op jit(solution)/shard_map/grad_before/pallas_call | solution.py:809
  209.9 3.2 %first_sums.3 = (bf16[4,2,24,1280]{3,2,1,0:T(8,128)(2,1)}, bf16[4,2,24,1280]{3,2,1,0:T(8,128)(2,1)}, bf16[4,2,24,1280]{3,2,1,0:T(8,128)(2,1)}, bf16[4,2,24,1280]{3,2,1,0:T(8,128)(2,1)}) custom-call(s32[2]{0:T(128)} %pad_add_fusion.bits, bf16[4,2,2,48,1280]{4,3,2,1,0:T(8,128)(2,1)} %bitcast.47), custom_call_target="tpu_custom_call" | custom-call | tf_op jit(solution)/shard_map/first_sums/pallas_call | solution.py:928
  213.2 2.4 third_sums.2
  215.5 3.7 %all-to-all-start.1 = ((bf16[4,48,1920]{2,1,0:T(8,128)(2,1)}), bf16[4,48,1920]{2,1,0:T(8,128)(2,1)S(1)}, u32[]{:S(2)}, u32[]{:S(2)}) async-start(bf16[4,48,1920]{2,1,0:T(8,128)(2,1)} %third_sums.2), calls=%async_computation.2 | async-start | bytes 1474560 | tf_op jit(solution)/shard_map/all_to_all | solution.py:981
  219.2 1.4 collective-permute-start.7
  220.6 1.4 collective-permute-start.8
  222.2 9.6 %input_grad.1 = (f32[2,512,768]{2,1,0:T(8,128)}, bf16[2,80,768]{2,1,0:T(8,128)(2,1)}) custom-call(s32[1]{0:T(128)} %bitcast.7.half.first.core, f32[2,512,768]{2,1,0:T(8,128)} %get-tuple-element.242.first_c, f32[2,80,768]{2,1,0:T(8,128)} %get-tuple-element.243.first_q, bf16[2,592,384]{2,1,0:T(8,128)(2,1)} %get-tuple-element.199.dq.dq_o, ...), custom_call_target="tpu_custom_call" | custom-call | tf_op jit(solution)/shard_map/input_grad/pallas_call | solution.py:849
  232.5 0.8 collective-permute-done.8.got_b
  233.3 0.8 copy-done.12
  234.1 2.6 second_sums.3
  236.7 1.1 collective-permute-start.9
  237.8 1.3 collective-permute-start.10
  240.0 3.3 %collective-permute-done.9.got_a = bf16[4,24,1280]{2,1,0:T(8,128)(2,1)S(1)} collective-permute-done((bf16[4,24,1280]{2,1,0:T(8,128)(2,1)}, bf16[4,24,1280]{2,1,0:T(8,128)(2,1)S(1)}, u32[]{:S(2)}, u32[]{:S(2)}) %collective-permute-start.9) | collective-permute-done | bytes 245792 | tf_op jit(solution)/shard_map/ppermute | solution.py:867
  243.2 1.0 collective-permute-done.10.got_b
  244.3 0.7 copy-done.19
  244.9 2.2 third_sums.3
  247.2 0.9 copy-done
  248.0 1.9 part_sums.2
  249.9 4.8 %all-to-all-start.2 = ((bf16[4,48,1280]{2,1,0:T(8,128)(2,1)}), bf16[4,48,1280]{2,1,0:T(8,128)(2,1)S(1)}, u32[]{:S(2)}, u32[]{:S(2)}) async-start(bf16[4,48,1280]{2,1,0:T(8,128)(2,1)} %third_sums.3), calls=%async_computation.3 | async-start | bytes 983040 | tf_op jit(solution)/shard_map/all_to_all | solution.py:981
  254.7 1.3 collective-permute-start.12
  256.0 0.7 collective-permute-start.11
  256.8 1.3 collective-permute-start.14
  258.6 9.9 %collective-permute-done.14 = bf16[2,20,1536]{2,0,1:T(2,128)(2,1)S(1)} collective-permute-done((bf16[2,20,1536]{2,0,1:T(2,128)(2,1)S(1)}, bf16[2,20,1536]{2,0,1:T(2,128)(2,1)S(1)}, u32[]{:S(2)}, u32[]{:S(2)}) %collective-permute-start.14) | collective-permute-done | bytes 122912 | tf_op jit(solution)/shard_map/ppermute | solution.py:867
  268.7 0.8 copy-done.2
  269.4 1.7 part_sums.3
  271.4 0.7 copy-done.10
  272.1 1.2 collective-permute-start.16
  273.3 0.8 collective-permute-start.17
  274.1 0.9 pad_maximum_fusion.2
  275.9 2.3 collective-permute-done.16
  279.0 2.2 place_sums.3
  281.2 2.4 place_sums.4
  283.5 0.9 slice_convert_fusion
  284.4 0.7 copy-done.17
  285.1 2.0 place_sums.5
  287.2 1.3 reshape.152
  288.5 1.3 reshape.153
  (121 shorter events, 10.6 us)
Async XLA Ops:
  7.2 7.1 %copy-start.31 = (s32[8]{0:T(128)S(1)}, s32[8]{0:T(128)}, u32[]{:S(2)}) copy-start(s32[8]{0:T(128)} %param.20) | copy-start | bytes 100
  7.2 8.6 %copy-start.22 = (bf16[12,32]{1,0:T(8,128)(2,1)S(1)}, bf16[12,32]{1,0:T(8,128)(2,1)}, u32[]{:S(2)}) copy-start(bf16[12,32]{1,0:T(8,128)(2,1)} %param.33) | copy-start | bytes 2308
  7.2 9.2 %copy-start.26 = (bf16[3072]{0:T(1024)(128)(2,1)S(1)}, bf16[3072]{0:T(1024)(128)(2,1)}, u32[]{:S(2)}) copy-start(bf16[3072]{0:T(1024)(128)(2,1)} %param.30) | copy-start | bytes 18436
  10.1 16.6 %all-to-all-start = ((bf16[8,20,1536]{2,1,0:T(8,128)(2,1)}), bf16[8,20,1536]{2,1,0:T(8,128)(2,1)S(1)}, u32[]{:S(2)}, u32[]{:S(2)}) async-start(bf16[8,20,1536]{2,1,0:T(8,128)(2,1)} %pad_maximum_fusion), calls=%async_computation | async-start | bytes 1179648 | tf_op jit(solution)/shard_map/all_to_all | solution.py:1077
  14.3 182.5 %reduce-scatter.2.cloned.1.call-start = ((), (), s32[]{:S(2)}) async-start(), calls=%async_computation.4 | async-start | bytes 5308416 | tf_op jit(solution)/shard_map/reduce_scatter | solution.py:1121
  132.6 17.1 %collective-permute-start = (bf16[768,1920]{1,0:T(8,128)(2,1)}, bf16[768,1920]{1,0:T(8,128)(2,1)S(1)}, u32[]{:S(2)}, u32[]{:S(2)}) collective-permute-start(bf16[768,1920]{1,0:T(8,128)(2,1)} %get-tuple-element.179), channel_id=1, source_target_pairs={{0,1},{1,0},{2,3},{3,2},{4,5},{5,4},{6,7},{7,6},{8,9},{9,8},{10,11... | collective-permute-start | bytes 8847368 | tf_op jit(solution)/shard_map/ppermute | solution.py:867
  149.7 1.6 copy-start.1
  156.2 10.2 %copy-start.25 = (f32[3,768]{1,0:T(4,128)S(1)}, f32[3,768]{1,0:T(4,128)}, u32[]{:S(2)}) copy-start(f32[3,768]{1,0:T(4,128)} %get-tuple-element.225) | copy-start | bytes 27652
  162.2 27.3 %collective-permute-start.3 = (bf16[768,1152]{1,0:T(8,128)(2,1)}, bf16[768,1152]{1,0:T(8,128)(2,1)S(1)}, u32[]{:S(2)}, u32[]{:S(2)}) collective-permute-start(bf16[768,1152]{1,0:T(8,128)(2,1)} %grad_before.2), channel_id=1, source_target_pairs={{0,1},{1,0},{2,3},{3,2},{4,5},{5,4},{6,7},{7,6},{8,9},{9,8},{10,11... | collective-permute-start | bytes 5308424 | tf_op jit(solution)/shard_map/ppermute | solution.py:867
  162.3 19.6 %collective-permute-start.1 = (bf16[4,2,24,1920]{3,2,1,0:T(8,128)(2,1)}, bf16[4,2,24,1920]{3,2,1,0:T(8,128)(2,1)S(1)}, u32[]{:S(2)}, u32[]{:S(2)}) collective-permute-start(bf16[4,2,24,1920]{3,2,1,0:T(8,128)(2,1)} %get-tuple-element.197), channel_id=1, source_target_pairs={{0,2},{1,3},{2,0},{3,1},{4,6},{5,7},{6,4},{7,5},{8,10},{9,11},{10,... | collective-permute-start | bytes 2211848 | tf_op jit(solution)/shard_map/ppermute | solution.py:867
  164.5 25.0 %collective-permute-start.2 = (bf16[4,2,24,1920]{3,2,1,0:T(8,128)(2,1)}, bf16[4,2,24,1920]{3,2,1,0:T(8,128)(2,1)S(1)}, u32[]{:S(2)}, u32[]{:S(2)}) collective-permute-start(bf16[4,2,24,1920]{3,2,1,0:T(8,128)(2,1)} %get-tuple-element.198), channel_id=1, source_target_pairs={{0,4},{4,0},{8,12},{12,8},{16,20},{20,16},{24,28},{28,24},{1,5},{5... | collective-permute-start | bytes 2211848 | tf_op jit(solution)/shard_map/ppermute | solution.py:867
  181.9 7.6 %copy-start.8 = (bf16[4,2,24,1920]{3,2,1,0:T(8,128)(2,1)}, bf16[4,2,24,1920]{3,2,1,0:T(8,128)(2,1)S(1)}, u32[]{:S(2)}) copy-start(bf16[4,2,24,1920]{3,2,1,0:T(8,128)(2,1)S(1)} %collective-permute-done.1.got_a) | copy-start | bytes 2211844
  189.5 0.9 copy-start.9
  189.5 8.7 %copy-start.3 = (bf16[768,1152]{1,0:T(8,128)(2,1)}, bf16[768,1152]{1,0:T(8,128)(2,1)S(1)}, u32[]{:S(2)}) copy-start(bf16[768,1152]{1,0:T(8,128)(2,1)S(1)} %collective-permute-done.3.rest_1_) | copy-start | bytes 5308420
  193.5 5.7 %copy-start.32 = (bf16[4,24,1920]{2,1,0:T(8,128)(2,1)S(1)}, bf16[4,24,1920]{2,1,0:T(8,128)(2,1)}, u32[]{:S(2)}) copy-start(bf16[4,24,1920]{2,1,0:T(8,128)(2,1)} %get-tuple-element.217) | copy-start | bytes 1105924
  193.5 7.2 %copy-start.24 = (f32[3,768]{1,0:T(4,128)S(1)}, f32[3,768]{1,0:T(4,128)}, u32[]{:S(2)}) copy-start(f32[3,768]{1,0:T(4,128)} %get-tuple-element.224) | copy-start | bytes 27652
  193.5 7.7 %copy-start.23 = (f32[1,3072]{1,0:T(1,128)S(1)}, f32[1,3072]{1,0:T(1,128)}, u32[]{:S(2)}) copy-start(f32[1,3072]{1,0:T(1,128)} %get-tuple-element.226) | copy-start | bytes 36868
  193.5 8.6 %copy-start.28 = (f32[3,2,128]{2,1,0:T(2,128)S(1)}, f32[3,2,128]{2,1,0:T(2,128)}, u32[]{:S(2)}) copy-start(f32[3,2,128]{2,1,0:T(2,128)} %get-tuple-element.228) | copy-start | bytes 9220
  193.5 8.6 %copy-start.30 = (f32[3,2,128]{2,1,0:T(2,128)S(1)}, f32[3,2,128]{2,1,0:T(2,128)}, u32[]{:S(2)}) copy-start(f32[3,2,128]{2,1,0:T(2,128)} %get-tuple-element.227) | copy-start | bytes 9220
  193.5 8.7 %copy-start.27 = (f32[2,384]{1,0:T(2,128)S(1)}, f32[2,384]{1,0:T(2,128)}, u32[]{:S(2)}) copy-start(f32[2,384]{1,0:T(2,128)} %get-tuple-element.223) | copy-start | bytes 9220
  193.5 8.7 %copy-start.29 = (f32[2,384]{1,0:T(2,128)S(1)}, f32[2,384]{1,0:T(2,128)}, u32[]{:S(2)}) copy-start(f32[2,384]{1,0:T(2,128)} %get-tuple-element.222) | copy-start | bytes 9220
  198.5 11.4 %collective-permute-start.6 = (bf16[384,384]{1,0:T(8,128)(2,1)S(1)}, bf16[384,384]{1,0:T(8,128)(2,1)S(1)}, u32[]{:S(2)}, u32[]{:S(2)}) collective-permute-start(bf16[384,384]{1,0:T(8,128)(2,1)S(1)} %bitcast.55), channel_id=1, source_target_pairs={{0,1},{1,0},{2,3},{3,2},{4,5},{5,4},{6,7},{7,6},{8,9},{9,8},{10,11... | collective-permute-start | bytes 884744 | tf_op jit(solution)/shard_map/ppermute | solution.py:867
  198.6 11.3 %collective-permute-start.4 = (bf16[4,24,1920]{2,1,0:T(8,128)(2,1)}, bf16[4,24,1920]{2,1,0:T(8,128)(2,1)S(1)}, u32[]{:S(2)}, u32[]{:S(2)}) collective-permute-start(bf16[4,24,1920]{2,1,0:T(8,128)(2,1)} %get-tuple-element.216), channel_id=1, source_target_pairs={{0,4},{4,0},{8,12},{12,8},{16,20},{20,16},{24,28},{28,24},{1,5},{5... | collective-permute-start | bytes 1105928 | tf_op jit(solution)/shard_map/ppermute | solution.py:867
  199.2 10.7 %collective-permute-start.5 = (bf16[4,24,1920]{2,1,0:T(8,128)(2,1)S(1)}, bf16[4,24,1920]{2,1,0:T(8,128)(2,1)S(1)}, u32[]{:S(2)}, u32[]{:S(2)}) collective-permute-start(bf16[4,24,1920]{2,1,0:T(8,128)(2,1)S(1)} %copy-done.32), channel_id=1, source_target_pairs={{0,2},{1,3},{2,0},{3,1},{4,6},{5,7},{6,4},{7,5},{8,10},{9,11},{10,... | collective-permute-start | bytes 1105928 | tf_op jit(solution)/shard_map/ppermute | solution.py:867
  209.9 3.3 %copy-start.13 = (bf16[4,24,1920]{2,1,0:T(8,128)(2,1)}, bf16[4,24,1920]{2,1,0:T(8,128)(2,1)S(1)}, u32[]{:S(2)}) copy-start(bf16[4,24,1920]{2,1,0:T(8,128)(2,1)S(1)} %collective-permute-done.4.got_a) | copy-start | bytes 1105924
  209.9 3.3 %copy-start.14 = (bf16[4,24,1920]{2,1,0:T(8,128)(2,1)}, bf16[4,24,1920]{2,1,0:T(8,128)(2,1)S(1)}, u32[]{:S(2)}) copy-start(bf16[4,24,1920]{2,1,0:T(8,128)(2,1)S(1)} %collective-permute-done.5.got_b) | copy-start | bytes 1105924
  215.5 31.6 %all-to-all-start.1 = ((bf16[4,48,1920]{2,1,0:T(8,128)(2,1)}), bf16[4,48,1920]{2,1,0:T(8,128)(2,1)S(1)}, u32[]{:S(2)}, u32[]{:S(2)}) async-start(bf16[4,48,1920]{2,1,0:T(8,128)(2,1)} %third_sums.2), calls=%async_computation.2 | async-start | bytes 1474560 | tf_op jit(solution)/shard_map/all_to_all | solution.py:981
  219.2 13.3 %collective-permute-start.7 = (bf16[4,2,24,1280]{3,2,1,0:T(8,128)(2,1)}, bf16[4,2,24,1280]{3,2,1,0:T(8,128)(2,1)S(1)}, u32[]{:S(2)}, u32[]{:S(2)}) collective-permute-start(bf16[4,2,24,1280]{3,2,1,0:T(8,128)(2,1)} %get-tuple-element.240), channel_id=1, source_target_pairs={{0,2},{1,3},{2,0},{3,1},{4,6},{5,7},{6,4},{7,5},{8,10},{9,11},{10,... | collective-permute-start | bytes 1474568 | tf_op jit(solution)/shard_map/ppermute | solution.py:867
  220.6 12.7 %collective-permute-start.8 = (bf16[4,2,24,1280]{3,2,1,0:T(8,128)(2,1)}, bf16[4,2,24,1280]{3,2,1,0:T(8,128)(2,1)S(1)}, u32[]{:S(2)}, u32[]{:S(2)}) collective-permute-start(bf16[4,2,24,1280]{3,2,1,0:T(8,128)(2,1)} %get-tuple-element.241), channel_id=1, source_target_pairs={{0,4},{4,0},{8,12},{12,8},{16,20},{20,16},{24,28},{28,24},{1,5},{5... | collective-permute-start | bytes 1474568 | tf_op jit(solution)/shard_map/ppermute | solution.py:867
  231.8 7.2 %copy-start.20 = (bf16[2,80,768]{2,1,0:T(8,128)(2,1)S(1)}, bf16[2,80,768]{2,1,0:T(8,128)(2,1)}, u32[]{:S(2)}) copy-start(bf16[2,80,768]{2,1,0:T(8,128)(2,1)} %get-tuple-element.256) | copy-start | bytes 737284
  231.8 7.2 %copy-start.21 = (bf16[2,80,768]{2,1,0:T(8,128)(2,1)S(1)}, bf16[2,80,768]{2,1,0:T(8,128)(2,1)}, u32[]{:S(2)}) copy-start(bf16[2,80,768]{2,1,0:T(8,128)(2,1)} %get-tuple-element.257) | copy-start | bytes 737284
  232.5 0.8 copy-start.11
  233.3 0.8 copy-start.12
  236.7 6.5 %collective-permute-start.9 = (bf16[4,24,1280]{2,1,0:T(8,128)(2,1)}, bf16[4,24,1280]{2,1,0:T(8,128)(2,1)S(1)}, u32[]{:S(2)}, u32[]{:S(2)}) collective-permute-start(bf16[4,24,1280]{2,1,0:T(8,128)(2,1)} %get-tuple-element.254), channel_id=1, source_target_pairs={{0,4},{4,0},{8,12},{12,8},{16,20},{20,16},{24,28},{28,24},{1,5},{5... | collective-permute-start | bytes 737288 | tf_op jit(solution)/shard_map/ppermute | solution.py:867
  237.8 6.5 %collective-permute-start.10 = (bf16[4,24,1280]{2,1,0:T(8,128)(2,1)}, bf16[4,24,1280]{2,1,0:T(8,128)(2,1)S(1)}, u32[]{:S(2)}, u32[]{:S(2)}) collective-permute-start(bf16[4,24,1280]{2,1,0:T(8,128)(2,1)} %get-tuple-element.255), channel_id=1, source_target_pairs={{0,2},{1,3},{2,0},{3,1},{4,6},{5,7},{6,4},{7,5},{8,10},{9,11},{10,... | collective-permute-start | bytes 737288 | tf_op jit(solution)/shard_map/ppermute | solution.py:867
  243.2 1.1 copy-start.18
  244.3 0.7 copy-start.19
  247.2 0.9 copy-start
  249.9 21.4 %copy-start.7 = (bf16[48,1920]{1,0:T(8,128)(2,1)S(1)}, bf16[48,1920]{1,0:T(8,128)(2,1)}, u32[]{:S(2)}) copy-start(bf16[48,1920]{1,0:T(8,128)(2,1)} %part_sums.2) | copy-start | bytes 552964
  249.9 18.7 %all-to-all-start.2 = ((bf16[4,48,1280]{2,1,0:T(8,128)(2,1)}), bf16[4,48,1280]{2,1,0:T(8,128)(2,1)S(1)}, u32[]{:S(2)}, u32[]{:S(2)}) async-start(bf16[4,48,1280]{2,1,0:T(8,128)(2,1)} %third_sums.3), calls=%async_computation.3 | async-start | bytes 983040 | tf_op jit(solution)/shard_map/all_to_all | solution.py:981
  254.7 13.9 %collective-permute-start.12 = (bf16[384,384]{1,0:T(8,128)(2,1)S(1)}, bf16[384,384]{1,0:T(8,128)(2,1)S(1)}, u32[]{:S(2)}, u32[]{:S(2)}) collective-permute-start(bf16[384,384]{1,0:T(8,128)(2,1)S(1)} %fusion), channel_id=1, source_target_pairs={{0,2},{1,3},{2,0},{3,1},{4,6},{5,7},{6,4},{7,5},{8,10},{9,11},{10,... | collective-permute-start | bytes 884744 | tf_op jit(solution)/shard_map/ppermute | solution.py:867
  256.0 12.6 %collective-permute-start.11 = (bf16[48,1920]{1,0:T(8,128)(2,1)}, bf16[48,1920]{1,0:T(8,128)(2,1)S(1)}, u32[]{:S(2)}, u32[]{:S(2)}) collective-permute-start(bf16[48,1920]{1,0:T(8,128)(2,1)} %part_sums.2), channel_id=1, source_target_pairs={{0,2},{1,3},{2,0},{3,1},{4,6},{5,7},{6,4},{7,5},{8,10},{9,11},{10,... | collective-permute-start | bytes 552968 | tf_op jit(solution)/shard_map/ppermute | solution.py:867
  256.8 1.9 collective-permute-start.13
  256.8 11.8 %collective-permute-start.14 = (bf16[2,20,1536]{2,0,1:T(2,128)(2,1)S(1)}, bf16[2,20,1536]{2,0,1:T(2,128)(2,1)S(1)}, u32[]{:S(2)}, u32[]{:S(2)}) collective-permute-start(bf16[2,20,1536]{2,0,1:T(2,128)(2,1)S(1)} %get-tuple-element.270), channel_id=1, source_target_pairs={{0,2},{1,3},{2,0},{3,1},{4,6},{5,7},{6,4},{7,5},{8,10},{9,11},{10,... | collective-permute-start | bytes 368648 | tf_op jit(solution)/shard_map/ppermute | solution.py:867
  258.0 10.6 %collective-permute-start.15 = (bf16[2,20,1536]{2,0,1:T(2,128)(2,1)S(1)}, bf16[2,20,1536]{2,0,1:T(2,128)(2,1)S(1)}, u32[]{:S(2)}, u32[]{:S(2)}) collective-permute-start(bf16[2,20,1536]{2,0,1:T(2,128)(2,1)S(1)} %get-tuple-element.271), channel_id=1, source_target_pairs={{0,3},{1,2},{2,1},{3,0},{4,7},{5,6},{6,5},{7,4},{8,11},{9,10},{10,... | collective-permute-start | bytes 368648 | tf_op jit(solution)/shard_map/ppermute | solution.py:867
  268.7 0.8 copy-start.2
  271.2 0.9 copy-start.10
  271.3 4.7 %copy-start.5 = (bf16[384,384]{1,0:T(8,128)(2,1)}, bf16[384,384]{1,0:T(8,128)(2,1)S(1)}, u32[]{:S(2)}) copy-start(bf16[384,384]{1,0:T(8,128)(2,1)S(1)} %add_convert_fusion.own) | copy-start | bytes 884740
  272.1 6.2 %copy-start.4 = (bf16[96,1920]{1,0:T(8,128)(2,1)}, bf16[96,1920]{1,0:T(8,128)(2,1)S(1)}, u32[]{:S(2)}) copy-start(bf16[96,1920]{1,0:T(8,128)(2,1)S(1)} %pad_maximum_fusion.4.own) | copy-start | bytes 1105924
  272.1 6.2 %collective-permute-start.16 = (bf16[48,1280]{1,0:T(8,128)(2,1)S(1)}, bf16[48,1280]{1,0:T(8,128)(2,1)S(1)}, u32[]{:S(2)}, u32[]{:S(2)}) collective-permute-start(bf16[48,1280]{1,0:T(8,128)(2,1)S(1)} %copy-done.10), channel_id=1, source_target_pairs={{0,2},{1,3},{2,0},{3,1},{4,6},{5,7},{6,4},{7,5},{8,10},{9,11},{10,... | collective-permute-start | bytes 368648 | tf_op jit(solution)/shard_map/ppermute | solution.py:867
  273.3 5.0 %collective-permute-start.17 = (bf16[384,384]{1,0:T(8,128)(2,1)S(1)}, bf16[384,384]{1,0:T(8,128)(2,1)S(1)}, u32[]{:S(2)}, u32[]{:S(2)}) collective-permute-start(bf16[384,384]{1,0:T(8,128)(2,1)S(1)} %add_convert_fusion.own), channel_id=1, source_target_pairs={{0,1},{1,0},{2,3},{3,2},{4,5},{5,4},{6,7},{7,6},{8,9},{9,8},{10,11... | collective-permute-start | bytes 884744 | tf_op jit(solution)/shard_map/ppermute | solution.py:867
  274.1 4.1 %collective-permute-start.18 = (bf16[96,1920]{1,0:T(8,128)(2,1)S(1)}, bf16[96,1920]{1,0:T(8,128)(2,1)S(1)}, u32[]{:S(2)}, u32[]{:S(2)}) collective-permute-start(bf16[96,1920]{1,0:T(8,128)(2,1)S(1)} %pad_maximum_fusion.4.own), channel_id=1, source_target_pairs={{0,1},{1,0},{2,3},{3,2},{4,5},{5,4},{6,7},{7,6},{8,9},{9,8},{10,11... | collective-permute-start | bytes 1105928 | tf_op jit(solution)/shard_map/ppermute | solution.py:867
  278.2 0.7 copy-start.16
  278.2 2.9 copy-start.15
  278.3 6.1 %copy-start.6 = (bf16[96,1280]{1,0:T(8,128)(2,1)}, bf16[96,1280]{1,0:T(8,128)(2,1)S(1)}, u32[]{:S(2)}) copy-start(bf16[96,1280]{1,0:T(8,128)(2,1)S(1)} %pad_maximum_fusion.5.own) | copy-start | bytes 737284
  278.3 6.1 %collective-permute-start.19 = (bf16[96,1280]{1,0:T(8,128)(2,1)S(1)}, bf16[96,1280]{1,0:T(8,128)(2,1)S(1)}, u32[]{:S(2)}, u32[]{:S(2)}) collective-permute-start(bf16[96,1280]{1,0:T(8,128)(2,1)S(1)} %pad_maximum_fusion.5.own), channel_id=1, source_target_pairs={{0,1},{1,0},{2,3},{3,2},{4,5},{5,4},{6,7},{7,6},{8,9},{9,8},{10,11... | collective-permute-start | bytes 737288 | tf_op jit(solution)/shard_map/ppermute | solution.py:867
  284.4 0.7 copy-start.17
Sparse Core Ops, SparseCore 0:
  94.1 102.6 reduce-scatter.1
